TPU v7x, 32 devices: a whole 2x2x4 slice. The times are simulated.
32 devices in a mesh: seg: 8 (over z, x), tp: 4 (over y, core).
Axes of the slice: x: 2, y: 2, z: 4, core: 2. Of those that a mesh axis runs over, the one named last changes fastest.
Arguments:
- queries: bfloat16 [2048, 8192], P('seg', 'tp'), may hold values from -8 to 8
- keys_own: bfloat16 [2048, 1024], P('seg', 'tp'), may hold values from -8 to 8
- values_own: bfloat16 [2048, 1024], P('seg', 'tp'), may hold values from -6 to 6
- out_grad: bfloat16 [2048, 8192], P('seg', 'tp'), may hold values from -6 to 6
- summary_states: bfloat16 [400, 8192], P('seg'), may hold values from -6 to 6
- w_key: bfloat16 [8192, 1024], P(None, 'tp'), may hold values from -0.0625 to 0.0625
- w_value: bfloat16 [8192, 1024], P(None, 'tp'), may hold values from -0.0625 to 0.0625
- summary_grad: bfloat16 [400, 8192], P('seg', 'tp'), may hold values from -6 to 6
Outputs:
- query_grad: bfloat16 [2048, 8192], P('seg', 'tp')
- key_grad: bfloat16 [2048, 1024], P('seg', 'tp')
- value_grad: bfloat16 [2048, 1024], P('seg', 'tp')
- state_grad: bfloat16 [400, 8192], P('seg', 'tp')
All inputs are finite; a program needn't handle non-finite values.
Results may differ from a plain program's by a relative error of at most 0.023.
Values may be sent and summed in bfloat16 or wider, within the bound.
No kernel may reach another device: no remote copies, remote signals or barrier semaphores. Data moves between devices by JAX's collectives and lax.ppermute only.
A program may use at most 256 MiB of HBM per device.

v0:
```python
import jax
import jax.numpy as jnp
from jax import lax
from jax.sharding import PartitionSpec as P

HEADS = 64
KVH = 8
HD = 128


def per_device(
    queries, keys_own, values_own, out_grad, summary_states, w_key, w_value, summary_grad
):
    rows = queries.shape[0]
    kv_local = keys_own.shape[1] // HD
    group = HEADS // KVH
    scale = HD ** (-0.5)
    count = summary_states.shape[0]
    segments = lax.axis_size("seg")
    position = lax.axis_index("seg")
    nsum = count * segments
    nkeys = nsum + rows
    width = kv_local * HD
    projected = jnp.concatenate(
        [
            jnp.dot(summary_states, w_key, preferred_element_type=jnp.float32).astype(jnp.bfloat16),
            jnp.dot(summary_states, w_value, preferred_element_type=jnp.float32).astype(
                jnp.bfloat16
            ),
        ],
        axis=1,
    )
    everyone = lax.all_gather(projected, "seg", axis=0, tiled=True)
    keys_all = jnp.concatenate([everyone[:, :width], keys_own], 0)
    vals_all = jnp.concatenate([everyone[:, width:], values_own], 0)
    row_pos = jnp.arange(rows)[:, None]
    col_pos = jnp.arange(nkeys)[None, :]
    visible = jnp.where(col_pos < nsum, col_pos < position * count, col_pos - nsum <= row_pos)
    query_heads = queries.reshape(rows, kv_local * group, HD).transpose(1, 0, 2)
    grad_heads = out_grad.reshape(rows, kv_local * group, HD).transpose(1, 0, 2)
    contract_last = (((1,), (1,)), ((), ()))
    contract_first = (((0,), (0,)), ((), ()))
    query_blocks = []
    key_sums = []
    value_sums = []
    for kv_index in range(kv_local):
        keyset = keys_all[:, kv_index * HD : (kv_index + 1) * HD]
        valset = vals_all[:, kv_index * HD : (kv_index + 1) * HD]

        def head_step(carry, inputs):
            key_acc, val_acc = carry
            query_head, grad_head = inputs
            scores = (
                lax.dot_general(
                    query_head, keyset, contract_last, preferred_element_type=jnp.float32
                )
                * scale
            )
            scores = jnp.where(visible, scores, -jnp.inf)
            probs = jnp.exp(scores - jnp.max(scores, axis=-1, keepdims=True))
            probs = probs / jnp.sum(probs, axis=-1, keepdims=True)
            probs_b = probs.astype(jnp.bfloat16)
            attn = jnp.dot(probs_b, valset, preferred_element_type=jnp.float32)
            delta = jnp.sum(grad_head.astype(jnp.float32) * attn, axis=-1)
            dprobs = lax.dot_general(
                grad_head, valset, contract_last, preferred_element_type=jnp.float32
            )
            dscores = (probs * (dprobs - delta[:, None])).astype(jnp.bfloat16)
            dquery = (jnp.dot(dscores, keyset, preferred_element_type=jnp.float32) * scale).astype(
                jnp.bfloat16
            )
            key_acc = key_acc + lax.dot_general(
                dscores, query_head, contract_first, preferred_element_type=jnp.float32
            )
            val_acc = val_acc + lax.dot_general(
                probs_b, grad_head, contract_first, preferred_element_type=jnp.float32
            )
            return ((key_acc, val_acc), dquery)

        start = kv_index * group
        zeros = jnp.zeros((nkeys, HD), jnp.float32)
        (key_acc, val_acc), dquery = lax.scan(
            head_step,
            (zeros, zeros),
            (query_heads[start : start + group], grad_heads[start : start + group]),
        )
        query_blocks.append(dquery)
        key_sums.append(key_acc * scale)
        value_sums.append(val_acc)
    query_grad = (
        jnp.concatenate(query_blocks, 0).transpose(1, 0, 2).reshape(rows, kv_local * group * HD)
    )
    key_grad = jnp.concatenate([acc[nsum:] for acc in key_sums], 1).astype(jnp.bfloat16)
    value_grad = jnp.concatenate([acc[nsum:] for acc in value_sums], 1).astype(jnp.bfloat16)
    summary_terms = jnp.concatenate(
        [acc[:nsum] for acc in key_sums] + [acc[:nsum] for acc in value_sums], 1
    )
    emitted = lax.psum_scatter(
        summary_terms.astype(jnp.bfloat16), "seg", scatter_dimension=0, tiled=True
    )
    partial_state = lax.dot_general(
        emitted[:, :width], w_key, contract_last, preferred_element_type=jnp.float32
    )
    partial_state = partial_state + lax.dot_general(
        emitted[:, width:], w_value, contract_last, preferred_element_type=jnp.float32
    )
    shared = lax.psum_scatter(
        partial_state.astype(jnp.bfloat16), "tp", scatter_dimension=1, tiled=True
    ).astype(jnp.float32)
    state_grad = (shared + summary_grad.astype(jnp.float32)).astype(jnp.bfloat16)
    return (query_grad, key_grad, value_grad, state_grad)


def solution(mesh):
    placed = (
        P("seg", "tp"),
        P("seg", "tp"),
        P("seg", "tp"),
        P("seg", "tp"),
        P("seg", None),
        P(None, "tp"),
        P(None, "tp"),
        P("seg", "tp"),
    )
    return jax.shard_map(
        per_device,
        mesh=mesh,
        in_specs=placed,
        out_specs=(P("seg", "tp"), P("seg", "tp"), P("seg", "tp"), P("seg", "tp")),
        check_vma=False,
    )
```

profile of v0, /device:TPU:0, one launch (start us, length us, event | category | flops | bytes accessed | tf_op | source)
XLA Modules:
  0.0 285.2 jit_solution(16385124431053222005)
XLA Ops:
  8.4 3.2 %convolution_convert_fusion = bf16[50,256]{1,0:T(8,128)(2,1)S(1)} fusion(bf16[50,8192]{1,0:T(8,128)(2,1)S(1)} %copy-done, bf16[8192,256]{1,0:T(8,128)(2,1)} %param.18), kind=kOutput, calls=%fused_computation.66 | convolution fusion | flops 209728000 | bytes 5039104 | tf_op jit(solution)/shard_map/dot_general | solution.py:27
  12.6 32.9 %all-gather = bf16[8,50,512]{2,1,0:T(8,128)(2,1)S(1)} all-gather(bf16[1,50,512]{2,1,0:T(8,128)(2,1)S(1)} %maximum_bitcast_fusion.1), channel_id=1, replica_groups=mesh['seg'=8,'tp'=4] {'seg'}, dimensions={0}, use_global_device_ids=true | all-gather | bytes 460800 | tf_op jit(solution)/shard_map/all_gather | solution.py:33
  45.7 1.5 copy.19
  47.2 2.3 copy.20
  49.5 2.6 fusion.63
  52.0 1.6 fusion.55
  53.8 56.5 %while.30 = (s32[]{:T(128)}, f32[656,128]{1,0:T(8,128)S(1)}, f32[656,128]{1,0:T(8,128)}, bf16[8,256,128]{2,1,0:T(8,128)(2,1)S(1)}, bf16[8,256,128]{1,2,0:T(8,128...) while((s32[]{:T(128)}, f32[656,128]{1,0:T(8,128)S(1)}, ...), condition=%wide.region_4.5_spmd.clone, body=%wide.region_0.4_spmd.clone.sunk | while | flops 261471488 | bytes 6792176 | solution.py:82
  53.8 1.2 fusion.127
  55.1 1.8 convolution_add_fusion.10
  57.0 1.1 fusion.129
  60.7 1.2 fusion.127
  62.0 2.0 convolution_add_fusion.10
  64.0 1.1 fusion.129
  67.8 1.2 fusion.127
  69.1 2.0 convolution_add_fusion.10
  71.1 1.1 fusion.129
  74.8 1.2 fusion.127
  76.2 2.0 convolution_add_fusion.10
  78.2 1.1 fusion.129
  80.8 1.1 convolution_add_fusion.9
  81.9 1.2 fusion.127
  83.3 2.0 convolution_add_fusion.10
  85.3 1.1 fusion.129
  89.0 1.2 fusion.127
  90.4 2.0 convolution_add_fusion.10
  92.4 1.1 fusion.129
  96.1 1.2 fusion.127
  97.4 2.0 convolution_add_fusion.10
  99.5 1.1 fusion.129
  103.2 1.2 fusion.127
  104.5 2.0 convolution_add_fusion.10
  106.5 1.1 fusion.129
  112.7 57.8 %while.31 = (s32[]{:T(128)}, f32[656,128]{1,0:T(8,128)S(1)}, f32[656,128]{1,0:T(8,128)}, bf16[8,256,128]{2,1,0:T(8,128)(2,1)S(1)}, bf16[8,256,128]{1,2,0:T(8,128...) while((s32[]{:T(128)}, f32[656,128]{1,0:T(8,128)S(1)}, ...), condition=%wide.region_9.10_spmd.clone, body=%wide.region_5.9_spmd.clone.sunk | while | flops 261471488 | bytes 7463948 | solution.py:82
  112.7 1.2 fusion.143
  114.1 1.9 convolution_add_fusion.12
  116.0 1.2 fusion.145
  119.7 1.2 fusion.143
  121.1 2.1 convolution_add_fusion.12
  123.2 1.2 fusion.145
  127.0 1.2 fusion.143
  128.4 2.1 convolution_add_fusion.12
  130.5 1.2 fusion.145
  134.2 1.2 fusion.143
  135.6 2.1 convolution_add_fusion.12
  137.7 1.2 fusion.145
  141.5 1.2 fusion.143
  142.9 2.1 convolution_add_fusion.12
  144.9 1.2 fusion.145
  148.7 1.2 fusion.143
  150.1 2.1 convolution_add_fusion.12
  152.2 1.2 fusion.145
  156.0 1.2 fusion.143
  157.3 2.1 convolution_add_fusion.12
  159.4 1.2 fusion.145
  163.2 1.2 fusion.143
  164.6 2.1 convolution_add_fusion.12
  166.7 1.2 fusion.145
  171.5 1.8 pad_maximum_fusion
  174.6 71.6 %all-reduce.3.cloned.1.call-done = bf16[400,512]{1,0:T(8,128)(2,1)} async-done(((bf16[400,512]{1,0:T(8,128)(2,1)}), bf16[400,512]{1,0:T(8,128)(2,1)}) %all-reduce.3.cloned.1.call-update) | async-done | bytes 409616
  246.2 3.7 %fusion.58 = f32[50,8192]{1,0:T(8,128)S(1)} fusion(bf16[8192,256]{1,0:T(8,128)(2,1)} %param.17, bf16[400,512]{1,0:T(8,128)(2,1)} %all-reduce.3.cloned.1.call-done, u32[]{:T(128)S(6)} %multiply.1), kind=kOutput, calls=%fused_computation.86 | convolution fusion | flops 209715200 | bytes 5861380 | tf_op jit(solution)/shard_map/dot_general | solution.py:101
  249.9 3.1 %fusion.54 = bf16[50,8192]{1,0:T(8,128)(2,1)} fusion(f32[50,8192]{1,0:T(8,128)S(1)} %fusion.58, bf16[8192,256]{1,0:T(8,128)(2,1)S(1)} %copy-done.1, bf16[400,512]{1,0:T(8,128)(2,1)} %all-reduce.3.cloned.1.call-done, u32[]{:T(128)S(6)} %multiply.1, u32[]{:T(128)S(6)} %convert.28), kind=kOutput, calls=%fused_computation.65 | convolution fusion | flops 210534400 | bytes 6680584 | tf_op jit(solution)/shard_map/dot_general | solution.py:104
  254.5 1.1 copy_bitcast_fusion
  255.6 21.1 %reduce-scatter.2.cloned.1.call-done = bf16[50,2048]{1,0:T(8,128)(2,1)} async-done(((bf16[50,8192]{1,0:T(8,128)(2,1)}), bf16[50,2048]{1,0:T(8,128)(2,1)}) %reduce-scatter.2.cloned.1.call-update) | async-done | bytes 204816 | tf_op jit(solution)/shard_map/reduce_scatter | solution.py:107
  276.7 1.7 add_convert_fusion
  (122 shorter events, 49.6 us)
Async XLA Ops:
  7.2 1.2 copy-start
  7.2 239.0 %all-reduce.3.cloned.1.call-start = ((), (), s32[]{:S(2)}) async-start(), calls=%async_computation.2 | async-start | bytes 819200
  8.3 3.4 %copy-start.2 = (bf16[8192,256]{1,0:T(8,128)(2,1)S(1)}, bf16[8192,256]{1,0:T(8,128)(2,1)}, u32[]{:S(2)}) copy-start(bf16[8192,256]{1,0:T(8,128)(2,1)} %param.17) | copy-start | bytes 12582916
  45.7 6.4 %copy-start.5 = (bf16[256,256]{1,0:T(8,128)(2,1)S(1)}, bf16[256,256]{1,0:T(8,128)(2,1)}, u32[]{:S(2)}) copy-start(bf16[256,256]{1,0:T(8,128)(2,1)} %param.14) | copy-start | bytes 393220
  112.7 60.7 %copy-start.6 = (u32[32]{0:T(128)S(1)}, u32[32]{0:T(128)}, u32[]{:S(2)}) copy-start(u32[32]{0:T(128)} %constant.56) | copy-start | bytes 388
  114.0 3.2 %copy-start.4 = (bf16[656,128]{1,0:T(8,128)(2,1)S(1)}, bf16[656,128]{1,0:T(8,128)(2,1)}, u32[]{:S(2)}) copy-start(bf16[656,128]{1,0:T(8,128)(2,1)} %get-tuple-element.473) | copy-start | bytes 503812 | tf_op jit(solution)/shard_map/while
  121.1 3.3 %copy-start.4 = (bf16[656,128]{1,0:T(8,128)(2,1)S(1)}, bf16[656,128]{1,0:T(8,128)(2,1)}, u32[]{:S(2)}) copy-start(bf16[656,128]{1,0:T(8,128)(2,1)} %get-tuple-element.473) | copy-start | bytes 503812 | tf_op jit(solution)/shard_map/while
  128.4 3.3 %copy-start.4 = (bf16[656,128]{1,0:T(8,128)(2,1)S(1)}, bf16[656,128]{1,0:T(8,128)(2,1)}, u32[]{:S(2)}) copy-start(bf16[656,128]{1,0:T(8,128)(2,1)} %get-tuple-element.473) | copy-start | bytes 503812 | tf_op jit(solution)/shard_map/while
  135.6 3.3 %copy-start.4 = (bf16[656,128]{1,0:T(8,128)(2,1)S(1)}, bf16[656,128]{1,0:T(8,128)(2,1)}, u32[]{:S(2)}) copy-start(bf16[656,128]{1,0:T(8,128)(2,1)} %get-tuple-element.473) | copy-start | bytes 503812 | tf_op jit(solution)/shard_map/while
  142.8 3.3 %copy-start.4 = (bf16[656,128]{1,0:T(8,128)(2,1)S(1)}, bf16[656,128]{1,0:T(8,128)(2,1)}, u32[]{:S(2)}) copy-start(bf16[656,128]{1,0:T(8,128)(2,1)} %get-tuple-element.473) | copy-start | bytes 503812 | tf_op jit(solution)/shard_map/while
  150.1 3.3 %copy-start.4 = (bf16[656,128]{1,0:T(8,128)(2,1)S(1)}, bf16[656,128]{1,0:T(8,128)(2,1)}, u32[]{:S(2)}) copy-start(bf16[656,128]{1,0:T(8,128)(2,1)} %get-tuple-element.473) | copy-start | bytes 503812 | tf_op jit(solution)/shard_map/while
  157.3 3.3 %copy-start.4 = (bf16[656,128]{1,0:T(8,128)(2,1)S(1)}, bf16[656,128]{1,0:T(8,128)(2,1)}, u32[]{:S(2)}) copy-start(bf16[656,128]{1,0:T(8,128)(2,1)} %get-tuple-element.473) | copy-start | bytes 503812 | tf_op jit(solution)/shard_map/while
  164.6 3.3 %copy-start.4 = (bf16[656,128]{1,0:T(8,128)(2,1)S(1)}, bf16[656,128]{1,0:T(8,128)(2,1)}, u32[]{:S(2)}) copy-start(bf16[656,128]{1,0:T(8,128)(2,1)} %get-tuple-element.473) | copy-start | bytes 503812 | tf_op jit(solution)/shard_map/while
  173.3 103.4 %reduce-scatter.2.cloned.1.call-start = ((), (), s32[]{:S(2)}) async-start(), calls=%async_computation.1 | async-start | bytes 1146880 | tf_op jit(solution)/shard_map/reduce_scatter | solution.py:107
  246.2 3.7 %copy-start.1 = (bf16[8192,256]{1,0:T(8,128)(2,1)S(1)}, bf16[8192,256]{1,0:T(8,128)(2,1)}, u32[]{:S(2)}) copy-start(bf16[8192,256]{1,0:T(8,128)(2,1)} %param.18) | copy-start | bytes 12582916
  249.9 26.8 %copy-start.3 = (bf16[50,2048]{1,0:T(8,128)(2,1)S(1)}, bf16[50,2048]{1,0:T(8,128)(2,1)}, u32[]{:S(2)}) copy-start(bf16[50,2048]{1,0:T(8,128)(2,1)} %param.19) | copy-start | bytes 614404
Sparse Core Ops, SparseCore 0:
  173.4 72.7 all-reduce.2
  253.2 23.4 reduce-scatter.1
where the time goes:
time: 289 us; the launch traced here: 285 us
  matrix products  122 us (42%)
  waiting for transfers between devices  92.7 us (32%)
  blocking collectives  32.9 us (11%)
  between operations  14.9 us (5%)
  other arithmetic  12.1 us (4%)
  local copies, waits for them, and re-layouts  10 us (3%)
    unnamed x3, waiting for transfers between devices  71.6 us
    all_gather x1, blocking collectives, per_device(): everyone = lax.all_gather(projected, 'seg', axis=0, tiled=True)  32.9 us
    dot_general x16, matrix products, head_step(): lax.dot_general(probs_b, grad_head, contract_first, preferred_element_typ...  32.4 us
    reduce_scatter x1, waiting for transfers between devices, per_device(): lax.psum_scatter(partial_state.astype(jnp.bfloat16), 'tp', scatter_dimens...  21.1 us
    dot_general x16, matrix products, head_step(): lax.dot_general(query_head, keyset, contract_last, preferred_element_type...  19.4 us
    dot_general x16, matrix products, head_step(): attn = jnp.dot(probs_b, valset, preferred_element_type=jnp.float32)  18.9 us
    dot_general x16, matrix products, head_step(): lax.dot_general(dscores, query_head, contract_first, preferred_element_ty...  17.6 us
    dot_general x16, matrix products, head_step(): lax.dot_general(grad_head, valset, contract_last, preferred_element_type=...  17.3 us
  transfers between devices with their start and end apart: 2, of which 2 were waited for; matrix products, arithmetic and copies ran while one was open for 1% of the time, Pallas kernels for 0%

commit v1 on v0

v1 whole, which is shorter than its diff:
```python
import functools
import math

import jax
import jax.numpy as jnp
from jax import lax
from jax.experimental import pallas as pl
from jax.experimental.pallas import tpu as pltpu
from jax.sharding import PartitionSpec as P

HEADS = 64
KVH = 8
HD = 128
GROUP = HEADS // KVH
SCALE = HD ** (-0.5)
LOG2E = math.log2(math.e)
F32 = jnp.float32
BF16 = jnp.bfloat16
LAST = (((1,), (1,)), ((), ()))
VMEM_LIMIT = 48 * 1024 * 1024


def dot(a, b, dims=(((1,), (0,)), ((), ()))):
    return lax.dot_general(a, b, dims, preferred_element_type=F32)


def params(limit=VMEM_LIMIT):
    return pltpu.CompilerParams(vmem_limit_bytes=limit)


def cost(flops, nbytes):
    return pl.CostEstimate(flops=int(flops), bytes_accessed=int(nbytes), transcendentals=0)


def head_lanes(head):
    return pl.ds(pl.multiple_of(head * HD, HD), HD)


def project_kernel(states_ref, wk_ref, wv_ref, out_ref, acc_ref):
    step = pl.program_id(0)
    width = wk_ref.shape[1]

    @pl.when(step == 0)
    def _():
        acc_ref[...] = jnp.zeros_like(acc_ref)

    states = states_ref[...]
    acc_ref[:, :width] += dot(states, wk_ref[...])
    acc_ref[:, width:] += dot(states, wv_ref[...])

    @pl.when(step == pl.num_programs(0) - 1)
    def _():
        out_ref[...] = acc_ref[...].astype(BF16)


def project(states, w_key, w_value, chunk=1024):
    rows, depth = states.shape
    width = w_key.shape[1]
    return pl.pallas_call(
        project_kernel,
        name="project",
        grid=(depth // chunk,),
        in_specs=[
            pl.BlockSpec((rows, chunk), lambda i: (0, i)),
            pl.BlockSpec((chunk, width), lambda i: (i, 0)),
            pl.BlockSpec((chunk, width), lambda i: (i, 0)),
        ],
        out_specs=pl.BlockSpec((rows, 2 * width), lambda i: (0, 0)),
        out_shape=jax.ShapeDtypeStruct((rows, 2 * width), BF16),
        scratch_shapes=[pltpu.VMEM((rows, 2 * width), F32)],
        compiler_params=params(),
        cost_estimate=cost(4 * rows * depth * width, 4 * depth * width),
    )(states, w_key, w_value)


def causal_bias(count):
    key_pos = lax.broadcasted_iota(jnp.int32, (count, count), 0)
    row_pos = lax.broadcasted_iota(jnp.int32, (count, count), 1)
    return jnp.where(key_pos <= row_pos, 0.0, -jnp.inf).astype(F32)


def own_stats_kernel(unroll, q_ref, g_ref, k_ref, v_ref, stats_ref, bias_ref):
    bias_ref[...] = causal_bias(bias_ref.shape[0])
    keys = k_ref[...]
    values = v_ref[...]

    def one(head, _):
        lanes = head_lanes(head)
        scores = dot(keys, q_ref[:, lanes], LAST) * (SCALE * LOG2E) + bias_ref[...]
        top = jnp.max(scores, axis=0, keepdims=True)
        weights = jnp.exp2(scores - top)
        total = jnp.sum(weights, axis=0, keepdims=True)
        dprobs = dot(values, g_ref[:, lanes], LAST)
        mixed = jnp.sum(weights * dprobs, axis=0, keepdims=True)
        stats_ref[head, 0:1, :] = top
        stats_ref[head, 1:2, :] = total
        stats_ref[head, 2:3, :] = mixed
        return 0

    lax.fori_loop(0, GROUP, one, 0, unroll=unroll)


def own_stats(queries, out_grad, keys_own, values_own, unroll):
    rows = queries.shape[0]
    kv_local = keys_own.shape[1] // HD
    heads = kv_local * GROUP
    wide = pl.BlockSpec((rows, GROUP * HD), lambda i: (0, i))
    narrow = pl.BlockSpec((rows, HD), lambda i: (0, i))
    return pl.pallas_call(
        functools.partial(own_stats_kernel, unroll),
        name="own_stats",
        grid=(kv_local,),
        in_specs=[wide, wide, narrow, narrow],
        out_specs=pl.BlockSpec((GROUP, 8, rows), lambda i: (i, 0, 0)),
        out_shape=jax.ShapeDtypeStruct((heads, 8, rows), F32),
        scratch_shapes=[pltpu.VMEM((rows, rows), F32)],
        compiler_params=params(),
        cost_estimate=cost(40 * heads * rows * rows * HD, 4 * rows * heads * HD),
    )(queries, out_grad, keys_own, values_own)


def summary_kernel(
    unroll, count, slots, seg_ref, q_ref, g_ref, k_ref, v_ref, own_ref,
    ds_ref, stats_ref, dk_ref, dv_ref, bias_ref, dk_acc, dv_acc,
):
    position = seg_ref[0]
    rows = q_ref.shape[0]
    padded = k_ref.shape[0]
    row = lax.broadcasted_iota(jnp.int32, (padded, rows), 0)
    bias = jnp.full((padded, rows), -jnp.inf, F32)
    for slot in range(1, slots):
        start = (slot - 1) * count
        shown = jnp.where((position ^ slot) < position, 0.0, -jnp.inf).astype(F32)
        bias = jnp.where((row >= start) & (row < start + count), shown, bias)
    bias_ref[...] = bias
    dk_acc[...] = jnp.zeros_like(dk_acc)
    dv_acc[...] = jnp.zeros_like(dv_acc)
    keys = k_ref[...]
    values = v_ref[...]

    def one(head, _):
        lanes = head_lanes(head)
        query = q_ref[:, lanes]
        grad = g_ref[:, lanes]
        scores = dot(keys, query, LAST) * (SCALE * LOG2E) + bias_ref[...]
        own_top = own_ref[head, 0:1, :]
        top = jnp.maximum(jnp.max(scores, axis=0, keepdims=True), own_top)
        weights = jnp.exp2(scores - top)
        shrink = jnp.exp2(own_top - top)
        total = jnp.sum(weights, axis=0, keepdims=True) + own_ref[head, 1:2, :] * shrink
        inverse = 1.0 / total
        probs = weights * inverse
        dprobs = dot(values, grad, LAST)
        delta = (
            jnp.sum(probs * dprobs, axis=0, keepdims=True)
            + own_ref[head, 2:3, :] * shrink * inverse
        )
        dscores = (probs * (dprobs - delta)).astype(BF16)
        ds_ref[head] = dscores
        stats_ref[head, 0:1, :] = top
        stats_ref[head, 1:2, :] = inverse
        stats_ref[head, 2:3, :] = delta
        dk_acc[...] += dot(dscores, query)
        dv_acc[...] += dot(probs.astype(BF16), grad)
        return 0

    lax.fori_loop(0, GROUP, one, 0, unroll=unroll)
    dk_ref[...] = (dk_acc[...] * SCALE).astype(BF16)
    dv_ref[...] = dv_acc[...].astype(BF16)


def summary_part(position, queries, out_grad, keys, values, own, count, slots, unroll):
    rows = queries.shape[0]
    padded = keys.shape[0]
    kv_local = keys.shape[1] // HD
    heads = kv_local * GROUP
    wide = pl.BlockSpec((rows, GROUP * HD), lambda i, s: (0, i))
    narrow = pl.BlockSpec((padded, HD), lambda i, s: (0, i))
    stats = pl.BlockSpec((GROUP, 8, rows), lambda i, s: (i, 0, 0))
    return pl.pallas_call(
        functools.partial(summary_kernel, unroll, count, slots),
        name="summary_part",
        grid_spec=pltpu.PrefetchScalarGridSpec(
            num_scalar_prefetch=1,
            grid=(kv_local,),
            in_specs=[wide, wide, narrow, narrow, stats],
            out_specs=[
                pl.BlockSpec((GROUP, padded, rows), lambda i, s: (i, 0, 0)),
                stats,
                narrow,
                narrow,
            ],
            scratch_shapes=[
                pltpu.VMEM((padded, rows), F32),
                pltpu.VMEM((padded, HD), F32),
                pltpu.VMEM((padded, HD), F32),
            ],
        ),
        out_shape=[
            jax.ShapeDtypeStruct((heads, padded, rows), BF16),
            jax.ShapeDtypeStruct((heads, 8, rows), F32),
            jax.ShapeDtypeStruct((padded, kv_local * HD), BF16),
            jax.ShapeDtypeStruct((padded, kv_local * HD), BF16),
        ],
        compiler_params=params(),
        cost_estimate=cost(40 * heads * rows * padded * HD, 4 * rows * heads * HD),
    )(position, queries, out_grad, keys, values, own)


def own_grads_kernel(
    unroll, q_ref, g_ref, k_ref, v_ref, sk_ref, ds_ref, stats_ref,
    dq_ref, dk_ref, dv_ref, bias_ref, dk_acc, dv_acc,
):
    bias_ref[...] = causal_bias(bias_ref.shape[0])
    dk_acc[...] = jnp.zeros_like(dk_acc)
    dv_acc[...] = jnp.zeros_like(dv_acc)
    keys = k_ref[...]
    values = v_ref[...]
    keys_t = keys.T
    sum_keys_t = sk_ref[...].T

    def one(head, _):
        lanes = head_lanes(head)
        query = q_ref[:, lanes]
        grad = g_ref[:, lanes]
        scores = dot(keys, query, LAST) * (SCALE * LOG2E) + bias_ref[...]
        top = stats_ref[head, 0:1, :]
        inverse = stats_ref[head, 1:2, :]
        delta = stats_ref[head, 2:3, :]
        probs = jnp.exp2(scores - top) * inverse
        dprobs = dot(values, grad, LAST)
        dscores = (probs * (dprobs - delta)).astype(BF16)
        dk_acc[...] += dot(dscores, query)
        dv_acc[...] += dot(probs.astype(BF16), grad)
        dquery = dot(keys_t, dscores) + dot(sum_keys_t, ds_ref[head])
        dq_ref[:, lanes] = (dquery * SCALE).T.astype(BF16)
        return 0

    lax.fori_loop(0, GROUP, one, 0, unroll=unroll)
    dk_ref[...] = (dk_acc[...] * SCALE).astype(BF16)
    dv_ref[...] = dv_acc[...].astype(BF16)


def own_grads(queries, out_grad, keys_own, values_own, sum_keys, dscores, stats, unroll):
    rows = queries.shape[0]
    padded = sum_keys.shape[0]
    kv_local = keys_own.shape[1] // HD
    heads = kv_local * GROUP
    wide = pl.BlockSpec((rows, GROUP * HD), lambda i: (0, i))
    narrow = pl.BlockSpec((rows, HD), lambda i: (0, i))
    return pl.pallas_call(
        functools.partial(own_grads_kernel, unroll),
        name="own_grads",
        grid=(kv_local,),
        in_specs=[
            wide,
            wide,
            narrow,
            narrow,
            pl.BlockSpec((padded, HD), lambda i: (0, i)),
            pl.BlockSpec((GROUP, padded, rows), lambda i: (i, 0, 0)),
            pl.BlockSpec((GROUP, 8, rows), lambda i: (i, 0, 0)),
        ],
        out_specs=[wide, narrow, narrow],
        out_shape=[
            jax.ShapeDtypeStruct((rows, heads * HD), BF16),
            jax.ShapeDtypeStruct((rows, kv_local * HD), BF16),
            jax.ShapeDtypeStruct((rows, kv_local * HD), BF16),
        ],
        scratch_shapes=[
            pltpu.VMEM((rows, rows), F32),
            pltpu.VMEM((rows, HD), F32),
            pltpu.VMEM((rows, HD), F32),
        ],
        compiler_params=params(),
        cost_estimate=cost(40 * heads * rows * rows * HD, 4 * rows * heads * HD),
    )(queries, out_grad, keys_own, values_own, sum_keys, dscores, stats)


def state_kernel(order_ref, dk_ref, dv_ref, wk_ref, wv_ref, out_ref):
    total = dot(dk_ref[...], wk_ref[...], LAST) + dot(dv_ref[...], wv_ref[...], LAST)
    out_ref[...] = total.astype(BF16)


def state_part(order, emitted_k, emitted_v, w_key, w_value, slices, chunk=1024):
    rows, width = emitted_k.shape
    depth = w_key.shape[0]
    per = depth // slices // chunk
    steps = order.shape[0] * per
    weight = pl.BlockSpec((chunk, width), lambda i, o: (o[i // per] * per + i % per, 0))
    whole = pl.BlockSpec((rows, width), lambda i, o: (0, 0))
    return pl.pallas_call(
        state_kernel,
        name="state_part",
        grid_spec=pltpu.PrefetchScalarGridSpec(
            num_scalar_prefetch=1,
            grid=(steps,),
            in_specs=[whole, whole, weight, weight],
            out_specs=pl.BlockSpec((rows, chunk), lambda i, o: (0, i)),
        ),
        out_shape=jax.ShapeDtypeStruct((rows, steps * chunk), BF16),
        compiler_params=params(),
        cost_estimate=cost(4 * rows * steps * chunk * width, 4 * steps * chunk * width),
    )(order, emitted_k, emitted_v, w_key, w_value)


def exchange(block, axis, size, bit):
    return lax.ppermute(block, axis, [(i, i ^ bit) for i in range(size)])


def per_device(
    queries, keys_own, values_own, out_grad, summary_states, w_key, w_value, summary_grad
):
    rows = queries.shape[0]
    width = keys_own.shape[1]
    count = summary_states.shape[0]
    n_seg = lax.axis_size("seg")
    n_tp = lax.axis_size("tp")
    position = lax.axis_index("seg").astype(jnp.int32).reshape(1)
    mine = lax.axis_index("tp").astype(jnp.int32)
    unroll = GROUP if n_seg <= 8 else 1

    projected = project(summary_states, w_key, w_value)
    own = own_stats(queries, out_grad, keys_own, values_own, unroll)

    chunks = {0: projected}
    bit = n_seg // 2
    while bit:
        held = sorted(chunks)
        got = exchange(jnp.concatenate([chunks[j] for j in held], 0), "seg", n_seg, bit)
        for at, j in enumerate(held):
            chunks[j ^ bit] = got[at * count : (at + 1) * count]
        bit //= 2
    shown = (n_seg - 1) * count
    padded = -(-shown // 16) * 16
    tail = [jnp.zeros((padded - shown, 2 * width), BF16)] if padded > shown else []
    gathered = jnp.concatenate([chunks[j] for j in range(1, n_seg)] + tail, 0)
    sum_keys, sum_values = gathered[:, :width], gathered[:, width:]

    dscores, stats, dk, dv = summary_part(
        position, queries, out_grad, sum_keys, sum_values, own, count, n_seg, unroll
    )

    both = jnp.concatenate([dk, dv], 1)
    parts = {j: both[(j - 1) * count : j * count].astype(F32) for j in range(1, n_seg)}
    bit = 1
    while bit < n_seg:
        sent = sorted(j for j in parts if j & bit)
        block = jnp.concatenate([parts.pop(j).astype(BF16) for j in sent], 0)
        got = exchange(block, "seg", n_seg, bit).astype(F32)
        for at, j in enumerate(sent):
            piece = got[at * count : (at + 1) * count]
            parts[j ^ bit] = parts[j ^ bit] + piece if j ^ bit in parts else piece
        bit *= 2
    emitted = parts[0].astype(BF16)

    query_grad, key_grad, value_grad = own_grads(
        queries, out_grad, keys_own, values_own, sum_keys, dscores, stats, unroll
    )

    slice_width = w_key.shape[0] // n_tp
    far = list(range(n_tp - 1, 1, -1))
    near = [1, 0] if n_tp > 1 else [0]
    terms = {}
    for group in (far, near):
        if group:
            order = jnp.stack([mine ^ j for j in group])
            block = state_part(
                order, emitted[:, :width], emitted[:, width:], w_key, w_value, n_tp
            )
            for at, j in enumerate(group):
                terms[j] = block[:, at * slice_width : (at + 1) * slice_width].astype(F32)
    bit = 1
    while bit < n_tp:
        for group in ([j for j in terms if j & bit and j > bit], [bit]):
            if not group:
                continue
            block = jnp.concatenate([terms.pop(j).astype(BF16) for j in group], 1)
            got = exchange(block, "tp", n_tp, bit).astype(F32)
            for at, j in enumerate(group):
                terms[j ^ bit] += got[:, at * slice_width : (at + 1) * slice_width]
        bit *= 2
    state_grad = (terms[0] + summary_grad.astype(F32)).astype(BF16)
    return (query_grad, key_grad, value_grad, state_grad)


def solution(mesh):
    placed = (
        P("seg", "tp"),
        P("seg", "tp"),
        P("seg", "tp"),
        P("seg", "tp"),
        P("seg", None),
        P(None, "tp"),
        P(None, "tp"),
        P("seg", "tp"),
    )
    return jax.shard_map(
        per_device,
        mesh=mesh,
        in_specs=placed,
        out_specs=(P("seg", "tp"), P("seg", "tp"), P("seg", "tp"), P("seg", "tp")),
        check_vma=False,
    )
```

time: 289 us -> 79.6 us (0.28); the launches traced: 285 us -> 79.2 us
  matrix products: 122 us -> 0 us
  waiting for transfers between devices: 92.7 us -> 18.4 us
  blocking collectives: 32.9 us -> 0 us
  Pallas kernels: 0 us -> 31.3 us
  starting transfers between devices: 0.08 us -> 15.2 us
  between operations: 14.9 us -> 0.85 us
  other arithmetic: 12.1 us -> 2.93 us
    dot_general x100 -> x0, matrix products: 122 us -> none  [the longest x16 32.4 us: head_step(): lax.dot_general(probs_b, grad_head, contract_first, preferred_element_typ...]
    unnamed x3 -> x0, waiting for transfers between devices: 71.6 us -> none
    all_gather x1 -> x0, blocking collectives: 32.9 us -> none  [per_device(): everyone = lax.all_gather(projected, 'seg', axis=0, tiled=True)]
    pallas_call x0 -> x6, Pallas kernels: none -> 31.3 us  [the longest x1 8.48 us: summary_part(): pl.pallas_call(functools.partial(summary_kernel, unroll, count, slots), n...]
    reduce_scatter x1 -> x0, waiting for transfers between devices: 21.1 us -> none  [per_device(): lax.psum_scatter(partial_state.astype(jnp.bfloat16), 'tp', scatter_dimens...]
    ppermute x0 -> x9, waiting for transfers between devices: none -> 18.4 us  [exchange(): return lax.ppermute(block, axis, [(i, i ^ bit) for i in range(size)])]
    ppermute x0 -> x9, starting transfers between devices: none -> 15.2 us  [exchange(): return lax.ppermute(block, axis, [(i, i ^ bit) for i in range(size)])]
    concatenate x4, other arithmetic: 4.73 us -> 0.8 us  [the longest x2 0.72 us: per_device(): block = jnp.concatenate([parts.pop(j).astype(BF16) for j in sent], 0)]
  transfers between devices with their start and end apart: 2 -> 9, of which waited for: 2 -> 6; matrix products, arithmetic and copies ran while one was open for 1% -> 1% of each run, Pallas kernels for 0% -> 16%
where the time goes in v1:
time: 79.6 us; the launch traced here: 79.2 us
  Pallas kernels  31.3 us (39%)
  waiting for transfers between devices  18.4 us (23%)
  starting transfers between devices  15.2 us (19%)
  local copies, waits for them, and re-layouts  10.4 us (13%)
  other arithmetic  2.93 us (4%)
  between operations  0.85 us (1%)
    ppermute x9, waiting for transfers between devices, exchange(): return lax.ppermute(block, axis, [(i, i ^ bit) for i in range(size)])  18.4 us
    ppermute x9, starting transfers between devices, exchange(): return lax.ppermute(block, axis, [(i, i ^ bit) for i in range(size)])  15.2 us
    unnamed x23, local copies, waits for them, and re-layouts  9.31 us
    pallas_call x1, Pallas kernels, summary_part(): pl.pallas_call(functools.partial(summary_kernel, unroll, count, slots), n...  8.48 us
    pallas_call x2, Pallas kernels, state_part(): pl.pallas_call(state_kernel, name='state_part', grid_spec=pltpu.PrefetchS...  8.45 us
    pallas_call x1, Pallas kernels, own_grads(): pl.pallas_call(functools.partial(own_grads_kernel, unroll), name='own_gra...  6.29 us
    pallas_call x1, Pallas kernels, project(): pl.pallas_call(project_kernel, name='project', grid=(depth // chunk,), in...  6.07 us
    pallas_call x1, Pallas kernels, own_stats(): pl.pallas_call(functools.partial(own_stats_kernel, unroll), name='own_sta...  2.06 us
  transfers between devices with their start and end apart: 9, of which 6 were waited for; matrix products, arithmetic and copies ran while one was open for 1% of the time, Pallas kernels for 16%

profile of v1, /device:TPU:0, one launch (start us, length us, event | category | flops | bytes accessed | tf_op | source)
XLA Modules:
  0.0 79.2 jit_solution(8042543441189433907)
XLA Ops:
  0.6 0.0 copy-start
  0.6 2.2 %copy-done = bf16[8192,256]{1,0:T(8,128)(2,1)S(1)} copy-done((bf16[8192,256]{1,0:T(8,128)(2,1)S(1)}, bf16[8192,256]{1,0:T(8,128)(2,1)}, u32[]{:S(2)}) %copy-start) | copy-done | bytes 4194328
  2.8 0.0 copy-start.3
  2.8 1.2 %copy-done.3 = bf16[50,8192]{1,0:T(8,128)(2,1)S(1)} copy-done((bf16[50,8192]{1,0:T(8,128)(2,1)S(1)}, bf16[50,8192]{1,0:T(8,128)(2,1)}, u32[]{:S(2)}) %copy-start.3) | copy-done | bytes 819224
  4.0 0.0 copy-start.4
  4.0 0.0 copy-start.5
  4.0 0.0 copy-start.6
  4.0 0.0 copy-start.7
  4.0 6.1 %project.1 = bf16[50,512]{1,0:T(8,128)(2,1)S(1)} custom-call(bf16[50,8192]{1,0:T(8,128)(2,1)S(1)} %copy-done.3, bf16[8192,256]{1,0:T(8,128)(2,1)S(1)} %copy-done, bf16[8192,256]{1,0:T(8,128)(2,1)} %wv_ref.5), custom_call_target="tpu_custom_call" | custom-call | flops 419430400 | bytes 8388608 | tf_op jit(solution)/shard_map/project/pallas_call | solution.py:59
  10.1 4.1 %collective-permute-start = (bf16[50,512]{1,0:T(8,128)(2,1)S(1)}, bf16[50,512]{1,0:T(8,128)(2,1)S(1)}, u32[]{:S(2)}, u32[]{:S(2)}) collective-permute-start(bf16[50,512]{1,0:T(8,128)(2,1)S(1)} %project.1), channel_id=1, source_target_pairs={{0,16},{4,20},{8,24},{12,28},{16,0},{20,4},{24,8},{28,12},{1,17},{... | collective-permute-start | bytes 153608 | tf_op jit(solution)/shard_map/ppermute | solution.py:308
  14.2 2.8 %collective-permute-done = bf16[50,512]{1,0:T(8,128)(2,1)S(1)} collective-permute-done((bf16[50,512]{1,0:T(8,128)(2,1)S(1)}, bf16[50,512]{1,0:T(8,128)(2,1)S(1)}, u32[]{:S(2)}, u32[]{:S(2)}) %collective-permute-start) | collective-permute-done | bytes 51232 | tf_op jit(solution)/shard_map/ppermute | solution.py:308
  17.0 1.4 %collective-permute-start.1 = (bf16[100,512]{1,0:T(8,128)(2,1)S(1)}, bf16[100,512]{1,0:T(8,128)(2,1)S(1)}, u32[]{:S(2)}, u32[]{:S(2)}) collective-permute-start(bf16[100,512]{1,0:T(8,128)(2,1)S(1)} %pad_maximum_fusion.2), channel_id=1, source_target_pairs={{0,8},{4,12},{8,0},{12,4},{16,24},{20,28},{24,16},{28,20},{1,9},{5... | collective-permute-start | bytes 307208 | tf_op jit(solution)/shard_map/ppermute | solution.py:308
  18.3 3.4 %collective-permute-done.1 = bf16[100,512]{1,0:T(8,128)(2,1)S(1)} collective-permute-done((bf16[100,512]{1,0:T(8,128)(2,1)S(1)}, bf16[100,512]{1,0:T(8,128)(2,1)S(1)}, u32[]{:S(2)}, u32[]{:S(2)}) %collective-permute-start.1) | collective-permute-done | bytes 102432 | tf_op jit(solution)/shard_map/ppermute | solution.py:308
  21.8 0.1 pad_maximum_fusion
  21.8 1.8 %collective-permute-start.2 = (bf16[200,512]{1,0:T(8,128)(2,1)S(1)}, bf16[200,512]{1,0:T(8,128)(2,1)S(1)}, u32[]{:S(2)}, u32[]{:S(2)}) collective-permute-start(bf16[200,512]{1,0:T(8,128)(2,1)S(1)} %pad_maximum_fusion), channel_id=1, source_target_pairs={{0,4},{4,0},{8,12},{12,8},{16,20},{20,16},{24,28},{28,24},{1,5},{5... | collective-permute-start | bytes 614408 | tf_op jit(solution)/shard_map/ppermute | solution.py:308
  23.6 0.0 copy-done.4
  23.6 0.0 copy-done.5
  23.6 0.0 copy-done.6
  23.6 0.0 copy-done.7
  23.6 2.1 %own_stats.1.own_ref = f32[16,8,256]{2,1,0:T(8,128)S(1)} custom-call(bf16[256,2048]{1,0:T(8,128)(2,1)S(1)} %copy-done.4, bf16[256,2048]{1,0:T(8,128)(2,1)S(1)} %copy-done.5, bf16[256,256]{1,0:T(8,128)(2,1)S(1)} %copy-done.6, bf16[256,256]{1,0:T(8,128)(2,1)S(1)} %copy-done.7), custom_call_target="tpu_custom_call" | custom-call | flops 5368709120 | bytes 2097152 | tf_op jit(solution)/shard_map/own_stats/pallas_call | solution.py:109
  25.7 2.0 %collective-permute-done.2 = bf16[200,512]{1,0:T(8,128)(2,1)S(1)} collective-permute-done((bf16[200,512]{1,0:T(8,128)(2,1)S(1)}, bf16[200,512]{1,0:T(8,128)(2,1)S(1)}, u32[]{:S(2)}, u32[]{:S(2)}) %collective-permute-start.2) | collective-permute-done | bytes 204832 | tf_op jit(solution)/shard_map/ppermute | solution.py:308
  27.7 1.0 %concatenate.20 = bf16[352,512]{1,0:T(8,128)(2,1)S(1)} concatenate(bf16[50,512]{1,0:T(8,128)(2,1)S(1)} %get-tuple-element.29, bf16[50,512]{1,0:T(8,128)(2,1)S(1)} %get-tuple-element.30, bf16[50,512]{1,0:T(8,128)(2,1)S(1)} %get-tuple-element.28, bf16[50,512]{1,0:T(8,128)(2,1)S(1)} %collective-permute-done, bf16[50,512]{1,0:T(8,128)(2,1)S(1)} %get-tuple-element.27, ...), dimensions={0} | concatenate | bytes 720896 | tf_op jit(solution)/shard_map/concatenate | solution.py:337
  28.7 8.5 %summary_part.1 = (bf16[16,352,256]{2,1,0:T(8,128)(2,1)S(1)}, f32[16,8,256]{2,1,0:T(8,128)S(1)}, bf16[352,256]{1,0:T(8,128)(2,1)S(1)}, bf16[352,256]{1,0:T(8,128)(2,1)S(1)}) custom-call(s32[1]{0:T(128)} %bitcast.seg_ref, bf16[256,2048]{1,0:T(8,128)(2,1)S(1)} %copy-done.4, bf16[256,2048]{1,0:T(8,128)(2,1)S(1)} %copy-done.5, ...), custom_call_target="tpu_custom_call" | custom-call | flops 7381975040 | bytes 2097152 | tf_op jit(solution)/shard_map/summary_part/pallas_call | solution.py:180
  37.2 0.0 copy-start.8
  37.2 1.5 %copy-done.8 = bf16[16,352,256]{2,1,0:T(8,128)(2,1)} copy-done((bf16[16,352,256]{2,1,0:T(8,128)(2,1)}, bf16[16,352,256]{2,1,0:T(8,128)(2,1)S(1)}, u32[]{:S(2)}) %copy-start.8) | copy-done | bytes 2883608
  38.8 0.1 pad_maximum_fusion.1
  38.9 1.8 %collective-permute-start.3 = (bf16[200,512]{1,0:T(8,128)(2,1)S(1)}, bf16[200,512]{1,0:T(8,128)(2,1)S(1)}, u32[]{:S(2)}, u32[]{:S(2)}) collective-permute-start(bf16[200,512]{1,0:T(8,128)(2,1)S(1)} %pad_maximum_fusion.1), channel_id=1, source_target_pairs={{0,4},{4,0},{8,12},{12,8},{16,20},{20,16},{24,28},{28,24},{1,5},{5... | collective-permute-start | bytes 614408 | tf_op jit(solution)/shard_map/ppermute | solution.py:308
  40.7 4.0 %collective-permute-done.3 = bf16[200,512]{1,0:T(8,128)(2,1)S(1)} collective-permute-done((bf16[200,512]{1,0:T(8,128)(2,1)S(1)}, bf16[200,512]{1,0:T(8,128)(2,1)S(1)}, u32[]{:S(2)}, u32[]{:S(2)}) %collective-permute-start.3) | collective-permute-done | bytes 204832 | tf_op jit(solution)/shard_map/ppermute | solution.py:308
  44.7 0.1 fusion.4
  44.8 0.7 pad_maximum_fusion.3
  45.5 1.3 %collective-permute-start.4 = (bf16[100,512]{1,0:T(8,128)(2,1)}, bf16[100,512]{1,0:T(8,128)(2,1)S(1)}, u32[]{:S(2)}, u32[]{:S(2)}) collective-permute-start(bf16[100,512]{1,0:T(8,128)(2,1)} %pad_maximum_fusion.3), channel_id=1, source_target_pairs={{0,8},{4,12},{8,0},{12,4},{16,24},{20,28},{24,16},{28,20},{1,9},{5... | collective-permute-start | bytes 307208 | tf_op jit(solution)/shard_map/ppermute | solution.py:308
  46.8 3.6 %collective-permute-done.4 = bf16[100,512]{1,0:T(8,128)(2,1)S(1)} collective-permute-done((bf16[100,512]{1,0:T(8,128)(2,1)}, bf16[100,512]{1,0:T(8,128)(2,1)S(1)}, u32[]{:S(2)}, u32[]{:S(2)}) %collective-permute-start.4) | collective-permute-done | bytes 102432 | tf_op jit(solution)/shard_map/ppermute | solution.py:308
  50.5 2.5 %collective-permute-start.5 = (bf16[50,512]{1,0:T(8,128)(2,1)S(1)}, bf16[50,512]{1,0:T(8,128)(2,1)S(1)}, u32[]{:S(2)}, u32[]{:S(2)}) collective-permute-start(bf16[50,512]{1,0:T(8,128)(2,1)S(1)} %fusion), channel_id=1, source_target_pairs={{0,16},{4,20},{8,24},{12,28},{16,0},{20,4},{24,8},{28,12},{1,17},{... | collective-permute-start | bytes 153608 | tf_op jit(solution)/shard_map/ppermute | solution.py:308
  53.0 0.1 pad_add_fusion.1.order_ref
  53.1 2.6 %collective-permute-done.5 = bf16[50,512]{1,0:T(8,128)(2,1)S(1)} collective-permute-done((bf16[50,512]{1,0:T(8,128)(2,1)S(1)}, bf16[50,512]{1,0:T(8,128)(2,1)S(1)}, u32[]{:S(2)}, u32[]{:S(2)}) %collective-permute-start.5) | collective-permute-done | bytes 51232 | tf_op jit(solution)/shard_map/ppermute | solution.py:308
  55.6 0.0 copy-start.1
  55.7 2.2 %copy-done.1 = bf16[8192,256]{1,0:T(8,128)(2,1)S(1)} copy-done((bf16[8192,256]{1,0:T(8,128)(2,1)S(1)}, bf16[8192,256]{1,0:T(8,128)(2,1)}, u32[]{:S(2)}) %copy-start.1) | copy-done | bytes 4194328
  57.8 4.1 %state_part.3 = bf16[50,4096]{1,0:T(8,128)(2,1)S(1)} custom-call(s32[2]{0:T(128)S(1)} %pad_add_fusion.1.order_ref, bf16[50,256]{1,0:T(8,128)(2,1)S(1)} %get-tuple-element.33.dk_ref, bf16[50,256]{1,0:T(8,128)(2,1)S(1)} %get-tuple-element.32.dv_ref, bf16[8192,256]{1,0:T(8,128)(2,1)S(1)} %copy-done.1, bf16[8192,256]{1,0:T(8,128)(2,1)} %wv_ref.5), custom_call_target="tpu_custom_call" | custom-call | flops 209715200 | bytes 4194304 | tf_op jit(solution)/shard_map/state_part/pallas_call | solution.py:292
  62.0 0.1 collective-permute-start.7
  62.0 0.1 pad_add_fusion.order_ref
  62.1 0.0 copy-start.2
  62.1 2.2 %copy-done.2 = bf16[8192,256]{1,0:T(8,128)(2,1)S(1)} copy-done((bf16[8192,256]{1,0:T(8,128)(2,1)S(1)}, bf16[8192,256]{1,0:T(8,128)(2,1)}, u32[]{:S(2)}) %copy-start.2) | copy-done | bytes 4194328
  64.3 0.0 copy-start.9
  64.3 4.4 %state_part.2 = bf16[50,4096]{1,0:T(8,128)(2,1)S(1)} custom-call(s32[2]{0:T(128)S(1)} %pad_add_fusion.order_ref, bf16[50,256]{1,0:T(8,128)(2,1)S(1)} %get-tuple-element.33.dk_ref, bf16[50,256]{1,0:T(8,128)(2,1)S(1)} %get-tuple-element.32.dv_ref, bf16[8192,256]{1,0:T(8,128)(2,1)S(1)} %copy-done.2, bf16[8192,256]{1,0:T(8,128)(2,1)} %wv_ref.5), custom_call_target="tpu_custom_call" | custom-call | flops 209715200 | bytes 4194304 | tf_op jit(solution)/shard_map/state_part/pallas_call | solution.py:292
  68.7 0.6 collective-permute-start.6
  69.3 0.0 collective-permute-done.7
  69.3 1.0 %add_convert_fusion.1 = bf16[50,2048]{1,0:T(8,128)(2,1)S(1)} fusion(bf16[50,2048]{1,0:T(8,128)(2,1)} %collective-permute-done.7, bf16[50,4096]{1,0:T(8,128)(2,1)S(1)} %state_part.3), kind=kLoop, calls=%fused_computation.1 | loop fusion | flops 409600 | bytes 614400 | tf_op jit(solution)/shard_map/convert_element_type | solution.py:378
  70.3 1.8 %collective-permute-start.8 = (bf16[50,2048]{1,0:T(8,128)(2,1)S(1)}, bf16[50,2048]{1,0:T(8,128)(2,1)S(1)}, u32[]{:S(2)}, u32[]{:S(2)}) collective-permute-start(bf16[50,2048]{1,0:T(8,128)(2,1)S(1)} %add_convert_fusion.1), channel_id=1, source_target_pairs={{0,2},{1,3},{2,0},{3,1},{4,6},{5,7},{6,4},{7,5},{8,10},{9,11},{10,... | collective-permute-start | bytes 614408 | tf_op jit(solution)/shard_map/ppermute | solution.py:308
  72.1 0.0 copy-done.9
  72.1 0.0 copy-start.10
  72.1 6.3 %own_grads.1 = (bf16[256,2048]{1,0:T(8,128)(2,1)}, bf16[256,256]{1,0:T(8,128)(2,1)}, bf16[256,256]{1,0:T(8,128)(2,1)}) custom-call(bf16[256,2048]{1,0:T(8,128)(2,1)S(1)} %copy-done.4, bf16[256,2048]{1,0:T(8,128)(2,1)S(1)} %copy-done.5, bf16[256,256]{1,0:T(8,128)(2,1)S(1)} %copy-done.6, bf16[256,256]{1,0:T(8,128)(2,1)S(1)} %copy-done.7, ...), custom_call_target="tpu_custom_call" | custom-call | flops 5368709120 | bytes 2097152 | tf_op jit(solution)/shard_map/own_grads/pallas_call | solution.py:251
  78.4 0.0 collective-permute-done.6
  78.4 0.0 collective-permute-done.8
  78.4 0.0 copy-done.10
  78.4 0.8 %add_convert_fusion = bf16[50,2048]{1,0:T(8,128)(2,1)} fusion(bf16[50,2048]{1,0:T(8,128)(2,1)S(1)} %copy-done.10, bf16[50,2048]{1,0:T(8,128)(2,1)S(1)} %collective-permute-done.8, bf16[50,2048]{1,0:T(8,128)(2,1)S(1)} %collective-permute-done.6, bf16[50,4096]{1,0:T(8,128)(2,1)S(1)} %state_part.2), kind=kLoop, calls=%fused_computation | loop fusion | flops 819200 | bytes 1024000 | tf_op jit(solution)/shard_map/convert_element_type | solution.py:383
  (15 shorter events, 0.3 us)
Async XLA Ops:
  0.6 2.2 %copy-start = (bf16[8192,256]{1,0:T(8,128)(2,1)S(1)}, bf16[8192,256]{1,0:T(8,128)(2,1)}, u32[]{:S(2)}) copy-start(bf16[8192,256]{1,0:T(8,128)(2,1)} %wk_ref.5) | copy-start | bytes 12582916
  2.8 1.2 %copy-start.3 = (bf16[50,8192]{1,0:T(8,128)(2,1)S(1)}, bf16[50,8192]{1,0:T(8,128)(2,1)}, u32[]{:S(2)}) copy-start(bf16[50,8192]{1,0:T(8,128)(2,1)} %states_ref.1) | copy-start | bytes 2457604
  4.0 19.6 %copy-start.4 = (bf16[256,2048]{1,0:T(8,128)(2,1)S(1)}, bf16[256,2048]{1,0:T(8,128)(2,1)}, u32[]{:S(2)}) copy-start(bf16[256,2048]{1,0:T(8,128)(2,1)} %q_ref.5) | copy-start | bytes 3145732
  4.0 19.6 %copy-start.5 = (bf16[256,2048]{1,0:T(8,128)(2,1)S(1)}, bf16[256,2048]{1,0:T(8,128)(2,1)}, u32[]{:S(2)}) copy-start(bf16[256,2048]{1,0:T(8,128)(2,1)} %g_ref.5) | copy-start | bytes 3145732
  4.0 19.6 %copy-start.6 = (bf16[256,256]{1,0:T(8,128)(2,1)S(1)}, bf16[256,256]{1,0:T(8,128)(2,1)}, u32[]{:S(2)}) copy-start(bf16[256,256]{1,0:T(8,128)(2,1)} %k_ref.3) | copy-start | bytes 393220
  4.0 19.6 %copy-start.7 = (bf16[256,256]{1,0:T(8,128)(2,1)S(1)}, bf16[256,256]{1,0:T(8,128)(2,1)}, u32[]{:S(2)}) copy-start(bf16[256,256]{1,0:T(8,128)(2,1)} %v_ref.3) | copy-start | bytes 393220
  10.1 6.9 %collective-permute-start = (bf16[50,512]{1,0:T(8,128)(2,1)S(1)}, bf16[50,512]{1,0:T(8,128)(2,1)S(1)}, u32[]{:S(2)}, u32[]{:S(2)}) collective-permute-start(bf16[50,512]{1,0:T(8,128)(2,1)S(1)} %project.1), channel_id=1, source_target_pairs={{0,16},{4,20},{8,24},{12,28},{16,0},{20,4},{24,8},{28,12},{1,17},{... | collective-permute-start | bytes 153608 | tf_op jit(solution)/shard_map/ppermute | solution.py:308
  17.0 4.8 %collective-permute-start.1 = (bf16[100,512]{1,0:T(8,128)(2,1)S(1)}, bf16[100,512]{1,0:T(8,128)(2,1)S(1)}, u32[]{:S(2)}, u32[]{:S(2)}) collective-permute-start(bf16[100,512]{1,0:T(8,128)(2,1)S(1)} %pad_maximum_fusion.2), channel_id=1, source_target_pairs={{0,8},{4,12},{8,0},{12,4},{16,24},{20,28},{24,16},{28,20},{1,9},{5... | collective-permute-start | bytes 307208 | tf_op jit(solution)/shard_map/ppermute | solution.py:308
  21.8 5.8 %collective-permute-start.2 = (bf16[200,512]{1,0:T(8,128)(2,1)S(1)}, bf16[200,512]{1,0:T(8,128)(2,1)S(1)}, u32[]{:S(2)}, u32[]{:S(2)}) collective-permute-start(bf16[200,512]{1,0:T(8,128)(2,1)S(1)} %pad_maximum_fusion), channel_id=1, source_target_pairs={{0,4},{4,0},{8,12},{12,8},{16,20},{20,16},{24,28},{28,24},{1,5},{5... | collective-permute-start | bytes 614408 | tf_op jit(solution)/shard_map/ppermute | solution.py:308
  37.2 1.5 %copy-start.8 = (bf16[16,352,256]{2,1,0:T(8,128)(2,1)}, bf16[16,352,256]{2,1,0:T(8,128)(2,1)S(1)}, u32[]{:S(2)}) copy-start(bf16[16,352,256]{2,1,0:T(8,128)(2,1)S(1)} %get-tuple-element.11.ds_ref) | copy-start | bytes 8650756
  38.9 5.8 %collective-permute-start.3 = (bf16[200,512]{1,0:T(8,128)(2,1)S(1)}, bf16[200,512]{1,0:T(8,128)(2,1)S(1)}, u32[]{:S(2)}, u32[]{:S(2)}) collective-permute-start(bf16[200,512]{1,0:T(8,128)(2,1)S(1)} %pad_maximum_fusion.1), channel_id=1, source_target_pairs={{0,4},{4,0},{8,12},{12,8},{16,20},{20,16},{24,28},{28,24},{1,5},{5... | collective-permute-start | bytes 614408 | tf_op jit(solution)/shard_map/ppermute | solution.py:308
  45.5 4.9 %collective-permute-start.4 = (bf16[100,512]{1,0:T(8,128)(2,1)}, bf16[100,512]{1,0:T(8,128)(2,1)S(1)}, u32[]{:S(2)}, u32[]{:S(2)}) collective-permute-start(bf16[100,512]{1,0:T(8,128)(2,1)} %pad_maximum_fusion.3), channel_id=1, source_target_pairs={{0,8},{4,12},{8,0},{12,4},{16,24},{20,28},{24,16},{28,20},{1,9},{5... | collective-permute-start | bytes 307208 | tf_op jit(solution)/shard_map/ppermute | solution.py:308
  50.5 5.1 %collective-permute-start.5 = (bf16[50,512]{1,0:T(8,128)(2,1)S(1)}, bf16[50,512]{1,0:T(8,128)(2,1)S(1)}, u32[]{:S(2)}, u32[]{:S(2)}) collective-permute-start(bf16[50,512]{1,0:T(8,128)(2,1)S(1)} %fusion), channel_id=1, source_target_pairs={{0,16},{4,20},{8,24},{12,28},{16,0},{20,4},{24,8},{28,12},{1,17},{... | collective-permute-start | bytes 153608 | tf_op jit(solution)/shard_map/ppermute | solution.py:308
  55.6 2.2 %copy-start.1 = (bf16[8192,256]{1,0:T(8,128)(2,1)S(1)}, bf16[8192,256]{1,0:T(8,128)(2,1)}, u32[]{:S(2)}) copy-start(bf16[8192,256]{1,0:T(8,128)(2,1)} %wk_ref.5) | copy-start | bytes 12582916
  62.0 7.3 %collective-permute-start.7 = (bf16[50,2048]{1,0:T(8,128)(2,1)S(1)}, bf16[50,2048]{1,0:T(8,128)(2,1)}, u32[]{:S(2)}, u32[]{:S(2)}) collective-permute-start(bf16[50,2048]{1,0:T(8,128)(2,1)S(1)} %slice.136), channel_id=1, source_target_pairs={{0,1},{1,0},{2,3},{3,2},{4,5},{5,4},{6,7},{7,6},{8,9},{9,8},{10,11... | collective-permute-start | bytes 614408 | tf_op jit(solution)/shard_map/ppermute | solution.py:308
  62.1 2.2 %copy-start.2 = (bf16[8192,256]{1,0:T(8,128)(2,1)S(1)}, bf16[8192,256]{1,0:T(8,128)(2,1)}, u32[]{:S(2)}) copy-start(bf16[8192,256]{1,0:T(8,128)(2,1)} %wk_ref.5) | copy-start | bytes 12582916
  64.3 7.8 %copy-start.9 = (bf16[16,352,256]{2,1,0:T(8,128)(2,1)S(1)}, bf16[16,352,256]{2,1,0:T(8,128)(2,1)}, u32[]{:S(2)}) copy-start(bf16[16,352,256]{2,1,0:T(8,128)(2,1)} %copy-done.8) | copy-start | bytes 8650756
  68.7 9.7 %collective-permute-start.6 = (bf16[50,2048]{1,0:T(8,128)(2,1)S(1)}, bf16[50,2048]{1,0:T(8,128)(2,1)S(1)}, u32[]{:S(2)}, u32[]{:S(2)}) collective-permute-start(bf16[50,2048]{1,0:T(8,128)(2,1)S(1)} %slice.134), channel_id=1, source_target_pairs={{0,1},{1,0},{2,3},{3,2},{4,5},{5,4},{6,7},{7,6},{8,9},{9,8},{10,11... | collective-permute-start | bytes 614408 | tf_op jit(solution)/shard_map/ppermute | solution.py:308
  70.3 8.1 %collective-permute-start.8 = (bf16[50,2048]{1,0:T(8,128)(2,1)S(1)}, bf16[50,2048]{1,0:T(8,128)(2,1)S(1)}, u32[]{:S(2)}, u32[]{:S(2)}) collective-permute-start(bf16[50,2048]{1,0:T(8,128)(2,1)S(1)} %add_convert_fusion.1), channel_id=1, source_target_pairs={{0,2},{1,3},{2,0},{3,1},{4,6},{5,7},{6,4},{7,5},{8,10},{9,11},{10,... | collective-permute-start | bytes 614408 | tf_op jit(solution)/shard_map/ppermute | solution.py:308
  72.1 6.3 %copy-start.10 = (bf16[50,2048]{1,0:T(8,128)(2,1)S(1)}, bf16[50,2048]{1,0:T(8,128)(2,1)}, u32[]{:S(2)}) copy-start(bf16[50,2048]{1,0:T(8,128)(2,1)} %param.15) | copy-start | bytes 614404

commit v2 on v0

v2 whole, which is shorter than its diff:
```python
import functools
import math

import jax
import jax.numpy as jnp
from jax import lax
from jax.experimental import pallas as pl
from jax.experimental.pallas import tpu as pltpu
from jax.sharding import PartitionSpec as P

HEADS = 64
KVH = 8
HD = 128
GROUP = HEADS // KVH
SCALE = HD ** (-0.5)
SCALE2 = SCALE * math.log2(math.e)
F32 = jnp.float32
BF16 = jnp.bfloat16
MIB = 1024 * 1024
LAST = (((1,), (1,)), ((), ()))
VMEM = pl.BlockSpec(memory_space=pltpu.VMEM)
ANY = pl.BlockSpec(memory_space=pl.ANY)
HBM = pl.BlockSpec(memory_space=pltpu.HBM)


def dot(a, b, dims=(((1,), (0,)), ((), ()))):
    return lax.dot_general(a, b, dims, preferred_element_type=F32)


def params(mib):
    return pltpu.CompilerParams(vmem_limit_bytes=mib * MIB)


def cost(flops, nbytes):
    return pl.CostEstimate(flops=int(flops), bytes_accessed=int(nbytes), transcendentals=0)


def shape(dims, dtype=BF16):
    return jax.ShapeDtypeStruct(dims, dtype)


def lanes(index):
    return slice(index * HD, (index + 1) * HD)


def round_up(value, unit):
    return -(-value // unit) * unit


def project_kernel(
    pieces, states_hbm, wk_hbm, wv_hbm, out_ref, wk_ref, wv_ref, states_ref, sems
):
    width = wk_ref.shape[1]
    chunk = wk_ref.shape[0] // pieces
    states_copy = pltpu.make_async_copy(states_hbm, states_ref, sems.at[2 * pieces])
    states_copy.start()
    copies = []
    for at in range(pieces):
        rows = pl.ds(at * chunk, chunk)
        pair = (
            pltpu.make_async_copy(wk_hbm.at[rows], wk_ref.at[rows], sems.at[2 * at]),
            pltpu.make_async_copy(wv_hbm.at[rows], wv_ref.at[rows], sems.at[2 * at + 1]),
        )
        for copy in pair:
            copy.start()
        copies.append(pair)
    states_copy.wait()
    keys = values = None
    for at, (key_copy, value_copy) in enumerate(copies):
        rows = slice(at * chunk, (at + 1) * chunk)
        states = states_ref[:, rows]
        key_copy.wait()
        term = dot(states, wk_ref[rows, :])
        keys = term if keys is None else keys + term
        value_copy.wait()
        term = dot(states, wv_ref[rows, :])
        values = term if values is None else values + term
    out_ref[:, :width] = keys.astype(BF16)
    out_ref[:, width:] = values.astype(BF16)


def project(states, w_key, w_value, pieces=8):
    rows, depth = states.shape
    width = w_key.shape[1]
    return pl.pallas_call(
        functools.partial(project_kernel, pieces),
        name="project",
        in_specs=[HBM] * 3,
        out_specs=VMEM,
        out_shape=shape((rows, 2 * width)),
        scratch_shapes=[
            pltpu.VMEM(w_key.shape, BF16),
            pltpu.VMEM(w_value.shape, BF16),
            pltpu.VMEM((rows, depth), BF16),
            pltpu.SemaphoreType.DMA((2 * pieces + 1,)),
        ],
        compiler_params=params(12),
        cost_estimate=cost(4 * rows * depth * width, 8 * depth * width),
    )(*(pltpu.with_memory_space_constraint(x, pltpu.HBM) for x in (states, w_key, w_value)))


def causal_bias(count):
    key_pos = lax.broadcasted_iota(jnp.int32, (count, count), 0)
    row_pos = lax.broadcasted_iota(jnp.int32, (count, count), 1)
    return jnp.where(key_pos <= row_pos, 0.0, -jnp.inf).astype(F32)


def own_stats_kernel(q_ref, g_ref, k_ref, v_ref, stats_ref, bias_ref):
    bias_ref[...] = causal_bias(bias_ref.shape[0])
    for kv in range(k_ref.shape[1] // HD):
        keys = k_ref[:, lanes(kv)]
        values = v_ref[:, lanes(kv)]
        for head in range(kv * GROUP, (kv + 1) * GROUP):
            scores = dot(keys, q_ref[:, lanes(head)], LAST) * SCALE2 + bias_ref[...]
            top = jnp.max(scores, axis=0, keepdims=True)
            weights = jnp.exp2(scores - top)
            dprobs = dot(values, g_ref[:, lanes(head)], LAST)
            stats_ref[head, 0:1, :] = top
            stats_ref[head, 1:2, :] = jnp.sum(weights, axis=0, keepdims=True)
            stats_ref[head, 2:3, :] = jnp.sum(weights * dprobs, axis=0, keepdims=True)


def own_stats(queries, out_grad, keys_own, values_own, held):
    rows = queries.shape[0]
    heads = queries.shape[1] // HD
    return pl.pallas_call(
        own_stats_kernel,
        name="own_stats",
        in_specs=[VMEM] * 4,
        out_specs=VMEM,
        out_shape=shape((heads, 8, rows), F32),
        scratch_shapes=[pltpu.VMEM((rows, rows), F32)],
        compiler_params=params(12),
        cost_estimate=cost(20 * heads * rows * rows * HD, 4 * rows * heads * HD),
    )(queries, out_grad, keys_own, values_own, *held)


def summary_kernel(
    count, slots, seg_ref, q_ref, g_ref, odd_ref, even_ref, own_ref,
    ds_ref, stats_ref, keys_ref, odd_grad_ref, even_grad_ref, bias_ref, both_ref,
):
    position = seg_ref[0]
    rows = q_ref.shape[0]
    padded = both_ref.shape[0]
    split = odd_ref.shape[0]
    shown = split + even_ref.shape[0]
    kv_local = keys_ref.shape[1] // HD
    width = kv_local * HD

    row = lax.broadcasted_iota(jnp.int32, (padded, rows), 0)
    bias = jnp.full((padded, rows), -jnp.inf, F32)
    for at, slot in enumerate(slots):
        level = jnp.where((position ^ slot) < position, 0.0, -jnp.inf).astype(F32)
        bias = jnp.where((row >= at * count) & (row < (at + 1) * count), level, bias)
    bias_ref[...] = bias
    if padded > shown:
        tail = round_up(shown, 8) - 8
        both_ref[tail:, :] = jnp.zeros((padded - tail, 2 * width), F32)
    both_ref[:split, :] = odd_ref[...].astype(F32)
    both_ref[split:shown, :] = even_ref[...].astype(F32)
    keys_ref[...] = both_ref[:, :width].astype(BF16)

    for kv in range(kv_local):
        keys = keys_ref[:, lanes(kv)]
        values = both_ref[:, width + kv * HD : width + (kv + 1) * HD].astype(BF16)
        heads = range(kv * GROUP, (kv + 1) * GROUP)
        all_dscores, all_probs = [], []
        for head in heads:
            scores = dot(keys, q_ref[:, lanes(head)], LAST) * SCALE2 + bias_ref[...]
            own_top = own_ref[head, 0:1, :]
            top = jnp.maximum(jnp.max(scores, axis=0, keepdims=True), own_top)
            weights = jnp.exp2(scores - top)
            shrink = jnp.exp2(own_top - top)
            total = jnp.sum(weights, axis=0, keepdims=True) + own_ref[head, 1:2, :] * shrink
            inverse = 1.0 / total
            probs = weights * inverse
            dprobs = dot(values, g_ref[:, lanes(head)], LAST)
            delta = jnp.sum(probs * dprobs, axis=0, keepdims=True)
            delta = delta + own_ref[head, 2:3, :] * shrink * inverse
            dscores = (probs * (dprobs - delta)).astype(BF16)
            ds_ref[head] = dscores
            all_dscores.append(dscores)
            all_probs.append(probs.astype(BF16))
            stats_ref[head, 0:1, :] = top
            stats_ref[head, 1:2, :] = inverse
            stats_ref[head, 2:3, :] = delta
        queries = jnp.concatenate([q_ref[:, lanes(head)] for head in heads], 0)
        grads = jnp.concatenate([g_ref[:, lanes(head)] for head in heads], 0)
        key_part = dot(jnp.concatenate(all_dscores, 1), queries) * SCALE
        value_part = dot(jnp.concatenate(all_probs, 1), grads)
        both_ref[:, lanes(kv)] = key_part
        both_ref[:, width + kv * HD : width + (kv + 1) * HD] = value_part
    odd_grad_ref[...] = both_ref[:split, :].astype(BF16)
    even_grad_ref[...] = both_ref[split:shown, :]


def summary_part(position, queries, out_grad, odd, even, own, held, count, slots):
    rows = queries.shape[0]
    width = odd.shape[1] // 2
    heads = queries.shape[1] // HD
    padded = round_up(odd.shape[0] + even.shape[0], 16)
    return pl.pallas_call(
        functools.partial(summary_kernel, count, slots),
        name="summary_part",
        in_specs=[pl.BlockSpec(memory_space=pltpu.SMEM)] + [VMEM] * 5,
        out_specs=[VMEM] * 5,
        out_shape=[
            shape((heads, padded, rows)),
            shape((heads, 8, rows), F32),
            shape((padded, width)),
            shape(odd.shape),
            shape(even.shape, F32),
        ],
        scratch_shapes=[
            pltpu.VMEM((padded, rows), F32),
            pltpu.VMEM((padded, 2 * width), F32),
        ],
        compiler_params=params(16 if padded <= 512 else 48),
        cost_estimate=cost(40 * heads * rows * padded * HD, 4 * rows * heads * HD),
    )(position, queries, out_grad, odd, even, own, *held)


def own_grads_kernel(
    kv, q_ref, g_ref, k_ref, v_ref, sk_ref, ds_ref, stats_ref, *rest
):
    dq_out, dk_ref, dv_ref, bias_ref, dq_ref, sem = rest[-6:]
    bias_ref[...] = causal_bias(bias_ref.shape[0])
    keys = k_ref[:, lanes(kv)]
    values = v_ref[:, lanes(kv)]
    keys_t = jnp.concatenate([sk_ref[:, lanes(kv)], keys], 0).T
    heads = range(kv * GROUP, (kv + 1) * GROUP)
    all_dscores, all_probs = [], []
    for at, head in enumerate(heads):
        scores = dot(keys, q_ref[:, lanes(head)], LAST) * SCALE2 + bias_ref[...]
        probs = jnp.exp2(scores - stats_ref[head, 0:1, :]) * stats_ref[head, 1:2, :]
        dprobs = dot(values, g_ref[:, lanes(head)], LAST)
        dscores = (probs * (dprobs - stats_ref[head, 2:3, :])).astype(BF16)
        all_dscores.append(dscores)
        all_probs.append(probs.astype(BF16))
        dquery = dot(keys_t, jnp.concatenate([ds_ref[head], dscores], 0))
        dq_ref[:, lanes(at)] = (dquery * SCALE).T.astype(BF16)
    columns = pl.ds(kv * GROUP * HD, GROUP * HD)
    copy = pltpu.make_async_copy(dq_ref, dq_out.at[:, columns], sem)
    copy.start()
    queries = jnp.concatenate([q_ref[:, lanes(head)] for head in heads], 0)
    grads = jnp.concatenate([g_ref[:, lanes(head)] for head in heads], 0)
    dk_ref[...] = (dot(jnp.concatenate(all_dscores, 1), queries) * SCALE).astype(BF16)
    dv_ref[...] = dot(jnp.concatenate(all_probs, 1), grads).astype(BF16)
    copy.wait()


def own_grads(kv, queries, out_grad, keys_own, values_own, sum_keys, dscores, stats, held, earlier):
    rows = queries.shape[0]
    heads = queries.shape[1] // HD
    padded = sum_keys.shape[0]
    operands = [queries, out_grad, keys_own, values_own, sum_keys, dscores, stats, *held]
    in_specs = [VMEM] * 7
    aliases = {}
    if earlier is not None:
        operands.append(earlier)
        in_specs.append(HBM)
        aliases = {7: 0}
    return pl.pallas_call(
        functools.partial(own_grads_kernel, kv),
        name="own_grads",
        in_specs=in_specs,
        out_specs=[HBM, VMEM, VMEM],
        out_shape=[shape((rows, heads * HD)), shape((rows, HD)), shape((rows, HD))],
        input_output_aliases=aliases,
        scratch_shapes=[
            pltpu.VMEM((rows, rows), F32),
            pltpu.VMEM((rows, GROUP * HD), BF16),
            pltpu.SemaphoreType.DMA,
        ],
        compiler_params=params(16 if padded <= 512 else 32),
        cost_estimate=cost(20 * heads * rows * rows * HD, 4 * rows * heads * HD),
    )(*operands)


def state_kernel(chunk, group, mine_ref, emitted_ref, wk_ref, wv_ref, *out_refs):
    width = wk_ref.shape[1]
    keys = emitted_ref[:, :width]
    values = emitted_ref[:, width:]
    wide = out_refs[0].shape[1]
    for at, out_ref in enumerate(out_refs):
        for step in range(wide // chunk):
            rows = pl.ds(pl.multiple_of((mine_ref[0] ^ group[at]) * wide + step * chunk, chunk), chunk)
            total = dot(keys, wk_ref[rows, :], LAST) + dot(values, wv_ref[rows, :], LAST)
            out_ref[:, step * chunk : (step + 1) * chunk] = total.astype(BF16)


def state_part(mine, emitted, w_key, w_value, wide, group, chunk=512):
    rows = emitted.shape[0]
    width = w_key.shape[1]
    count = len(group)
    return pl.pallas_call(
        functools.partial(state_kernel, chunk, group),
        name="state_part",
        in_specs=[pl.BlockSpec(memory_space=pltpu.SMEM)] + [VMEM] * 3,
        out_specs=[VMEM] * count,
        out_shape=[shape((rows, wide))] * count,
        compiler_params=params(14),
        cost_estimate=cost(4 * rows * count * wide * width, 4 * count * wide * width),
    )(mine, emitted, w_key, w_value)


def exchange(block, axis, size, key):
    return lax.ppermute(block, axis, [(i, i ^ key) for i in range(size)])


def per_device(
    queries, keys_own, values_own, out_grad, summary_states, w_key, w_value, summary_grad
):
    kv_local = keys_own.shape[1] // HD
    count = summary_states.shape[0]
    n_seg = lax.axis_size("seg")
    n_tp = lax.axis_size("tp")
    position = lax.axis_index("seg").astype(jnp.int32).reshape(1)
    mine = lax.axis_index("tp").astype(jnp.int32).reshape(1)

    projected = project(summary_states, w_key, w_value)
    held = ()
    own = own_stats(queries, out_grad, keys_own, values_own, held)

    evens = list(range(n_seg - 2, 0, -2))
    odds = [j + 1 for j in evens] + [1]
    chunks = {j: exchange(projected, "seg", n_seg, j) for j in evens}
    even = jnp.concatenate([chunks[j] for j in evens], 0)
    odd = jnp.concatenate(
        [exchange(even, "seg", n_seg, 1), exchange(projected, "seg", n_seg, 1)], 0
    )

    dscores, stats, sum_keys, odd_grad, even_grad = summary_part(
        position, queries, out_grad, odd, even, own, held, count, odds + evens
    )

    query_grad = None
    key_blocks, value_blocks = [], []

    def own_part(kv, earlier):
        query_grad, key_block, value_block = own_grads(
            kv, queries, out_grad, keys_own, values_own, sum_keys, dscores, stats, held, earlier
        )
        key_blocks.append(key_block)
        value_blocks.append(value_block)
        return query_grad

    got = exchange(odd_grad, "seg", n_seg, 1)
    query_grad = own_part(0, None)
    got, query_grad = lax.optimization_barrier((got, query_grad))
    got = got.astype(F32)
    emitted = got[len(evens) * count :]
    blocks = []
    for at, j in enumerate(evens):
        rows = slice(at * count, (at + 1) * count)
        block = (even_grad[rows] + got[rows]).astype(BF16)
        blocks.append(exchange(block, "seg", n_seg, j))
    for kv in range(1, kv_local):
        query_grad = own_part(kv, query_grad)
    blocks, query_grad = lax.optimization_barrier((blocks, query_grad))
    for block in blocks:
        emitted = emitted + block.astype(F32)
    emitted = emitted.astype(BF16)
    key_grad = jnp.concatenate(key_blocks, 1)
    value_grad = jnp.concatenate(value_blocks, 1)

    wide = w_key.shape[0] // n_tp
    terms = {}
    for group in (list(range(n_tp - 1, 1, -1)), [1, 0]):
        terms.update(zip(group, state_part(mine, emitted, w_key, w_value, wide, group)))
    bit = 1
    while bit < n_tp:
        for j in sorted((j for j in terms if j & bit), reverse=True):
            got = exchange(terms.pop(j).astype(BF16), "tp", n_tp, bit)
            terms[j ^ bit] = terms[j ^ bit].astype(F32) + got.astype(F32)
        bit *= 2
    state_grad = (terms[0] + summary_grad.astype(F32)).astype(BF16)
    return (query_grad, key_grad, value_grad, state_grad)


def solution(mesh):
    placed = (
        P("seg", "tp"),
        P("seg", "tp"),
        P("seg", "tp"),
        P("seg", "tp"),
        P("seg", None),
        P(None, "tp"),
        P(None, "tp"),
        P("seg", "tp"),
    )
    return jax.shard_map(
        per_device,
        mesh=mesh,
        in_specs=placed,
        out_specs=(P("seg", "tp"), P("seg", "tp"), P("seg", "tp"), P("seg", "tp")),
        check_vma=False,
    )
```

time: 289 us -> 53.8 us (0.19); the launches traced: 285 us -> 53.6 us
  matrix products: 122 us -> 0 us
  waiting for transfers between devices: 92.7 us -> 12.6 us
  blocking collectives: 32.9 us -> 0 us
  Pallas kernels: 0 us -> 21.2 us
  starting transfers between devices: 0.08 us -> 17.2 us
  between operations: 14.9 us -> 0.82 us
  other arithmetic: 12.1 us -> 1.8 us
  local copies, waits for them, and re-layouts: 10 us -> 0.03 us
    dot_general x100 -> x0, matrix products: 122 us -> none  [the longest x16 32.4 us: head_step(): lax.dot_general(probs_b, grad_head, contract_first, preferred_element_typ...]
    unnamed x3 -> x0, waiting for transfers between devices: 71.6 us -> none
    all_gather x1 -> x0, blocking collectives: 32.9 us -> none  [per_device(): everyone = lax.all_gather(projected, 'seg', axis=0, tiled=True)]
    pallas_call x0 -> x7, Pallas kernels: none -> 21.2 us  [the longest x2 6.64 us: own_grads(): pl.pallas_call(functools.partial(own_grads_kernel, kv), name='own_grads',...]
    reduce_scatter x1 -> x0, waiting for transfers between devices: 21.1 us -> none  [per_device(): lax.psum_scatter(partial_state.astype(jnp.bfloat16), 'tp', scatter_dimens...]
    ppermute x0 -> x12, starting transfers between devices: none -> 17.2 us  [exchange(): return lax.ppermute(block, axis, [(i, i ^ key) for i in range(size)])]
    ppermute x0 -> x12, waiting for transfers between devices: none -> 12.6 us  [exchange(): return lax.ppermute(block, axis, [(i, i ^ key) for i in range(size)])]
    unnamed x16 -> x14, local copies, waits for them, and re-layouts: 5.86 us -> 0.03 us
  transfers between devices with their start and end apart: 2 -> 12, of which waited for: 2 -> 5; matrix products, arithmetic and copies ran while one was open for 1% -> 2% of each run, Pallas kernels for 0% -> 18%
where the time goes in v2:
time: 53.8 us; the launch traced here: 53.6 us
  Pallas kernels  21.2 us (39%)
  starting transfers between devices  17.2 us (32%)
  waiting for transfers between devices  12.6 us (23%)
  other arithmetic  1.8 us (3%)
  between operations  0.82 us (2%)
    ppermute x12, starting transfers between devices, exchange(): return lax.ppermute(block, axis, [(i, i ^ key) for i in range(size)])  17.2 us
    ppermute x12, waiting for transfers between devices, exchange(): return lax.ppermute(block, axis, [(i, i ^ key) for i in range(size)])  12.6 us
    pallas_call x2, Pallas kernels, own_grads(): pl.pallas_call(functools.partial(own_grads_kernel, kv), name='own_grads',...  6.64 us
    pallas_call x1, Pallas kernels, summary_part(): pl.pallas_call(functools.partial(summary_kernel, count, slots), name='sum...  5.36 us
    pallas_call x1, Pallas kernels, project(): pl.pallas_call(functools.partial(project_kernel, pieces), name='project',...  4.77 us
    pallas_call x2, Pallas kernels, state_part(): pl.pallas_call(functools.partial(state_kernel, chunk, group), name='state...  2.76 us
    pallas_call x1, Pallas kernels, own_stats(): pl.pallas_call(own_stats_kernel, name='own_stats', in_specs=[VMEM] * 4, o...  1.67 us
  transfers between devices with their start and end apart: 12, of which 5 were waited for; matrix products, arithmetic and copies ran while one was open for 2% of the time, Pallas kernels for 18%

profile of v2, /device:TPU:0, one launch (start us, length us, event | category | flops | bytes accessed | tf_op | source)
XLA Modules:
  0.0 53.6 jit_solution(2484977530822409392)
XLA Ops:
  0.6 0.0 copy-start.3
  0.6 0.0 copy-start.2
  0.7 0.0 copy-start.5
  0.7 0.0 copy-start.4
  0.7 4.8 %project.1 = bf16[50,512]{1,0:T(8,128)(2,1)S(1)} custom-call(bf16[50,8192]{1,0:T(8,128)(2,1)} %states_hbm.1, bf16[8192,256]{1,0:T(8,128)(2,1)} %wk_ref.3, bf16[8192,256]{1,0:T(8,128)(2,1)} %wv_ref.3), custom_call_target="tpu_custom_call" | custom-call | flops 419430400 | bytes 16777216 | tf_op jit(solution)/shard_map/project/pallas_call | solution.py:85
  5.4 3.1 %collective-permute-start.2 = (bf16[50,512]{1,0:T(8,128)(2,1)S(1)}, bf16[50,512]{1,0:T(8,128)(2,1)S(1)}, u32[]{:S(2)}, u32[]{:S(2)}) collective-permute-start(bf16[50,512]{1,0:T(8,128)(2,1)S(1)} %project.1), channel_id=1, source_target_pairs={{0,8},{4,12},{8,0},{12,4},{16,24},{20,28},{24,16},{28,20},{1,9},{5... | collective-permute-start | bytes 153608 | tf_op jit(solution)/shard_map/ppermute | solution.py:308
  8.5 2.6 %collective-permute-start.1 = (bf16[50,512]{1,0:T(8,128)(2,1)S(1)}, bf16[50,512]{1,0:T(8,128)(2,1)S(1)}, u32[]{:S(2)}, u32[]{:S(2)}) collective-permute-start(bf16[50,512]{1,0:T(8,128)(2,1)S(1)} %project.1), channel_id=1, source_target_pairs={{0,16},{4,20},{8,24},{12,28},{16,0},{20,4},{24,8},{28,12},{1,17},{... | collective-permute-start | bytes 153608 | tf_op jit(solution)/shard_map/ppermute | solution.py:308
  11.1 0.0 collective-permute-start
  11.1 1.7 %collective-permute-start.4 = (bf16[50,512]{1,0:T(8,128)(2,1)S(1)}, bf16[50,512]{1,0:T(8,128)(2,1)S(1)}, u32[]{:S(2)}, u32[]{:S(2)}) collective-permute-start(bf16[50,512]{1,0:T(8,128)(2,1)S(1)} %project.1), channel_id=1, source_target_pairs={{0,4},{4,0},{8,12},{12,8},{16,20},{20,16},{24,28},{28,24},{1,5},{5... | collective-permute-start | bytes 153608 | tf_op jit(solution)/shard_map/ppermute | solution.py:308
  12.8 0.0 collective-permute-done.2
  12.8 1.9 %collective-permute-done.1 = bf16[50,512]{1,0:T(8,128)(2,1)S(1)} collective-permute-done((bf16[50,512]{1,0:T(8,128)(2,1)S(1)}, bf16[50,512]{1,0:T(8,128)(2,1)S(1)}, u32[]{:S(2)}, u32[]{:S(2)}) %collective-permute-start.1) | collective-permute-done | bytes 51232 | tf_op jit(solution)/shard_map/ppermute | solution.py:308
  14.7 2.4 %collective-permute-done = bf16[50,512]{1,0:T(8,128)(2,1)S(1)} collective-permute-done((bf16[50,512]{1,0:T(8,128)(2,1)S(1)}, bf16[50,512]{1,0:T(8,128)(2,1)S(1)}, u32[]{:S(2)}, u32[]{:S(2)}) %collective-permute-start) | collective-permute-done | bytes 51232 | tf_op jit(solution)/shard_map/ppermute | solution.py:308
  17.1 1.6 %collective-permute-start.3 = (bf16[150,512]{1,0:T(8,128)(2,1)S(1)}, bf16[150,512]{1,0:T(8,128)(2,1)S(1)}, u32[]{:S(2)}, u32[]{:S(2)}) collective-permute-start(bf16[150,512]{1,0:T(8,128)(2,1)S(1)} %pad_maximum_fusion.1.even_ref), channel_id=1, source_target_pairs={{0,4},{4,0},{8,12},{12,8},{16,20},{20,16},{24,28},{28,24},{1,5},{5... | collective-permute-start | bytes 460808 | tf_op jit(solution)/shard_map/ppermute | solution.py:308
  18.7 0.0 copy-done.3
  18.7 0.0 copy-done.2
  18.7 0.0 copy-done.5
  18.7 0.0 copy-done.4
  18.7 1.7 %own_stats.1.own_ref = f32[16,8,256]{2,1,0:T(8,128)S(1)} custom-call(bf16[256,2048]{1,0:T(8,128)(2,1)S(1)} %copy-done.2, bf16[256,2048]{1,0:T(8,128)(2,1)S(1)} %copy-done.3, bf16[256,256]{1,0:T(8,128)(2,1)S(1)} %copy-done.4, bf16[256,256]{1,0:T(8,128)(2,1)S(1)} %copy-done.5), custom_call_target="tpu_custom_call" | custom-call | flops 2684354560 | bytes 2097152 | tf_op jit(solution)/shard_map/own_stats/pallas_call | solution.py:126
  20.4 0.0 collective-permute-done.4
  20.4 2.0 %collective-permute-done.3 = bf16[150,512]{1,0:T(8,128)(2,1)S(1)} collective-permute-done((bf16[150,512]{1,0:T(8,128)(2,1)S(1)}, bf16[150,512]{1,0:T(8,128)(2,1)S(1)}, u32[]{:S(2)}, u32[]{:S(2)}) %collective-permute-start.3) | collective-permute-done | bytes 153632 | tf_op jit(solution)/shard_map/ppermute | solution.py:308
  22.5 5.4 %summary_part.1 = (bf16[16,352,256]{2,1,0:T(8,128)(2,1)S(1)}, f32[16,8,256]{2,1,0:T(8,128)S(1)}, bf16[352,256]{1,0:T(8,128)(2,1)S(1)}, bf16[200,512]{1,0:T(8,128)(2,1)S(1)}, f32[150,512]{1,0:T(8,128)S(1)}) custom-call(s32[1]{0:T(128)} %bitcast.seg_ref, bf16[256,2048]{1,0:T(8,128)(2,1)S(1)} %copy-done.2, bf16[256,2048]{1,0:T(8,128)(2,1)S(1)} %copy-done.3, ...), custom_call_target="tpu_custom_call" | custom-call | flops 7381975040 | bytes 2097152 | tf_op jit(solution)/shard_map/summary_part/pallas_call | solution.py:202
  27.8 1.6 %collective-permute-start.5 = (bf16[200,512]{1,0:T(8,128)(2,1)S(1)}, bf16[200,512]{1,0:T(8,128)(2,1)S(1)}, u32[]{:S(2)}, u32[]{:S(2)}) collective-permute-start(bf16[200,512]{1,0:T(8,128)(2,1)S(1)} %get-tuple-element.26), channel_id=1, source_target_pairs={{0,4},{4,0},{8,12},{12,8},{16,20},{20,16},{24,28},{28,24},{1,5},{5... | collective-permute-start | bytes 614408 | tf_op jit(solution)/shard_map/ppermute | solution.py:308
  29.4 3.2 %own_grads.2 = (bf16[256,2048]{1,0:T(8,128)(2,1)}, bf16[256,128]{1,0:T(8,128)(2,1)S(1)}, bf16[256,128]{1,0:T(8,128)(2,1)S(1)}) custom-call(bf16[256,2048]{1,0:T(8,128)(2,1)S(1)} %copy-done.2, bf16[256,2048]{1,0:T(8,128)(2,1)S(1)} %copy-done.3, bf16[256,256]{1,0:T(8,128)(2,1)S(1)} %copy-done.4, bf16[256,256]{1,0:T(8,128)(2,1)S(1)} %copy-done.5, ...), custom_call_target="tpu_custom_call" | custom-call | flops 2684354560 | bytes 2097152 | tf_op jit(solution)/shard_map/own_grads/pallas_call | solution.py:263
  32.6 1.0 %collective-permute-done.5 = bf16[200,512]{1,0:T(8,128)(2,1)S(1)} collective-permute-done((bf16[200,512]{1,0:T(8,128)(2,1)S(1)}, bf16[200,512]{1,0:T(8,128)(2,1)S(1)}, u32[]{:S(2)}, u32[]{:S(2)}) %collective-permute-start.5) | collective-permute-done | bytes 204832 | tf_op jit(solution)/shard_map/ppermute | solution.py:308
  33.7 0.1 fusion.3
  33.8 0.1 collective-permute-start.8
  33.9 1.8 %collective-permute-start.7 = (bf16[50,512]{1,0:T(8,128)(2,1)S(1)}, bf16[50,512]{1,0:T(8,128)(2,1)S(1)}, u32[]{:S(2)}, u32[]{:S(2)}) collective-permute-start(bf16[50,512]{1,0:T(8,128)(2,1)S(1)} %get-tuple-element.47), channel_id=1, source_target_pairs={{0,16},{4,20},{8,24},{12,28},{16,0},{20,4},{24,8},{28,12},{1,17},{... | collective-permute-start | bytes 153608 | tf_op jit(solution)/shard_map/ppermute | solution.py:308
  35.7 0.0 copy-start
  35.7 0.0 copy-start.1
  35.7 2.6 %collective-permute-start.6 = (bf16[50,512]{1,0:T(8,128)(2,1)S(1)}, bf16[50,512]{1,0:T(8,128)(2,1)S(1)}, u32[]{:S(2)}, u32[]{:S(2)}) collective-permute-start(bf16[50,512]{1,0:T(8,128)(2,1)S(1)} %get-tuple-element.48), channel_id=1, source_target_pairs={{0,24},{4,28},{8,16},{12,20},{16,8},{20,12},{24,0},{28,4},{1,25},{... | collective-permute-start | bytes 153608 | tf_op jit(solution)/shard_map/ppermute | solution.py:308
  38.2 3.4 %own_grads.3 = (bf16[256,2048]{1,0:T(8,128)(2,1)}, bf16[256,128]{1,0:T(8,128)(2,1)S(1)}, bf16[256,128]{1,0:T(8,128)(2,1)S(1)}) custom-call(bf16[256,2048]{1,0:T(8,128)(2,1)S(1)} %copy-done.2, bf16[256,2048]{1,0:T(8,128)(2,1)S(1)} %copy-done.3, bf16[256,256]{1,0:T(8,128)(2,1)S(1)} %copy-done.4, ...), custom_call_target="tpu_custom_call", output_to_operand_aliasing={{0}: (7, {})} | custom-call | flops 2684354560 | bytes 2097152 | tf_op jit(solution)/shard_map/own_grads/pallas_call | solution.py:263
  41.7 0.0 collective-permute-done.8
  41.7 0.0 collective-permute-done.7
  41.7 0.0 collective-permute-done.6
  41.7 0.0 copy-done
  41.7 0.0 copy-done.1
  41.8 1.4 %state_part.3 = (bf16[50,2048]{1,0:T(8,128)(2,1)S(1)}, bf16[50,2048]{1,0:T(8,128)(2,1)S(1)}) custom-call(s32[1]{0:T(128)} %bitcast.1.mine_ref, bf16[50,512]{1,0:T(8,128)(2,1)S(1)} %fusion.2.emitted_ref, bf16[8192,256]{1,0:T(8,128)(2,1)S(1)} %copy-done, bf16[8192,256]{1,0:T(8,128)(2,1)S(1)} %copy-done.1), custom_call_target="tpu_custom_call" | custom-call | flops 209715200 | bytes 4194304 | tf_op jit(solution)/shard_map/state_part/pallas_call | solution.py:296
  43.1 0.0 copy-start.6
  43.1 0.1 collective-permute-start.10
  43.2 1.4 %state_part.2 = (bf16[50,2048]{1,0:T(8,128)(2,1)S(1)}, bf16[50,2048]{1,0:T(8,128)(2,1)S(1)}) custom-call(s32[1]{0:T(128)} %bitcast.1.mine_ref, bf16[50,512]{1,0:T(8,128)(2,1)S(1)} %fusion.2.emitted_ref, bf16[8192,256]{1,0:T(8,128)(2,1)S(1)} %copy-done, bf16[8192,256]{1,0:T(8,128)(2,1)S(1)} %copy-done.1), custom_call_target="tpu_custom_call" | custom-call | flops 209715200 | bytes 4194304 | tf_op jit(solution)/shard_map/state_part/pallas_call | solution.py:296
  44.6 0.6 %collective-permute-start.9 = (bf16[50,2048]{1,0:T(8,128)(2,1)S(1)}, bf16[50,2048]{1,0:T(8,128)(2,1)S(1)}, u32[]{:S(2)}, u32[]{:S(2)}) collective-permute-start(bf16[50,2048]{1,0:T(8,128)(2,1)S(1)} %get-tuple-element.43), channel_id=1, source_target_pairs={{0,1},{1,0},{2,3},{3,2},{4,5},{5,4},{6,7},{7,6},{8,9},{9,8},{10,11... | collective-permute-start | bytes 614408 | tf_op jit(solution)/shard_map/ppermute | solution.py:308
  45.2 0.0 collective-permute-done.10
  45.2 0.1 add_convert_fusion.1
  45.2 1.6 %collective-permute-start.11 = (bf16[50,2048]{1,0:T(8,128)(2,1)S(1)}, bf16[50,2048]{1,0:T(8,128)(2,1)S(1)}, u32[]{:S(2)}, u32[]{:S(2)}) collective-permute-start(bf16[50,2048]{1,0:T(8,128)(2,1)S(1)} %add_convert_fusion.1), channel_id=1, source_target_pairs={{0,2},{1,3},{2,0},{3,1},{4,6},{5,7},{6,4},{7,5},{8,10},{9,11},{10,... | collective-permute-start | bytes 614408 | tf_op jit(solution)/shard_map/ppermute | solution.py:308
  46.8 0.7 %pad_maximum_fusion.2 = (bf16[256,256]{1,0:T(8,128)(2,1)}, bf16[256,256]{1,0:T(8,128)(2,1)}) fusion(bf16[256,128]{1,0:T(8,128)(2,1)S(1)} %get-tuple-element.36, bf16[256,128]{1,0:T(8,128)(2,1)S(1)} %get-tuple-element.35, bf16[256,128]{1,0:T(8,128)(2,1)S(1)} %get-tuple-element.38, bf16[256,128]{1,0:T(8,128)(2,1)S(1)} %get-tuple-element.37), kind=kLoop, calls=%fused_computation.4 | loop fusion | flops 524288 | bytes 524288 | tf_op jit(solution)/shard_map/concatenate | solution.py:364
  47.5 0.0 collective-permute-done.9
  47.5 5.3 %collective-permute-done.11 = bf16[50,2048]{1,0:T(8,128)(2,1)S(1)} collective-permute-done((bf16[50,2048]{1,0:T(8,128)(2,1)S(1)}, bf16[50,2048]{1,0:T(8,128)(2,1)S(1)}, u32[]{:S(2)}, u32[]{:S(2)}) %collective-permute-start.11) | collective-permute-done | bytes 204832 | tf_op jit(solution)/shard_map/ppermute | solution.py:308
  52.8 0.0 copy-done.6
  52.8 0.8 %add_convert_fusion = bf16[50,2048]{1,0:T(8,128)(2,1)} fusion(bf16[50,2048]{1,0:T(8,128)(2,1)S(1)} %copy-done.6, bf16[50,2048]{1,0:T(8,128)(2,1)S(1)} %collective-permute-done.11, bf16[50,2048]{1,0:T(8,128)(2,1)S(1)} %collective-permute-done.9, bf16[50,2048]{1,0:T(8,128)(2,1)S(1)} %get-tuple-element.42), kind=kLoop, calls=%fused_computation | loop fusion | flops 819200 | bytes 1024000 | tf_op jit(solution)/shard_map/convert_element_type | solution.py:377
  (4 shorter events, 0.1 us)
Async XLA Ops:
  0.6 18.1 %copy-start.3 = (bf16[256,2048]{1,0:T(8,128)(2,1)S(1)}, bf16[256,2048]{1,0:T(8,128)(2,1)}, u32[]{:S(2)}) copy-start(bf16[256,2048]{1,0:T(8,128)(2,1)} %g_ref.7) | copy-start | bytes 3145732
  0.6 18.1 %copy-start.2 = (bf16[256,2048]{1,0:T(8,128)(2,1)S(1)}, bf16[256,2048]{1,0:T(8,128)(2,1)}, u32[]{:S(2)}) copy-start(bf16[256,2048]{1,0:T(8,128)(2,1)} %q_ref.7) | copy-start | bytes 3145732
  0.7 18.1 %copy-start.5 = (bf16[256,256]{1,0:T(8,128)(2,1)S(1)}, bf16[256,256]{1,0:T(8,128)(2,1)}, u32[]{:S(2)}) copy-start(bf16[256,256]{1,0:T(8,128)(2,1)} %v_ref.5) | copy-start | bytes 393220
  0.7 18.0 %copy-start.4 = (bf16[256,256]{1,0:T(8,128)(2,1)S(1)}, bf16[256,256]{1,0:T(8,128)(2,1)}, u32[]{:S(2)}) copy-start(bf16[256,256]{1,0:T(8,128)(2,1)} %k_ref.5) | copy-start | bytes 393220
  5.4 7.4 %collective-permute-start.2 = (bf16[50,512]{1,0:T(8,128)(2,1)S(1)}, bf16[50,512]{1,0:T(8,128)(2,1)S(1)}, u32[]{:S(2)}, u32[]{:S(2)}) collective-permute-start(bf16[50,512]{1,0:T(8,128)(2,1)S(1)} %project.1), channel_id=1, source_target_pairs={{0,8},{4,12},{8,0},{12,4},{16,24},{20,28},{24,16},{28,20},{1,9},{5... | collective-permute-start | bytes 153608 | tf_op jit(solution)/shard_map/ppermute | solution.py:308
  8.5 6.2 %collective-permute-start.1 = (bf16[50,512]{1,0:T(8,128)(2,1)S(1)}, bf16[50,512]{1,0:T(8,128)(2,1)S(1)}, u32[]{:S(2)}, u32[]{:S(2)}) collective-permute-start(bf16[50,512]{1,0:T(8,128)(2,1)S(1)} %project.1), channel_id=1, source_target_pairs={{0,16},{4,20},{8,24},{12,28},{16,0},{20,4},{24,8},{28,12},{1,17},{... | collective-permute-start | bytes 153608 | tf_op jit(solution)/shard_map/ppermute | solution.py:308
  11.1 6.0 %collective-permute-start = (bf16[50,512]{1,0:T(8,128)(2,1)S(1)}, bf16[50,512]{1,0:T(8,128)(2,1)S(1)}, u32[]{:S(2)}, u32[]{:S(2)}) collective-permute-start(bf16[50,512]{1,0:T(8,128)(2,1)S(1)} %project.1), channel_id=1, source_target_pairs={{0,24},{4,28},{8,16},{12,20},{16,8},{20,12},{24,0},{28,4},{1,25},{... | collective-permute-start | bytes 153608 | tf_op jit(solution)/shard_map/ppermute | solution.py:308
  11.1 9.3 %collective-permute-start.4 = (bf16[50,512]{1,0:T(8,128)(2,1)S(1)}, bf16[50,512]{1,0:T(8,128)(2,1)S(1)}, u32[]{:S(2)}, u32[]{:S(2)}) collective-permute-start(bf16[50,512]{1,0:T(8,128)(2,1)S(1)} %project.1), channel_id=1, source_target_pairs={{0,4},{4,0},{8,12},{12,8},{16,20},{20,16},{24,28},{28,24},{1,5},{5... | collective-permute-start | bytes 153608 | tf_op jit(solution)/shard_map/ppermute | solution.py:308
  17.1 5.3 %collective-permute-start.3 = (bf16[150,512]{1,0:T(8,128)(2,1)S(1)}, bf16[150,512]{1,0:T(8,128)(2,1)S(1)}, u32[]{:S(2)}, u32[]{:S(2)}) collective-permute-start(bf16[150,512]{1,0:T(8,128)(2,1)S(1)} %pad_maximum_fusion.1.even_ref), channel_id=1, source_target_pairs={{0,4},{4,0},{8,12},{12,8},{16,20},{20,16},{24,28},{28,24},{1,5},{5... | collective-permute-start | bytes 460808 | tf_op jit(solution)/shard_map/ppermute | solution.py:308
  27.8 5.8 %collective-permute-start.5 = (bf16[200,512]{1,0:T(8,128)(2,1)S(1)}, bf16[200,512]{1,0:T(8,128)(2,1)S(1)}, u32[]{:S(2)}, u32[]{:S(2)}) collective-permute-start(bf16[200,512]{1,0:T(8,128)(2,1)S(1)} %get-tuple-element.26), channel_id=1, source_target_pairs={{0,4},{4,0},{8,12},{12,8},{16,20},{20,16},{24,28},{28,24},{1,5},{5... | collective-permute-start | bytes 614408 | tf_op jit(solution)/shard_map/ppermute | solution.py:308
  33.8 7.9 %collective-permute-start.8 = (bf16[50,512]{1,0:T(8,128)(2,1)S(1)}, bf16[50,512]{1,0:T(8,128)(2,1)S(1)}, u32[]{:S(2)}, u32[]{:S(2)}) collective-permute-start(bf16[50,512]{1,0:T(8,128)(2,1)S(1)} %get-tuple-element.46), channel_id=1, source_target_pairs={{0,8},{4,12},{8,0},{12,4},{16,24},{20,28},{24,16},{28,20},{1,9},{5... | collective-permute-start | bytes 153608 | tf_op jit(solution)/shard_map/ppermute | solution.py:308
  33.9 7.8 %collective-permute-start.7 = (bf16[50,512]{1,0:T(8,128)(2,1)S(1)}, bf16[50,512]{1,0:T(8,128)(2,1)S(1)}, u32[]{:S(2)}, u32[]{:S(2)}) collective-permute-start(bf16[50,512]{1,0:T(8,128)(2,1)S(1)} %get-tuple-element.47), channel_id=1, source_target_pairs={{0,16},{4,20},{8,24},{12,28},{16,0},{20,4},{24,8},{28,12},{1,17},{... | collective-permute-start | bytes 153608 | tf_op jit(solution)/shard_map/ppermute | solution.py:308
  35.7 6.1 %copy-start = (bf16[8192,256]{1,0:T(8,128)(2,1)S(1)}, bf16[8192,256]{1,0:T(8,128)(2,1)}, u32[]{:S(2)}) copy-start(bf16[8192,256]{1,0:T(8,128)(2,1)} %wk_ref.3) | copy-start | bytes 12582916
  35.7 6.1 %copy-start.1 = (bf16[8192,256]{1,0:T(8,128)(2,1)S(1)}, bf16[8192,256]{1,0:T(8,128)(2,1)}, u32[]{:S(2)}) copy-start(bf16[8192,256]{1,0:T(8,128)(2,1)} %wv_ref.3) | copy-start | bytes 12582916
  35.7 6.0 %collective-permute-start.6 = (bf16[50,512]{1,0:T(8,128)(2,1)S(1)}, bf16[50,512]{1,0:T(8,128)(2,1)S(1)}, u32[]{:S(2)}, u32[]{:S(2)}) collective-permute-start(bf16[50,512]{1,0:T(8,128)(2,1)S(1)} %get-tuple-element.48), channel_id=1, source_target_pairs={{0,24},{4,28},{8,16},{12,20},{16,8},{20,12},{24,0},{28,4},{1,25},{... | collective-permute-start | bytes 153608 | tf_op jit(solution)/shard_map/ppermute | solution.py:308
  43.1 9.7 %copy-start.6 = (bf16[50,2048]{1,0:T(8,128)(2,1)S(1)}, bf16[50,2048]{1,0:T(8,128)(2,1)}, u32[]{:S(2)}) copy-start(bf16[50,2048]{1,0:T(8,128)(2,1)} %param.15) | copy-start | bytes 614404
  43.1 2.0 %collective-permute-start.10 = (bf16[50,2048]{1,0:T(8,128)(2,1)S(1)}, bf16[50,2048]{1,0:T(8,128)(2,1)S(1)}, u32[]{:S(2)}, u32[]{:S(2)}) collective-permute-start(bf16[50,2048]{1,0:T(8,128)(2,1)S(1)} %get-tuple-element.45), channel_id=1, source_target_pairs={{0,1},{1,0},{2,3},{3,2},{4,5},{5,4},{6,7},{7,6},{8,9},{9,8},{10,11... | collective-permute-start | bytes 614408 | tf_op jit(solution)/shard_map/ppermute | solution.py:308
  44.6 2.9 %collective-permute-start.9 = (bf16[50,2048]{1,0:T(8,128)(2,1)S(1)}, bf16[50,2048]{1,0:T(8,128)(2,1)S(1)}, u32[]{:S(2)}, u32[]{:S(2)}) collective-permute-start(bf16[50,2048]{1,0:T(8,128)(2,1)S(1)} %get-tuple-element.43), channel_id=1, source_target_pairs={{0,1},{1,0},{2,3},{3,2},{4,5},{5,4},{6,7},{7,6},{8,9},{9,8},{10,11... | collective-permute-start | bytes 614408 | tf_op jit(solution)/shard_map/ppermute | solution.py:308
  45.2 7.6 %collective-permute-start.11 = (bf16[50,2048]{1,0:T(8,128)(2,1)S(1)}, bf16[50,2048]{1,0:T(8,128)(2,1)S(1)}, u32[]{:S(2)}, u32[]{:S(2)}) collective-permute-start(bf16[50,2048]{1,0:T(8,128)(2,1)S(1)} %add_convert_fusion.1), channel_id=1, source_target_pairs={{0,2},{1,3},{2,0},{3,1},{4,6},{5,7},{6,4},{7,5},{8,10},{9,11},{10,... | collective-permute-start | bytes 614408 | tf_op jit(solution)/shard_map/ppermute | solution.py:308

commit v3 on v2

--- a/solution.py
+++ b/solution.py
@@ -20,6 +20,7 @@
 LAST = (((1,), (1,)), ((), ()))
 VMEM = pl.BlockSpec(memory_space=pltpu.VMEM)
 ANY = pl.BlockSpec(memory_space=pl.ANY)
+SMEM = pl.BlockSpec(memory_space=pltpu.SMEM)
 HBM = pl.BlockSpec(memory_space=pltpu.HBM)
 
 
@@ -105,6 +106,24 @@
     return jnp.where(key_pos <= row_pos, 0.0, -jnp.inf).astype(F32)
 
 
+def slot_bias(position, slots, count, dims):
+    row = lax.broadcasted_iota(jnp.int32, dims, 0)
+    bias = jnp.full(dims, -jnp.inf, F32)
+    for at, slot in enumerate(slots):
+        level = jnp.where((position ^ slot) < position, 0.0, -jnp.inf).astype(F32)
+        bias = jnp.where((row >= at * count) & (row < (at + 1) * count), level, bias)
+    return bias
+
+
+def fill_padded(wide_ref, rows_ref):
+    shown = rows_ref.shape[0]
+    padded = wide_ref.shape[0]
+    tail = shown // 8 * 8
+    if padded > tail:
+        wide_ref[tail:, :] = jnp.zeros((padded - tail, wide_ref.shape[1]), F32)
+    wide_ref[:shown, :] = rows_ref[...].astype(F32)
+
+
 def own_stats_kernel(q_ref, g_ref, k_ref, v_ref, stats_ref, bias_ref):
     bias_ref[...] = causal_bias(bias_ref.shape[0])
     for kv in range(k_ref.shape[1] // HD):
@@ -120,7 +139,7 @@
             stats_ref[head, 2:3, :] = jnp.sum(weights * dprobs, axis=0, keepdims=True)
 
 
-def own_stats(queries, out_grad, keys_own, values_own, held):
+def own_stats(queries, out_grad, keys_own, values_own):
     rows = queries.shape[0]
     heads = queries.shape[1] // HD
     return pl.pallas_call(
@@ -132,102 +151,132 @@
         scratch_shapes=[pltpu.VMEM((rows, rows), F32)],
         compiler_params=params(12),
         cost_estimate=cost(20 * heads * rows * rows * HD, 4 * rows * heads * HD),
-    )(queries, out_grad, keys_own, values_own, *held)
-
-
-def summary_kernel(
-    count, slots, seg_ref, q_ref, g_ref, odd_ref, even_ref, own_ref,
-    ds_ref, stats_ref, keys_ref, odd_grad_ref, even_grad_ref, bias_ref, both_ref,
+    )(queries, out_grad, keys_own, values_own)
+
+
+def even_stats_kernel(
+    count, evens, odds, seg_ref, q_ref, g_ref, even_ref, own_ref,
+    stats_ref, even_bias_ref, odd_bias_ref, wide_ref,
 ):
     position = seg_ref[0]
-    rows = q_ref.shape[0]
-    padded = both_ref.shape[0]
-    split = odd_ref.shape[0]
-    shown = split + even_ref.shape[0]
+    width = even_ref.shape[1] // 2
+    even_bias_ref[...] = slot_bias(position, evens, count, even_bias_ref.shape)
+    odd_bias_ref[...] = slot_bias(position, odds, count, odd_bias_ref.shape)
+    fill_padded(wide_ref, even_ref)
+    for kv in range(width // HD):
+        keys = wide_ref[:, lanes(kv)].astype(BF16)
+        values = wide_ref[:, lanes(width // HD + kv)].astype(BF16)
+        for head in range(kv * GROUP, (kv + 1) * GROUP):
+            scores = dot(keys, q_ref[:, lanes(head)], LAST) * SCALE2 + even_bias_ref[...]
+            own_top = own_ref[head, 0:1, :]
+            top = jnp.maximum(jnp.max(scores, axis=0, keepdims=True), own_top)
+            weights = jnp.exp2(scores - top)
+            shrink = jnp.exp2(own_top - top)
+            dprobs = dot(values, g_ref[:, lanes(head)], LAST)
+            total = jnp.sum(weights, axis=0, keepdims=True)
+            mixed = jnp.sum(weights * dprobs, axis=0, keepdims=True)
+            stats_ref[head, 0:1, :] = top
+            stats_ref[head, 1:2, :] = total + own_ref[head, 1:2, :] * shrink
+            stats_ref[head, 2:3, :] = mixed + own_ref[head, 2:3, :] * shrink
+
+
+def even_stats(position, queries, out_grad, even, own, count, evens, odds):
+    rows = queries.shape[0]
+    heads = queries.shape[1] // HD
+    padded = round_up(even.shape[0], 16)
+    return pl.pallas_call(
+        functools.partial(even_stats_kernel, count, evens, odds),
+        name="even_stats",
+        in_specs=[SMEM] + [VMEM] * 4,
+        out_specs=[VMEM] * 3,
+        out_shape=[
+            shape((heads, 8, rows), F32),
+            shape((padded, rows), F32),
+            shape((round_up(len(odds) * count, 16), rows), F32),
+        ],
+        scratch_shapes=[pltpu.VMEM((padded, even.shape[1]), F32)],
+        compiler_params=params(12 if padded <= 512 else 32),
+        cost_estimate=cost(20 * heads * rows * padded * HD, 4 * rows * heads * HD),
+    )(position, queries, out_grad, even, own)
+
+
+def slots_kernel(
+    last, q_ref, g_ref, slots_ref, before_ref, bias_ref,
+    ds_ref, stats_ref, keys_ref, grad_ref, wide_ref,
+):
+    shown = slots_ref.shape[0]
     kv_local = keys_ref.shape[1] // HD
     width = kv_local * HD
-
-    row = lax.broadcasted_iota(jnp.int32, (padded, rows), 0)
-    bias = jnp.full((padded, rows), -jnp.inf, F32)
-    for at, slot in enumerate(slots):
-        level = jnp.where((position ^ slot) < position, 0.0, -jnp.inf).astype(F32)
-        bias = jnp.where((row >= at * count) & (row < (at + 1) * count), level, bias)
-    bias_ref[...] = bias
-    if padded > shown:
-        tail = round_up(shown, 8) - 8
-        both_ref[tail:, :] = jnp.zeros((padded - tail, 2 * width), F32)
-    both_ref[:split, :] = odd_ref[...].astype(F32)
-    both_ref[split:shown, :] = even_ref[...].astype(F32)
-    keys_ref[...] = both_ref[:, :width].astype(BF16)
-
+    fill_padded(wide_ref, slots_ref)
+    keys_ref[...] = wide_ref[:, :width].astype(BF16)
     for kv in range(kv_local):
         keys = keys_ref[:, lanes(kv)]
-        values = both_ref[:, width + kv * HD : width + (kv + 1) * HD].astype(BF16)
+        values = wide_ref[:, lanes(kv_local + kv)].astype(BF16)
         heads = range(kv * GROUP, (kv + 1) * GROUP)
         all_dscores, all_probs = [], []
         for head in heads:
             scores = dot(keys, q_ref[:, lanes(head)], LAST) * SCALE2 + bias_ref[...]
-            own_top = own_ref[head, 0:1, :]
-            top = jnp.maximum(jnp.max(scores, axis=0, keepdims=True), own_top)
-            weights = jnp.exp2(scores - top)
-            shrink = jnp.exp2(own_top - top)
-            total = jnp.sum(weights, axis=0, keepdims=True) + own_ref[head, 1:2, :] * shrink
-            inverse = 1.0 / total
-            probs = weights * inverse
             dprobs = dot(values, g_ref[:, lanes(head)], LAST)
-            delta = jnp.sum(probs * dprobs, axis=0, keepdims=True)
-            delta = delta + own_ref[head, 2:3, :] * shrink * inverse
+            old_top = before_ref[head, 0:1, :]
+            if last:
+                top = jnp.maximum(jnp.max(scores, axis=0, keepdims=True), old_top)
+                weights = jnp.exp2(scores - top)
+                shrink = jnp.exp2(old_top - top)
+                total = jnp.sum(weights, axis=0, keepdims=True)
+                inverse = 1.0 / (total + before_ref[head, 1:2, :] * shrink)
+                mixed = jnp.sum(weights * dprobs, axis=0, keepdims=True)
+                delta = (mixed + before_ref[head, 2:3, :] * shrink) * inverse
+                probs = weights * inverse
+                stats_ref[head, 0:1, :] = top
+                stats_ref[head, 1:2, :] = inverse
+                stats_ref[head, 2:3, :] = delta
+            else:
+                probs = jnp.exp2(scores - old_top) * before_ref[head, 1:2, :]
+                delta = before_ref[head, 2:3, :]
             dscores = (probs * (dprobs - delta)).astype(BF16)
             ds_ref[head] = dscores
             all_dscores.append(dscores)
             all_probs.append(probs.astype(BF16))
-            stats_ref[head, 0:1, :] = top
-            stats_ref[head, 1:2, :] = inverse
-            stats_ref[head, 2:3, :] = delta
         queries = jnp.concatenate([q_ref[:, lanes(head)] for head in heads], 0)
         grads = jnp.concatenate([g_ref[:, lanes(head)] for head in heads], 0)
         key_part = dot(jnp.concatenate(all_dscores, 1), queries) * SCALE
         value_part = dot(jnp.concatenate(all_probs, 1), grads)
-        both_ref[:, lanes(kv)] = key_part
-        both_ref[:, width + kv * HD : width + (kv + 1) * HD] = value_part
-    odd_grad_ref[...] = both_ref[:split, :].astype(BF16)
-    even_grad_ref[...] = both_ref[split:shown, :]
-
-
-def summary_part(position, queries, out_grad, odd, even, own, held, count, slots):
+        grad_ref[:, lanes(kv)] = key_part[:shown].astype(grad_ref.dtype)
+        grad_ref[:, lanes(kv_local + kv)] = value_part[:shown].astype(grad_ref.dtype)
+    if not last:
+        stats_ref[...] = jnp.zeros_like(stats_ref)
+
+
+def slots_part(last, queries, out_grad, slots, before, bias):
     rows = queries.shape[0]
-    width = odd.shape[1] // 2
+    shown, width = slots.shape[0], slots.shape[1] // 2
     heads = queries.shape[1] // HD
-    padded = round_up(odd.shape[0] + even.shape[0], 16)
-    return pl.pallas_call(
-        functools.partial(summary_kernel, count, slots),
-        name="summary_part",
-        in_specs=[pl.BlockSpec(memory_space=pltpu.SMEM)] + [VMEM] * 5,
-        out_specs=[VMEM] * 5,
+    padded = round_up(shown, 16)
+    return pl.pallas_call(
+        functools.partial(slots_kernel, last),
+        name="odd_slots" if last else "even_slots",
+        in_specs=[VMEM] * 5,
+        out_specs=[VMEM] * 4,
         out_shape=[
             shape((heads, padded, rows)),
-            shape((heads, 8, rows), F32),
+            shape((heads, 8, rows) if last else (8, HD), F32),
             shape((padded, width)),
-            shape(odd.shape),
-            shape(even.shape, F32),
+            shape(slots.shape, BF16 if last else F32),
         ],
-        scratch_shapes=[
-            pltpu.VMEM((padded, rows), F32),
-            pltpu.VMEM((padded, 2 * width), F32),
-        ],
-        compiler_params=params(16 if padded <= 512 else 48),
-        cost_estimate=cost(40 * heads * rows * padded * HD, 4 * rows * heads * HD),
-    )(position, queries, out_grad, odd, even, own, *held)
+        scratch_shapes=[pltpu.VMEM((padded, 2 * width), F32)],
+        compiler_params=params(16 if padded <= 512 else 40),
+        cost_estimate=cost(30 * heads * rows * padded * HD, 4 * rows * heads * HD),
+    )(queries, out_grad, slots, before, bias)
 
 
 def own_grads_kernel(
-    kv, q_ref, g_ref, k_ref, v_ref, sk_ref, ds_ref, stats_ref, *rest
+    kv, q_ref, g_ref, k_ref, v_ref, ok_ref, ek_ref, ods_ref, eds_ref, stats_ref, *rest
 ):
     dq_out, dk_ref, dv_ref, bias_ref, dq_ref, sem = rest[-6:]
     bias_ref[...] = causal_bias(bias_ref.shape[0])
     keys = k_ref[:, lanes(kv)]
     values = v_ref[:, lanes(kv)]
-    keys_t = jnp.concatenate([sk_ref[:, lanes(kv)], keys], 0).T
+    keys_t = jnp.concatenate([ok_ref[:, lanes(kv)], ek_ref[:, lanes(kv)], keys], 0).T
     heads = range(kv * GROUP, (kv + 1) * GROUP)
     all_dscores, all_probs = [], []
     for at, head in enumerate(heads):
@@ -237,7 +286,7 @@
         dscores = (probs * (dprobs - stats_ref[head, 2:3, :])).astype(BF16)
         all_dscores.append(dscores)
         all_probs.append(probs.astype(BF16))
-        dquery = dot(keys_t, jnp.concatenate([ds_ref[head], dscores], 0))
+        dquery = dot(keys_t, jnp.concatenate([ods_ref[head], eds_ref[head], dscores], 0))
         dq_ref[:, lanes(at)] = (dquery * SCALE).T.astype(BF16)
     columns = pl.ds(kv * GROUP * HD, GROUP * HD)
     copy = pltpu.make_async_copy(dq_ref, dq_out.at[:, columns], sem)
@@ -249,17 +298,17 @@
     copy.wait()
 
 
-def own_grads(kv, queries, out_grad, keys_own, values_own, sum_keys, dscores, stats, held, earlier):
+def own_grads(kv, operands, earlier):
+    queries, odd_keys, even_keys = operands[0], operands[4], operands[5]
     rows = queries.shape[0]
     heads = queries.shape[1] // HD
-    padded = sum_keys.shape[0]
-    operands = [queries, out_grad, keys_own, values_own, sum_keys, dscores, stats, *held]
-    in_specs = [VMEM] * 7
+    padded = odd_keys.shape[0] + even_keys.shape[0]
+    in_specs = [VMEM] * len(operands)
     aliases = {}
     if earlier is not None:
-        operands.append(earlier)
+        aliases = {len(operands): 0}
+        operands = [*operands, earlier]
         in_specs.append(HBM)
-        aliases = {7: 0}
     return pl.pallas_call(
         functools.partial(own_grads_kernel, kv),
         name="own_grads",
@@ -296,7 +345,7 @@
     return pl.pallas_call(
         functools.partial(state_kernel, chunk, group),
         name="state_part",
-        in_specs=[pl.BlockSpec(memory_space=pltpu.SMEM)] + [VMEM] * 3,
+        in_specs=[SMEM] + [VMEM] * 3,
         out_specs=[VMEM] * count,
         out_shape=[shape((rows, wide))] * count,
         compiler_params=params(14),
@@ -319,50 +368,43 @@
     mine = lax.axis_index("tp").astype(jnp.int32).reshape(1)
 
     projected = project(summary_states, w_key, w_value)
-    held = ()
-    own = own_stats(queries, out_grad, keys_own, values_own, held)
-
-    evens = list(range(n_seg - 2, 0, -2))
-    odds = [j + 1 for j in evens] + [1]
+    own = own_stats(queries, out_grad, keys_own, values_own)
+
+    evens = sorted(range(2, n_seg, 2), key=lambda j: (j.bit_count(), -j))
+    odds = [1] + [j + 1 for j in evens]
     chunks = {j: exchange(projected, "seg", n_seg, j) for j in evens}
+    chunks[0] = projected
+    half = n_seg // 4
+    near = jnp.concatenate([chunks[j - 1] for j in odds[:half]], 0)
+    far = jnp.concatenate([chunks[j - 1] for j in odds[half:]], 0)
+    odd = jnp.concatenate([exchange(near, "seg", n_seg, 1), exchange(far, "seg", n_seg, 1)], 0)
     even = jnp.concatenate([chunks[j] for j in evens], 0)
-    odd = jnp.concatenate(
-        [exchange(even, "seg", n_seg, 1), exchange(projected, "seg", n_seg, 1)], 0
+
+    before, even_bias, odd_bias = even_stats(
+        position, queries, out_grad, even, own, count, evens, odds
     )
-
-    dscores, stats, sum_keys, odd_grad, even_grad = summary_part(
-        position, queries, out_grad, odd, even, own, held, count, odds + evens
+    odd_ds, stats, odd_keys, odd_grad = slots_part(
+        True, queries, out_grad, odd, before, odd_bias
     )
 
-    query_grad = None
-    key_blocks, value_blocks = [], []
-
-    def own_part(kv, earlier):
-        query_grad, key_block, value_block = own_grads(
-            kv, queries, out_grad, keys_own, values_own, sum_keys, dscores, stats, held, earlier
-        )
-        key_blocks.append(key_block)
-        value_blocks.append(value_block)
-        return query_grad
-
-    got = exchange(odd_grad, "seg", n_seg, 1)
-    query_grad = own_part(0, None)
-    got, query_grad = lax.optimization_barrier((got, query_grad))
-    got = got.astype(F32)
-    emitted = got[len(evens) * count :]
-    blocks = []
-    for at, j in enumerate(evens):
-        rows = slice(at * count, (at + 1) * count)
-        block = (even_grad[rows] + got[rows]).astype(BF16)
-        blocks.append(exchange(block, "seg", n_seg, j))
-    for kv in range(1, kv_local):
-        query_grad = own_part(kv, query_grad)
+    got = exchange(odd_grad, "seg", n_seg, 1).astype(F32)
+    even_ds, _, even_keys, even_grad = slots_part(
+        False, queries, out_grad, even, stats, even_bias
+    )
+    blocks = {}
+    for j in sorted(evens, key=lambda j: (-j.bit_length(), j)):
+        at = evens.index(j) * count
+        block = (even_grad[at : at + count] + got[at + count : at + 2 * count]).astype(BF16)
+        blocks[j] = exchange(block, "seg", n_seg, j)
+    operands = [
+        queries, out_grad, keys_own, values_own, odd_keys, even_keys, odd_ds, even_ds, stats
+    ]
+    query_grad, *first = own_grads(0, operands, None)
     blocks, query_grad = lax.optimization_barrier((blocks, query_grad))
-    for block in blocks:
+    emitted = got[:count]
+    for block in blocks.values():
         emitted = emitted + block.astype(F32)
     emitted = emitted.astype(BF16)
-    key_grad = jnp.concatenate(key_blocks, 1)
-    value_grad = jnp.concatenate(value_blocks, 1)
 
     wide = w_key.shape[0] // n_tp
     terms = {}
@@ -375,6 +417,14 @@
             terms[j ^ bit] = terms[j ^ bit].astype(F32) + got.astype(F32)
         bit *= 2
     state_grad = (terms[0] + summary_grad.astype(F32)).astype(BF16)
+
+    key_blocks, value_blocks = [first[0]], [first[1]]
+    for kv in range(1, kv_local):
+        query_grad, key_block, value_block = own_grads(kv, operands, query_grad)
+        key_blocks.append(key_block)
+        value_blocks.append(value_block)
+    key_grad = jnp.concatenate(key_blocks, 1)
+    value_grad = jnp.concatenate(value_blocks, 1)
     return (query_grad, key_grad, value_grad, state_grad)
 
 

time: 53.8 us -> 50.6 us (0.941)
  waiting for transfers between devices: 12.6 us -> 8.93 us
  Pallas kernels: 21.2 us -> 22.6 us
  starting transfers between devices: 17.2 us -> 16.2 us
    ppermute x12, waiting for transfers between devices: 12.6 us -> 8.93 us  [exchange(): return lax.ppermute(block, axis, [(i, i ^ key) for i in range(size)])]
    pallas_call x1 -> x3, Pallas kernels: 5.36 us -> 6.44 us  [the longest x2 5.07 us: slots_part(): pl.pallas_call(functools.partial(slots_kernel, last), name='odd_slots' if...]
    ppermute x12, starting transfers between devices: 17.2 us -> 16.2 us  [exchange(): return lax.ppermute(block, axis, [(i, i ^ key) for i in range(size)])]
  transfers between devices with their start and end apart: 12 -> 12, of which waited for: 5 -> 6; matrix products, arithmetic and copies ran while one was open for 2% -> 2% of each run, Pallas kernels for 18% -> 26%
where the time goes in v3:
time: 50.6 us; the launch traced here: 50.4 us
  Pallas kernels  22.6 us (45%)
  starting transfers between devices  16.2 us (32%)
  waiting for transfers between devices  8.93 us (18%)
  other arithmetic  1.85 us (4%)
  between operations  0.82 us (2%)
    ppermute x12, starting transfers between devices, exchange(): return lax.ppermute(block, axis, [(i, i ^ key) for i in range(size)])  16.2 us
    ppermute x12, waiting for transfers between devices, exchange(): return lax.ppermute(block, axis, [(i, i ^ key) for i in range(size)])  8.93 us
    pallas_call x2, Pallas kernels, own_grads(): pl.pallas_call(functools.partial(own_grads_kernel, kv), name='own_grads',...  6.73 us
    pallas_call x2, Pallas kernels, slots_part(): pl.pallas_call(functools.partial(slots_kernel, last), name='odd_slots' if...  5.07 us
    pallas_call x1, Pallas kernels, project(): pl.pallas_call(functools.partial(project_kernel, pieces), name='project',...  4.77 us
    pallas_call x2, Pallas kernels, state_part(): pl.pallas_call(functools.partial(state_kernel, chunk, group), name='state...  2.75 us
    pallas_call x1, Pallas kernels, own_stats(): pl.pallas_call(own_stats_kernel, name='own_stats', in_specs=[VMEM] * 4, o...  1.87 us
    pallas_call x1, Pallas kernels, even_stats(): pl.pallas_call(functools.partial(even_stats_kernel, count, evens, odds),...  1.37 us
  transfers between devices with their start and end apart: 12, of which 6 were waited for; matrix products, arithmetic and copies ran while one was open for 2% of the time, Pallas kernels for 26%

profile of v3, /device:TPU:0, one launch (start us, length us, event | category | flops | bytes accessed | tf_op | source)
XLA Modules:
  0.0 50.4 jit_solution(6490185537411104551)
XLA Ops:
  0.6 0.0 copy-start.3
  0.6 0.0 copy-start.2
  0.7 0.0 copy-start.5
  0.7 0.0 copy-start.4
  0.7 4.8 %project.1 = bf16[50,512]{1,0:T(8,128)(2,1)S(1)} custom-call(bf16[50,8192]{1,0:T(8,128)(2,1)} %states_hbm.1, bf16[8192,256]{1,0:T(8,128)(2,1)} %wk_ref.3, bf16[8192,256]{1,0:T(8,128)(2,1)} %wv_ref.3), custom_call_target="tpu_custom_call" | custom-call | flops 419430400 | bytes 16777216 | tf_op jit(solution)/shard_map/project/pallas_call | solution.py:86
  5.4 5.1 %collective-permute-start.3 = (bf16[50,512]{1,0:T(8,128)(2,1)S(1)}, bf16[50,512]{1,0:T(8,128)(2,1)S(1)}, u32[]{:S(2)}, u32[]{:S(2)}) collective-permute-start(bf16[50,512]{1,0:T(8,128)(2,1)S(1)} %project.1), channel_id=1, source_target_pairs={{0,24},{4,28},{8,16},{12,20},{16,8},{20,12},{24,0},{28,4},{1,25},{... | collective-permute-start | bytes 153608 | tf_op jit(solution)/shard_map/ppermute | solution.py:357
  10.6 0.0 collective-permute-start.2
  10.6 0.6 %collective-permute-start = (bf16[50,512]{1,0:T(8,128)(2,1)S(1)}, bf16[50,512]{1,0:T(8,128)(2,1)S(1)}, u32[]{:S(2)}, u32[]{:S(2)}) collective-permute-start(bf16[50,512]{1,0:T(8,128)(2,1)S(1)} %project.1), channel_id=1, source_target_pairs={{0,16},{4,20},{8,24},{12,28},{16,0},{20,4},{24,8},{28,12},{1,17},{... | collective-permute-start | bytes 153608 | tf_op jit(solution)/shard_map/ppermute | solution.py:357
  11.2 0.0 copy-done.3
  11.2 0.0 copy-done.2
  11.2 0.0 copy-done.5
  11.2 0.0 copy-done.4
  11.2 1.9 %own_stats.1.own_ref = f32[16,8,256]{2,1,0:T(8,128)S(1)} custom-call(bf16[256,2048]{1,0:T(8,128)(2,1)S(1)} %copy-done.2, bf16[256,2048]{1,0:T(8,128)(2,1)S(1)} %copy-done.3, bf16[256,256]{1,0:T(8,128)(2,1)S(1)} %copy-done.4, bf16[256,256]{1,0:T(8,128)(2,1)S(1)} %copy-done.5), custom_call_target="tpu_custom_call" | custom-call | flops 2684354560 | bytes 2097152 | tf_op jit(solution)/shard_map/own_stats/pallas_call | solution.py:145
  13.1 0.1 collective-permute-done.3
  13.2 1.7 %collective-permute-done.2 = bf16[50,512]{1,0:T(8,128)(2,1)S(1)} collective-permute-done((bf16[50,512]{1,0:T(8,128)(2,1)S(1)}, bf16[50,512]{1,0:T(8,128)(2,1)S(1)}, u32[]{:S(2)}, u32[]{:S(2)}) %collective-permute-start.2) | collective-permute-done | bytes 51232 | tf_op jit(solution)/shard_map/ppermute | solution.py:357
  14.9 1.6 %collective-permute-start.4 = (bf16[100,512]{1,0:T(8,128)(2,1)S(1)}, bf16[100,512]{1,0:T(8,128)(2,1)S(1)}, u32[]{:S(2)}, u32[]{:S(2)}) collective-permute-start(bf16[100,512]{1,0:T(8,128)(2,1)S(1)} %pad_maximum_fusion.5), channel_id=1, source_target_pairs={{0,4},{4,0},{8,12},{12,8},{16,20},{20,16},{24,28},{28,24},{1,5},{5... | collective-permute-start | bytes 307208 | tf_op jit(solution)/shard_map/ppermute | solution.py:357
  16.5 0.0 collective-permute-done
  16.5 1.1 %collective-permute-start.1 = (bf16[100,512]{1,0:T(8,128)(2,1)S(1)}, bf16[100,512]{1,0:T(8,128)(2,1)S(1)}, u32[]{:S(2)}, u32[]{:S(2)}) collective-permute-start(bf16[100,512]{1,0:T(8,128)(2,1)S(1)} %pad_maximum_fusion.4), channel_id=1, source_target_pairs={{0,4},{4,0},{8,12},{12,8},{16,20},{20,16},{24,28},{28,24},{1,5},{5... | collective-permute-start | bytes 307208 | tf_op jit(solution)/shard_map/ppermute | solution.py:357
  17.6 1.4 %even_stats.1 = (f32[16,8,256]{2,1,0:T(8,128)S(1)}, f32[160,256]{1,0:T(8,128)S(1)}, f32[208,256]{1,0:T(8,128)S(1)}) custom-call(s32[1]{0:T(128)} %bitcast.seg_ref, bf16[256,2048]{1,0:T(8,128)(2,1)S(1)} %copy-done.2, bf16[256,2048]{1,0:T(8,128)(2,1)S(1)} %copy-done.3, bf16[150,512]{1,0:T(8,128)(2,1)S(1)} %pad_maximum_fusion.1.even_ref.slots_ref, ...), custom_call_target="tpu_custom_call" | custom-call | flops 1677721600 | bytes 2097152 | tf_op jit(solution)/shard_map/even_stats/pallas_call | solution.py:187
  19.0 0.8 %collective-permute-done.4 = bf16[100,512]{1,0:T(8,128)(2,1)S(1)} collective-permute-done((bf16[100,512]{1,0:T(8,128)(2,1)S(1)}, bf16[100,512]{1,0:T(8,128)(2,1)S(1)}, u32[]{:S(2)}, u32[]{:S(2)}) %collective-permute-start.4) | collective-permute-done | bytes 102432 | tf_op jit(solution)/shard_map/ppermute | solution.py:357
  19.8 1.5 %collective-permute-done.1 = bf16[100,512]{1,0:T(8,128)(2,1)S(1)} collective-permute-done((bf16[100,512]{1,0:T(8,128)(2,1)S(1)}, bf16[100,512]{1,0:T(8,128)(2,1)S(1)}, u32[]{:S(2)}, u32[]{:S(2)}) %collective-permute-start.1) | collective-permute-done | bytes 102432 | tf_op jit(solution)/shard_map/ppermute | solution.py:357
  21.4 3.2 %odd_slots.1 = (bf16[16,208,256]{2,1,0:T(8,128)(2,1)S(1)}, f32[16,8,256]{2,1,0:T(8,128)S(1)}, bf16[208,256]{1,0:T(8,128)(2,1)S(1)}, bf16[200,512]{1,0:T(8,128)(2,1)S(1)}) custom-call(bf16[256,2048]{1,0:T(8,128)(2,1)S(1)} %copy-done.2, bf16[256,2048]{1,0:T(8,128)(2,1)S(1)} %copy-done.3, bf16[200,512]{1,0:T(8,128)(2,1)S(1)} %pad_maximum_fusion.slots_ref, ...), custom_call_target="tpu_custom_call" | custom-call | flops 3271557120 | bytes 2097152 | tf_op jit(solution)/shard_map/odd_slots/pallas_call | solution.py:255
  24.6 1.1 %collective-permute-start.5 = (bf16[200,512]{1,0:T(8,128)(2,1)S(1)}, bf16[200,512]{1,0:T(8,128)(2,1)S(1)}, u32[]{:S(2)}, u32[]{:S(2)}) collective-permute-start(bf16[200,512]{1,0:T(8,128)(2,1)S(1)} %get-tuple-element.37), channel_id=1, source_target_pairs={{0,4},{4,0},{8,12},{12,8},{16,20},{20,16},{24,28},{28,24},{1,5},{5... | collective-permute-start | bytes 614408 | tf_op jit(solution)/shard_map/ppermute | solution.py:357
  25.7 1.9 %even_slots.1 = (bf16[16,160,256]{2,1,0:T(8,128)(2,1)S(1)}, f32[8,128]{1,0:T(8,128)}, bf16[160,256]{1,0:T(8,128)(2,1)S(1)}, f32[150,512]{1,0:T(8,128)S(1)}) custom-call(bf16[256,2048]{1,0:T(8,128)(2,1)S(1)} %copy-done.2, bf16[256,2048]{1,0:T(8,128)(2,1)S(1)} %copy-done.3, bf16[150,512]{1,0:T(8,128)(2,1)S(1)} %pad_maximum_fusion.1.even_ref.slots_ref, ...), custom_call_target="tpu_custom_call" | custom-call | flops 2516582400 | bytes 2097152 | tf_op jit(solution)/shard_map/even_slots/pallas_call | solution.py:255
  27.6 2.8 %collective-permute-done.5 = bf16[200,512]{1,0:T(8,128)(2,1)S(1)} collective-permute-done((bf16[200,512]{1,0:T(8,128)(2,1)S(1)}, bf16[200,512]{1,0:T(8,128)(2,1)S(1)}, u32[]{:S(2)}, u32[]{:S(2)}) %collective-permute-start.5) | collective-permute-done | bytes 204832 | tf_op jit(solution)/shard_map/ppermute | solution.py:357
  30.4 0.1 fusion.3
  30.5 2.4 %collective-permute-start.8 = (bf16[50,512]{1,0:T(8,128)(2,1)S(1)}, bf16[50,512]{1,0:T(8,128)(2,1)S(1)}, u32[]{:S(2)}, u32[]{:S(2)}) collective-permute-start(bf16[50,512]{1,0:T(8,128)(2,1)S(1)} %get-tuple-element.52), channel_id=1, source_target_pairs={{0,24},{4,28},{8,16},{12,20},{16,8},{20,12},{24,0},{28,4},{1,25},{... | collective-permute-start | bytes 153608 | tf_op jit(solution)/shard_map/ppermute | solution.py:357
  32.9 0.3 collective-permute-start.7
  33.2 1.8 %collective-permute-start.6 = (bf16[50,512]{1,0:T(8,128)(2,1)S(1)}, bf16[50,512]{1,0:T(8,128)(2,1)S(1)}, u32[]{:S(2)}, u32[]{:S(2)}) collective-permute-start(bf16[50,512]{1,0:T(8,128)(2,1)S(1)} %get-tuple-element.54), channel_id=1, source_target_pairs={{0,8},{4,12},{8,0},{12,4},{16,24},{20,28},{24,16},{28,20},{1,9},{5... | collective-permute-start | bytes 153608 | tf_op jit(solution)/shard_map/ppermute | solution.py:357
  35.0 0.0 copy-start
  35.0 0.0 copy-start.1
  35.0 3.5 %own_grads.2 = (bf16[256,2048]{1,0:T(8,128)(2,1)}, bf16[256,128]{1,0:T(8,128)(2,1)S(1)}, bf16[256,128]{1,0:T(8,128)(2,1)S(1)}) custom-call(bf16[256,2048]{1,0:T(8,128)(2,1)S(1)} %copy-done.2, bf16[256,2048]{1,0:T(8,128)(2,1)S(1)} %copy-done.3, bf16[256,256]{1,0:T(8,128)(2,1)S(1)} %copy-done.4, bf16[256,256]{1,0:T(8,128)(2,1)S(1)} %copy-done.5, ...), custom_call_target="tpu_custom_call" | custom-call | flops 2684354560 | bytes 2097152 | tf_op jit(solution)/shard_map/own_grads/pallas_call | solution.py:312
  38.5 0.0 collective-permute-done.8
  38.5 0.0 collective-permute-done.7
  38.5 0.0 collective-permute-done.6
  38.5 0.0 copy-done
  38.5 0.0 copy-done.1
  38.5 1.4 %state_part.3 = (bf16[50,2048]{1,0:T(8,128)(2,1)S(1)}, bf16[50,2048]{1,0:T(8,128)(2,1)S(1)}) custom-call(s32[1]{0:T(128)} %bitcast.1.mine_ref, bf16[50,512]{1,0:T(8,128)(2,1)S(1)} %fusion.2.emitted_ref, bf16[8192,256]{1,0:T(8,128)(2,1)S(1)} %copy-done, bf16[8192,256]{1,0:T(8,128)(2,1)S(1)} %copy-done.1), custom_call_target="tpu_custom_call" | custom-call | flops 209715200 | bytes 4194304 | tf_op jit(solution)/shard_map/state_part/pallas_call | solution.py:345
  39.9 0.1 collective-permute-start.10
  40.0 1.4 %state_part.2 = (bf16[50,2048]{1,0:T(8,128)(2,1)S(1)}, bf16[50,2048]{1,0:T(8,128)(2,1)S(1)}) custom-call(s32[1]{0:T(128)} %bitcast.1.mine_ref, bf16[50,512]{1,0:T(8,128)(2,1)S(1)} %fusion.2.emitted_ref, bf16[8192,256]{1,0:T(8,128)(2,1)S(1)} %copy-done, bf16[8192,256]{1,0:T(8,128)(2,1)S(1)} %copy-done.1), custom_call_target="tpu_custom_call" | custom-call | flops 209715200 | bytes 4194304 | tf_op jit(solution)/shard_map/state_part/pallas_call | solution.py:345
  41.4 0.6 %collective-permute-start.9 = (bf16[50,2048]{1,0:T(8,128)(2,1)S(1)}, bf16[50,2048]{1,0:T(8,128)(2,1)S(1)}, u32[]{:S(2)}, u32[]{:S(2)}) collective-permute-start(bf16[50,2048]{1,0:T(8,128)(2,1)S(1)} %get-tuple-element.49), channel_id=1, source_target_pairs={{0,1},{1,0},{2,3},{3,2},{4,5},{5,4},{6,7},{7,6},{8,9},{9,8},{10,11... | collective-permute-start | bytes 614408 | tf_op jit(solution)/shard_map/ppermute | solution.py:357
  41.9 0.0 collective-permute-done.10
  41.9 0.1 add_convert_fusion.1
  42.0 0.0 copy-start.6
  42.0 1.6 %collective-permute-start.11 = (bf16[50,2048]{1,0:T(8,128)(2,1)S(1)}, bf16[50,2048]{1,0:T(8,128)(2,1)S(1)}, u32[]{:S(2)}, u32[]{:S(2)}) collective-permute-start(bf16[50,2048]{1,0:T(8,128)(2,1)S(1)} %add_convert_fusion.1), channel_id=1, source_target_pairs={{0,2},{1,3},{2,0},{3,1},{4,6},{5,7},{6,4},{7,5},{8,10},{9,11},{10,... | collective-permute-start | bytes 614408 | tf_op jit(solution)/shard_map/ppermute | solution.py:357
  43.6 3.3 %own_grads.3 = (bf16[256,2048]{1,0:T(8,128)(2,1)}, bf16[256,128]{1,0:T(8,128)(2,1)S(1)}, bf16[256,128]{1,0:T(8,128)(2,1)S(1)}) custom-call(bf16[256,2048]{1,0:T(8,128)(2,1)S(1)} %copy-done.2, bf16[256,2048]{1,0:T(8,128)(2,1)S(1)} %copy-done.3, bf16[256,256]{1,0:T(8,128)(2,1)S(1)} %copy-done.4, ...), custom_call_target="tpu_custom_call", output_to_operand_aliasing={{0}: (9, {})} | custom-call | flops 2684354560 | bytes 2097152 | tf_op jit(solution)/shard_map/own_grads/pallas_call | solution.py:312
  46.9 0.7 %pad_maximum_fusion.2 = (bf16[256,256]{1,0:T(8,128)(2,1)}, bf16[256,256]{1,0:T(8,128)(2,1)}) fusion(bf16[256,128]{1,0:T(8,128)(2,1)S(1)} %get-tuple-element.42, bf16[256,128]{1,0:T(8,128)(2,1)S(1)} %get-tuple-element.41, bf16[256,128]{1,0:T(8,128)(2,1)S(1)} %get-tuple-element.44, bf16[256,128]{1,0:T(8,128)(2,1)S(1)} %get-tuple-element.43), kind=kLoop, calls=%fused_computation.4 | loop fusion | flops 524288 | bytes 524288 | tf_op jit(solution)/shard_map/concatenate | solution.py:426
  47.6 0.0 collective-permute-done.9
  47.6 2.0 %collective-permute-done.11 = bf16[50,2048]{1,0:T(8,128)(2,1)S(1)} collective-permute-done((bf16[50,2048]{1,0:T(8,128)(2,1)S(1)}, bf16[50,2048]{1,0:T(8,128)(2,1)S(1)}, u32[]{:S(2)}, u32[]{:S(2)}) %collective-permute-start.11) | collective-permute-done | bytes 204832 | tf_op jit(solution)/shard_map/ppermute | solution.py:357
  49.6 0.0 copy-done.6
  49.6 0.8 %add_convert_fusion = bf16[50,2048]{1,0:T(8,128)(2,1)} fusion(bf16[50,2048]{1,0:T(8,128)(2,1)S(1)} %copy-done.6, bf16[50,2048]{1,0:T(8,128)(2,1)S(1)} %collective-permute-done.11, bf16[50,2048]{1,0:T(8,128)(2,1)S(1)} %collective-permute-done.9, bf16[50,2048]{1,0:T(8,128)(2,1)S(1)} %get-tuple-element.48), kind=kLoop, calls=%fused_computation | loop fusion | flops 819200 | bytes 1024000 | tf_op jit(solution)/shard_map/convert_element_type | solution.py:419
  (6 shorter events, 0.2 us)
Async XLA Ops:
  0.6 10.6 %copy-start.3 = (bf16[256,2048]{1,0:T(8,128)(2,1)S(1)}, bf16[256,2048]{1,0:T(8,128)(2,1)}, u32[]{:S(2)}) copy-start(bf16[256,2048]{1,0:T(8,128)(2,1)} %g_ref.11) | copy-start | bytes 3145732
  0.6 10.6 %copy-start.2 = (bf16[256,2048]{1,0:T(8,128)(2,1)S(1)}, bf16[256,2048]{1,0:T(8,128)(2,1)}, u32[]{:S(2)}) copy-start(bf16[256,2048]{1,0:T(8,128)(2,1)} %q_ref.11) | copy-start | bytes 3145732
  0.7 10.6 %copy-start.5 = (bf16[256,256]{1,0:T(8,128)(2,1)S(1)}, bf16[256,256]{1,0:T(8,128)(2,1)}, u32[]{:S(2)}) copy-start(bf16[256,256]{1,0:T(8,128)(2,1)} %v_ref.5) | copy-start | bytes 393220
  0.7 10.6 %copy-start.4 = (bf16[256,256]{1,0:T(8,128)(2,1)S(1)}, bf16[256,256]{1,0:T(8,128)(2,1)}, u32[]{:S(2)}) copy-start(bf16[256,256]{1,0:T(8,128)(2,1)} %k_ref.5) | copy-start | bytes 393220
  5.4 7.8 %collective-permute-start.3 = (bf16[50,512]{1,0:T(8,128)(2,1)S(1)}, bf16[50,512]{1,0:T(8,128)(2,1)S(1)}, u32[]{:S(2)}, u32[]{:S(2)}) collective-permute-start(bf16[50,512]{1,0:T(8,128)(2,1)S(1)} %project.1), channel_id=1, source_target_pairs={{0,24},{4,28},{8,16},{12,20},{16,8},{20,12},{24,0},{28,4},{1,25},{... | collective-permute-start | bytes 153608 | tf_op jit(solution)/shard_map/ppermute | solution.py:357
  10.6 4.3 %collective-permute-start.2 = (bf16[50,512]{1,0:T(8,128)(2,1)S(1)}, bf16[50,512]{1,0:T(8,128)(2,1)S(1)}, u32[]{:S(2)}, u32[]{:S(2)}) collective-permute-start(bf16[50,512]{1,0:T(8,128)(2,1)S(1)} %project.1), channel_id=1, source_target_pairs={{0,8},{4,12},{8,0},{12,4},{16,24},{20,28},{24,16},{28,20},{1,9},{5... | collective-permute-start | bytes 153608 | tf_op jit(solution)/shard_map/ppermute | solution.py:357
  10.6 6.0 %collective-permute-start = (bf16[50,512]{1,0:T(8,128)(2,1)S(1)}, bf16[50,512]{1,0:T(8,128)(2,1)S(1)}, u32[]{:S(2)}, u32[]{:S(2)}) collective-permute-start(bf16[50,512]{1,0:T(8,128)(2,1)S(1)} %project.1), channel_id=1, source_target_pairs={{0,16},{4,20},{8,24},{12,28},{16,0},{20,4},{24,8},{28,12},{1,17},{... | collective-permute-start | bytes 153608 | tf_op jit(solution)/shard_map/ppermute | solution.py:357
  14.9 4.9 %collective-permute-start.4 = (bf16[100,512]{1,0:T(8,128)(2,1)S(1)}, bf16[100,512]{1,0:T(8,128)(2,1)S(1)}, u32[]{:S(2)}, u32[]{:S(2)}) collective-permute-start(bf16[100,512]{1,0:T(8,128)(2,1)S(1)} %pad_maximum_fusion.5), channel_id=1, source_target_pairs={{0,4},{4,0},{8,12},{12,8},{16,20},{20,16},{24,28},{28,24},{1,5},{5... | collective-permute-start | bytes 307208 | tf_op jit(solution)/shard_map/ppermute | solution.py:357
  16.5 4.8 %collective-permute-start.1 = (bf16[100,512]{1,0:T(8,128)(2,1)S(1)}, bf16[100,512]{1,0:T(8,128)(2,1)S(1)}, u32[]{:S(2)}, u32[]{:S(2)}) collective-permute-start(bf16[100,512]{1,0:T(8,128)(2,1)S(1)} %pad_maximum_fusion.4), channel_id=1, source_target_pairs={{0,4},{4,0},{8,12},{12,8},{16,20},{20,16},{24,28},{28,24},{1,5},{5... | collective-permute-start | bytes 307208 | tf_op jit(solution)/shard_map/ppermute | solution.py:357
  24.6 5.8 %collective-permute-start.5 = (bf16[200,512]{1,0:T(8,128)(2,1)S(1)}, bf16[200,512]{1,0:T(8,128)(2,1)S(1)}, u32[]{:S(2)}, u32[]{:S(2)}) collective-permute-start(bf16[200,512]{1,0:T(8,128)(2,1)S(1)} %get-tuple-element.37), channel_id=1, source_target_pairs={{0,4},{4,0},{8,12},{12,8},{16,20},{20,16},{24,28},{28,24},{1,5},{5... | collective-permute-start | bytes 614408 | tf_op jit(solution)/shard_map/ppermute | solution.py:357
  30.5 7.9 %collective-permute-start.8 = (bf16[50,512]{1,0:T(8,128)(2,1)S(1)}, bf16[50,512]{1,0:T(8,128)(2,1)S(1)}, u32[]{:S(2)}, u32[]{:S(2)}) collective-permute-start(bf16[50,512]{1,0:T(8,128)(2,1)S(1)} %get-tuple-element.52), channel_id=1, source_target_pairs={{0,24},{4,28},{8,16},{12,20},{16,8},{20,12},{24,0},{28,4},{1,25},{... | collective-permute-start | bytes 153608 | tf_op jit(solution)/shard_map/ppermute | solution.py:357
  32.9 5.5 %collective-permute-start.7 = (bf16[50,512]{1,0:T(8,128)(2,1)S(1)}, bf16[50,512]{1,0:T(8,128)(2,1)S(1)}, u32[]{:S(2)}, u32[]{:S(2)}) collective-permute-start(bf16[50,512]{1,0:T(8,128)(2,1)S(1)} %get-tuple-element.53), channel_id=1, source_target_pairs={{0,16},{4,20},{8,24},{12,28},{16,0},{20,4},{24,8},{28,12},{1,17},{... | collective-permute-start | bytes 153608 | tf_op jit(solution)/shard_map/ppermute | solution.py:357
  33.2 5.3 %collective-permute-start.6 = (bf16[50,512]{1,0:T(8,128)(2,1)S(1)}, bf16[50,512]{1,0:T(8,128)(2,1)S(1)}, u32[]{:S(2)}, u32[]{:S(2)}) collective-permute-start(bf16[50,512]{1,0:T(8,128)(2,1)S(1)} %get-tuple-element.54), channel_id=1, source_target_pairs={{0,8},{4,12},{8,0},{12,4},{16,24},{20,28},{24,16},{28,20},{1,9},{5... | collective-permute-start | bytes 153608 | tf_op jit(solution)/shard_map/ppermute | solution.py:357
  35.0 3.5 %copy-start = (bf16[8192,256]{1,0:T(8,128)(2,1)S(1)}, bf16[8192,256]{1,0:T(8,128)(2,1)}, u32[]{:S(2)}) copy-start(bf16[8192,256]{1,0:T(8,128)(2,1)} %wk_ref.3) | copy-start | bytes 12582916
  35.0 3.6 %copy-start.1 = (bf16[8192,256]{1,0:T(8,128)(2,1)S(1)}, bf16[8192,256]{1,0:T(8,128)(2,1)}, u32[]{:S(2)}) copy-start(bf16[8192,256]{1,0:T(8,128)(2,1)} %wv_ref.3) | copy-start | bytes 12582916
  39.9 2.0 %collective-permute-start.10 = (bf16[50,2048]{1,0:T(8,128)(2,1)S(1)}, bf16[50,2048]{1,0:T(8,128)(2,1)S(1)}, u32[]{:S(2)}, u32[]{:S(2)}) collective-permute-start(bf16[50,2048]{1,0:T(8,128)(2,1)S(1)} %get-tuple-element.51), channel_id=1, source_target_pairs={{0,1},{1,0},{2,3},{3,2},{4,5},{5,4},{6,7},{7,6},{8,9},{9,8},{10,11... | collective-permute-start | bytes 614408 | tf_op jit(solution)/shard_map/ppermute | solution.py:357
  41.4 6.2 %collective-permute-start.9 = (bf16[50,2048]{1,0:T(8,128)(2,1)S(1)}, bf16[50,2048]{1,0:T(8,128)(2,1)S(1)}, u32[]{:S(2)}, u32[]{:S(2)}) collective-permute-start(bf16[50,2048]{1,0:T(8,128)(2,1)S(1)} %get-tuple-element.49), channel_id=1, source_target_pairs={{0,1},{1,0},{2,3},{3,2},{4,5},{5,4},{6,7},{7,6},{8,9},{9,8},{10,11... | collective-permute-start | bytes 614408 | tf_op jit(solution)/shard_map/ppermute | solution.py:357
  42.0 7.6 %copy-start.6 = (bf16[50,2048]{1,0:T(8,128)(2,1)S(1)}, bf16[50,2048]{1,0:T(8,128)(2,1)}, u32[]{:S(2)}) copy-start(bf16[50,2048]{1,0:T(8,128)(2,1)} %param.15) | copy-start | bytes 614404
  42.0 7.6 %collective-permute-start.11 = (bf16[50,2048]{1,0:T(8,128)(2,1)S(1)}, bf16[50,2048]{1,0:T(8,128)(2,1)S(1)}, u32[]{:S(2)}, u32[]{:S(2)}) collective-permute-start(bf16[50,2048]{1,0:T(8,128)(2,1)S(1)} %add_convert_fusion.1), channel_id=1, source_target_pairs={{0,2},{1,3},{2,0},{3,1},{4,6},{5,7},{6,4},{7,5},{8,10},{9,11},{10,... | collective-permute-start | bytes 614408 | tf_op jit(solution)/shard_map/ppermute | solution.py:357

commit v4 on v3

--- a/solution.py
+++ b/solution.py
@@ -52,12 +52,11 @@
     pieces, states_hbm, wk_hbm, wv_hbm, out_ref, wk_ref, wv_ref, states_ref, sems
 ):
     width = wk_ref.shape[1]
-    chunk = wk_ref.shape[0] // pieces
-    states_copy = pltpu.make_async_copy(states_hbm, states_ref, sems.at[2 * pieces])
+    states_copy = pltpu.make_async_copy(states_hbm, states_ref, sems.at[2 * len(pieces)])
     states_copy.start()
     copies = []
-    for at in range(pieces):
-        rows = pl.ds(at * chunk, chunk)
+    for at, (start, stop) in enumerate(pieces):
+        rows = pl.ds(start, stop - start)
         pair = (
             pltpu.make_async_copy(wk_hbm.at[rows], wk_ref.at[rows], sems.at[2 * at]),
             pltpu.make_async_copy(wv_hbm.at[rows], wv_ref.at[rows], sems.at[2 * at + 1]),
@@ -67,21 +66,22 @@
         copies.append(pair)
     states_copy.wait()
     keys = values = None
-    for at, (key_copy, value_copy) in enumerate(copies):
-        rows = slice(at * chunk, (at + 1) * chunk)
-        states = states_ref[:, rows]
-        key_copy.wait()
-        term = dot(states, wk_ref[rows, :])
-        keys = term if keys is None else keys + term
-        value_copy.wait()
-        term = dot(states, wv_ref[rows, :])
-        values = term if values is None else values + term
+    for (start, stop), pair in zip(pieces, copies):
+        states = states_ref[:, start:stop]
+        for copy in pair:
+            copy.wait()
+        key_term = dot(states, wk_ref[start:stop, :])
+        value_term = dot(states, wv_ref[start:stop, :])
+        keys = key_term if keys is None else keys + key_term
+        values = value_term if values is None else values + value_term
     out_ref[:, :width] = keys.astype(BF16)
     out_ref[:, width:] = values.astype(BF16)
 
 
-def project(states, w_key, w_value, pieces=8):
+def project(states, w_key, w_value):
     rows, depth = states.shape
+    edges = [depth * part // 64 for part in (0, 8, 16, 24, 32, 40, 48, 56, 60, 62, 63, 64)]
+    pieces = list(zip(edges, edges[1:]))
     width = w_key.shape[1]
     return pl.pallas_call(
         functools.partial(project_kernel, pieces),
@@ -93,7 +93,7 @@
             pltpu.VMEM(w_key.shape, BF16),
             pltpu.VMEM(w_value.shape, BF16),
             pltpu.VMEM((rows, depth), BF16),
-            pltpu.SemaphoreType.DMA((2 * pieces + 1,)),
+            pltpu.SemaphoreType.DMA((2 * len(pieces) + 1,)),
         ],
         compiler_params=params(12),
         cost_estimate=cost(4 * rows * depth * width, 8 * depth * width),
@@ -370,14 +370,19 @@
     projected = project(summary_states, w_key, w_value)
     own = own_stats(queries, out_grad, keys_own, values_own)
 
-    evens = sorted(range(2, n_seg, 2), key=lambda j: (j.bit_count(), -j))
-    odds = [1] + [j + 1 for j in evens]
-    chunks = {j: exchange(projected, "seg", n_seg, j) for j in evens}
+    near = [j for j in range(0, n_seg, 2) if not j & 2]
+    far = [j for j in range(0, n_seg, 2) if j & 2]
+    evens = (near + far)[1:]
+    odds = [j + 1 for j in near + far]
+    chunks = {j: exchange(projected, "seg", n_seg, j) for j in range(2, n_seg, 2)}
     chunks[0] = projected
-    half = n_seg // 4
-    near = jnp.concatenate([chunks[j - 1] for j in odds[:half]], 0)
-    far = jnp.concatenate([chunks[j - 1] for j in odds[half:]], 0)
-    odd = jnp.concatenate([exchange(near, "seg", n_seg, 1), exchange(far, "seg", n_seg, 1)], 0)
+    odd = jnp.concatenate(
+        [
+            exchange(jnp.concatenate([chunks[j] for j in group], 0), "seg", n_seg, 1)
+            for group in (near, far)
+        ],
+        0,
+    )
     even = jnp.concatenate([chunks[j] for j in evens], 0)
 
     before, even_bias, odd_bias = even_stats(
@@ -392,7 +397,7 @@
         False, queries, out_grad, even, stats, even_bias
     )
     blocks = {}
-    for j in sorted(evens, key=lambda j: (-j.bit_length(), j)):
+    for j in sorted(evens, key=lambda j: (j.bit_count(), -j)):
         at = evens.index(j) * count
         block = (even_grad[at : at + count] + got[at + count : at + 2 * count]).astype(BF16)
         blocks[j] = exchange(block, "seg", n_seg, j)
@@ -407,15 +412,24 @@
     emitted = emitted.astype(BF16)
 
     wide = w_key.shape[0] // n_tp
+    far_group, near_group = list(range(n_tp - 1, 1, -1)), [1, 0]
     terms = {}
-    for group in (list(range(n_tp - 1, 1, -1)), [1, 0]):
+    for group in ([j for j in far_group if j & 1], [j for j in far_group if not j & 1]):
         terms.update(zip(group, state_part(mine, emitted, w_key, w_value, wide, group)))
     bit = 1
     while bit < n_tp:
-        for j in sorted((j for j in terms if j & bit), reverse=True):
+        for j in sorted((j for j in terms if j & bit and j > bit), reverse=True):
             got = exchange(terms.pop(j).astype(BF16), "tp", n_tp, bit)
             terms[j ^ bit] = terms[j ^ bit].astype(F32) + got.astype(F32)
         bit *= 2
+    terms = {j: terms[j].astype(BF16) for j in terms}
+    terms, emitted = lax.optimization_barrier((terms, emitted))
+    sent = {j: exchange(terms[j], "tp", n_tp, j) for j in terms}
+    other, state = state_part(mine, emitted, w_key, w_value, wide, near_group)
+    state = state.astype(F32) + exchange(other, "tp", n_tp, 1).astype(F32)
+    for j in sent:
+        state = state + sent[j].astype(F32)
+    terms = {0: state}
     state_grad = (terms[0] + summary_grad.astype(F32)).astype(BF16)
 
     key_blocks, value_blocks = [first[0]], [first[1]]

time: 50.6 us -> 49 us (0.968)
  waiting for transfers between devices: 8.93 us -> 8.28 us
    ppermute x12, waiting for transfers between devices: 8.93 us -> 8.28 us  [exchange(): return lax.ppermute(block, axis, [(i, i ^ key) for i in range(size)])]
    pallas_call x1, Pallas kernels: 4.77 us -> 4.26 us  [project(): pl.pallas_call(functools.partial(project_kernel, pieces), name='project',...]
    pallas_call x2 -> x3, Pallas kernels: 2.75 us -> 2.88 us  [state_part(): pl.pallas_call(functools.partial(state_kernel, chunk, group), name='state...]
  transfers between devices with their start and end apart: 12 -> 12, of which waited for: 6 -> 7; matrix products, arithmetic and copies ran while one was open for 2% -> 2% of each run, Pallas kernels for 26% -> 28%
where the time goes in v4:
time: 49 us; the launch traced here: 48.9 us
  Pallas kernels  22.1 us (45%)
  starting transfers between devices  15.7 us (32%)
  waiting for transfers between devices  8.28 us (17%)
  other arithmetic  1.86 us (4%)
  between operations  0.83 us (2%)
    ppermute x12, starting transfers between devices, exchange(): return lax.ppermute(block, axis, [(i, i ^ key) for i in range(size)])  15.7 us
    ppermute x12, waiting for transfers between devices, exchange(): return lax.ppermute(block, axis, [(i, i ^ key) for i in range(size)])  8.28 us
    pallas_call x2, Pallas kernels, own_grads(): pl.pallas_call(functools.partial(own_grads_kernel, kv), name='own_grads',...  6.71 us
    pallas_call x2, Pallas kernels, slots_part(): pl.pallas_call(functools.partial(slots_kernel, last), name='odd_slots' if...  5.05 us
    pallas_call x1, Pallas kernels, project(): pl.pallas_call(functools.partial(project_kernel, pieces), name='project',...  4.26 us
    pallas_call x3, Pallas kernels, state_part(): pl.pallas_call(functools.partial(state_kernel, chunk, group), name='state...  2.88 us
    pallas_call x1, Pallas kernels, own_stats(): pl.pallas_call(own_stats_kernel, name='own_stats', in_specs=[VMEM] * 4, o...  1.87 us
    pallas_call x1, Pallas kernels, even_stats(): pl.pallas_call(functools.partial(even_stats_kernel, count, evens, odds),...  1.37 us
  transfers between devices with their start and end apart: 12, of which 7 were waited for; matrix products, arithmetic and copies ran while one was open for 2% of the time, Pallas kernels for 28%

profile of v4, /device:TPU:0, one launch (start us, length us, event | category | flops | bytes accessed | tf_op | source)
XLA Modules:
  0.0 48.9 jit_solution(2629144826655456403)
XLA Ops:
  0.6 0.0 copy-start.3
  0.6 0.0 copy-start.2
  0.7 0.0 copy-start.5
  0.7 0.0 copy-start.4
  0.7 4.3 %project.1 = bf16[50,512]{1,0:T(8,128)(2,1)S(1)} custom-call(bf16[50,8192]{1,0:T(8,128)(2,1)} %states_hbm.1, bf16[8192,256]{1,0:T(8,128)(2,1)} %wk_ref.5, bf16[8192,256]{1,0:T(8,128)(2,1)} %wv_ref.5), custom_call_target="tpu_custom_call" | custom-call | flops 419430400 | bytes 16777216 | tf_op jit(solution)/shard_map/project/pallas_call | solution.py:86
  4.9 5.1 %collective-permute-start.3 = (bf16[50,512]{1,0:T(8,128)(2,1)S(1)}, bf16[50,512]{1,0:T(8,128)(2,1)S(1)}, u32[]{:S(2)}, u32[]{:S(2)}) collective-permute-start(bf16[50,512]{1,0:T(8,128)(2,1)S(1)} %project.1), channel_id=1, source_target_pairs={{0,24},{4,28},{8,16},{12,20},{16,8},{20,12},{24,0},{28,4},{1,25},{... | collective-permute-start | bytes 153608 | tf_op jit(solution)/shard_map/ppermute | solution.py:357
  10.1 0.0 collective-permute-start.2
  10.1 0.6 %collective-permute-start = (bf16[50,512]{1,0:T(8,128)(2,1)S(1)}, bf16[50,512]{1,0:T(8,128)(2,1)S(1)}, u32[]{:S(2)}, u32[]{:S(2)}) collective-permute-start(bf16[50,512]{1,0:T(8,128)(2,1)S(1)} %project.1), channel_id=1, source_target_pairs={{0,16},{4,20},{8,24},{12,28},{16,0},{20,4},{24,8},{28,12},{1,17},{... | collective-permute-start | bytes 153608 | tf_op jit(solution)/shard_map/ppermute | solution.py:357
  10.7 0.0 copy-done.3
  10.7 0.0 copy-done.2
  10.7 0.0 copy-done.5
  10.7 0.0 copy-done.4
  10.7 1.9 %own_stats.1.own_ref = f32[16,8,256]{2,1,0:T(8,128)S(1)} custom-call(bf16[256,2048]{1,0:T(8,128)(2,1)S(1)} %copy-done.2, bf16[256,2048]{1,0:T(8,128)(2,1)S(1)} %copy-done.3, bf16[256,256]{1,0:T(8,128)(2,1)S(1)} %copy-done.4, bf16[256,256]{1,0:T(8,128)(2,1)S(1)} %copy-done.5), custom_call_target="tpu_custom_call" | custom-call | flops 2684354560 | bytes 2097152 | tf_op jit(solution)/shard_map/own_stats/pallas_call | solution.py:145
  12.6 0.1 collective-permute-done.3
  12.7 1.7 %collective-permute-done.2 = bf16[50,512]{1,0:T(8,128)(2,1)S(1)} collective-permute-done((bf16[50,512]{1,0:T(8,128)(2,1)S(1)}, bf16[50,512]{1,0:T(8,128)(2,1)S(1)}, u32[]{:S(2)}, u32[]{:S(2)}) %collective-permute-start.2) | collective-permute-done | bytes 51232 | tf_op jit(solution)/shard_map/ppermute | solution.py:357
  14.4 1.6 %collective-permute-start.4 = (bf16[100,512]{1,0:T(8,128)(2,1)S(1)}, bf16[100,512]{1,0:T(8,128)(2,1)S(1)}, u32[]{:S(2)}, u32[]{:S(2)}) collective-permute-start(bf16[100,512]{1,0:T(8,128)(2,1)S(1)} %pad_maximum_fusion.5), channel_id=1, source_target_pairs={{0,4},{4,0},{8,12},{12,8},{16,20},{20,16},{24,28},{28,24},{1,5},{5... | collective-permute-start | bytes 307208 | tf_op jit(solution)/shard_map/ppermute | solution.py:357
  16.0 0.0 collective-permute-done
  16.0 1.1 %collective-permute-start.1 = (bf16[100,512]{1,0:T(8,128)(2,1)S(1)}, bf16[100,512]{1,0:T(8,128)(2,1)S(1)}, u32[]{:S(2)}, u32[]{:S(2)}) collective-permute-start(bf16[100,512]{1,0:T(8,128)(2,1)S(1)} %pad_maximum_fusion.4), channel_id=1, source_target_pairs={{0,4},{4,0},{8,12},{12,8},{16,20},{20,16},{24,28},{28,24},{1,5},{5... | collective-permute-start | bytes 307208 | tf_op jit(solution)/shard_map/ppermute | solution.py:357
  17.1 1.4 %even_stats.1 = (f32[16,8,256]{2,1,0:T(8,128)S(1)}, f32[160,256]{1,0:T(8,128)S(1)}, f32[208,256]{1,0:T(8,128)S(1)}) custom-call(s32[1]{0:T(128)} %bitcast.seg_ref, bf16[256,2048]{1,0:T(8,128)(2,1)S(1)} %copy-done.2, bf16[256,2048]{1,0:T(8,128)(2,1)S(1)} %copy-done.3, bf16[150,512]{1,0:T(8,128)(2,1)S(1)} %pad_maximum_fusion.1.even_ref.slots_ref, ...), custom_call_target="tpu_custom_call" | custom-call | flops 1677721600 | bytes 2097152 | tf_op jit(solution)/shard_map/even_stats/pallas_call | solution.py:187
  18.5 0.8 %collective-permute-done.4 = bf16[100,512]{1,0:T(8,128)(2,1)S(1)} collective-permute-done((bf16[100,512]{1,0:T(8,128)(2,1)S(1)}, bf16[100,512]{1,0:T(8,128)(2,1)S(1)}, u32[]{:S(2)}, u32[]{:S(2)}) %collective-permute-start.4) | collective-permute-done | bytes 102432 | tf_op jit(solution)/shard_map/ppermute | solution.py:357
  19.3 1.5 %collective-permute-done.1 = bf16[100,512]{1,0:T(8,128)(2,1)S(1)} collective-permute-done((bf16[100,512]{1,0:T(8,128)(2,1)S(1)}, bf16[100,512]{1,0:T(8,128)(2,1)S(1)}, u32[]{:S(2)}, u32[]{:S(2)}) %collective-permute-start.1) | collective-permute-done | bytes 102432 | tf_op jit(solution)/shard_map/ppermute | solution.py:357
  20.8 3.2 %odd_slots.1 = (bf16[16,208,256]{2,1,0:T(8,128)(2,1)S(1)}, f32[16,8,256]{2,1,0:T(8,128)S(1)}, bf16[208,256]{1,0:T(8,128)(2,1)S(1)}, bf16[200,512]{1,0:T(8,128)(2,1)S(1)}) custom-call(bf16[256,2048]{1,0:T(8,128)(2,1)S(1)} %copy-done.2, bf16[256,2048]{1,0:T(8,128)(2,1)S(1)} %copy-done.3, bf16[200,512]{1,0:T(8,128)(2,1)S(1)} %pad_maximum_fusion.slots_ref, ...), custom_call_target="tpu_custom_call" | custom-call | flops 3271557120 | bytes 2097152 | tf_op jit(solution)/shard_map/odd_slots/pallas_call | solution.py:255
  24.0 1.1 %collective-permute-start.5 = (bf16[200,512]{1,0:T(8,128)(2,1)S(1)}, bf16[200,512]{1,0:T(8,128)(2,1)S(1)}, u32[]{:S(2)}, u32[]{:S(2)}) collective-permute-start(bf16[200,512]{1,0:T(8,128)(2,1)S(1)} %get-tuple-element.37), channel_id=1, source_target_pairs={{0,4},{4,0},{8,12},{12,8},{16,20},{20,16},{24,28},{28,24},{1,5},{5... | collective-permute-start | bytes 614408 | tf_op jit(solution)/shard_map/ppermute | solution.py:357
  25.2 1.9 %even_slots.1 = (bf16[16,160,256]{2,1,0:T(8,128)(2,1)S(1)}, f32[8,128]{1,0:T(8,128)}, bf16[160,256]{1,0:T(8,128)(2,1)S(1)}, f32[150,512]{1,0:T(8,128)S(1)}) custom-call(bf16[256,2048]{1,0:T(8,128)(2,1)S(1)} %copy-done.2, bf16[256,2048]{1,0:T(8,128)(2,1)S(1)} %copy-done.3, bf16[150,512]{1,0:T(8,128)(2,1)S(1)} %pad_maximum_fusion.1.even_ref.slots_ref, ...), custom_call_target="tpu_custom_call" | custom-call | flops 2516582400 | bytes 2097152 | tf_op jit(solution)/shard_map/even_slots/pallas_call | solution.py:255
  27.0 2.8 %collective-permute-done.5 = bf16[200,512]{1,0:T(8,128)(2,1)S(1)} collective-permute-done((bf16[200,512]{1,0:T(8,128)(2,1)S(1)}, bf16[200,512]{1,0:T(8,128)(2,1)S(1)}, u32[]{:S(2)}, u32[]{:S(2)}) %collective-permute-start.5) | collective-permute-done | bytes 204832 | tf_op jit(solution)/shard_map/ppermute | solution.py:357
  29.9 0.1 fusion.3
  30.0 2.4 %collective-permute-start.8 = (bf16[50,512]{1,0:T(8,128)(2,1)S(1)}, bf16[50,512]{1,0:T(8,128)(2,1)S(1)}, u32[]{:S(2)}, u32[]{:S(2)}) collective-permute-start(bf16[50,512]{1,0:T(8,128)(2,1)S(1)} %get-tuple-element.52), channel_id=1, source_target_pairs={{0,24},{4,28},{8,16},{12,20},{16,8},{20,12},{24,0},{28,4},{1,25},{... | collective-permute-start | bytes 153608 | tf_op jit(solution)/shard_map/ppermute | solution.py:357
  32.4 0.3 collective-permute-start.7
  32.7 1.8 %collective-permute-start.6 = (bf16[50,512]{1,0:T(8,128)(2,1)S(1)}, bf16[50,512]{1,0:T(8,128)(2,1)S(1)}, u32[]{:S(2)}, u32[]{:S(2)}) collective-permute-start(bf16[50,512]{1,0:T(8,128)(2,1)S(1)} %get-tuple-element.54), channel_id=1, source_target_pairs={{0,8},{4,12},{8,0},{12,4},{16,24},{20,28},{24,16},{28,20},{1,9},{5... | collective-permute-start | bytes 153608 | tf_op jit(solution)/shard_map/ppermute | solution.py:357
  34.4 0.0 copy-start
  34.4 0.0 copy-start.1
  34.5 3.4 %own_grads.2 = (bf16[256,2048]{1,0:T(8,128)(2,1)}, bf16[256,128]{1,0:T(8,128)(2,1)S(1)}, bf16[256,128]{1,0:T(8,128)(2,1)S(1)}) custom-call(bf16[256,2048]{1,0:T(8,128)(2,1)S(1)} %copy-done.2, bf16[256,2048]{1,0:T(8,128)(2,1)S(1)} %copy-done.3, bf16[256,256]{1,0:T(8,128)(2,1)S(1)} %copy-done.4, bf16[256,256]{1,0:T(8,128)(2,1)S(1)} %copy-done.5, ...), custom_call_target="tpu_custom_call" | custom-call | flops 2684354560 | bytes 2097152 | tf_op jit(solution)/shard_map/own_grads/pallas_call | solution.py:312
  37.9 0.0 collective-permute-done.8
  37.9 0.0 collective-permute-done.7
  37.9 0.0 collective-permute-done.6
  38.0 0.0 copy-done
  38.0 0.0 copy-done.1
  38.0 0.8 %state_part.4 = bf16[50,2048]{1,0:T(8,128)(2,1)S(1)} custom-call(s32[1]{0:T(128)} %bitcast.1.mine_ref, bf16[50,512]{1,0:T(8,128)(2,1)S(1)} %fusion.2.emitted_ref, bf16[8192,256]{1,0:T(8,128)(2,1)S(1)} %copy-done, bf16[8192,256]{1,0:T(8,128)(2,1)S(1)} %copy-done.1), custom_call_target="tpu_custom_call" | custom-call | flops 104857600 | bytes 2097152 | tf_op jit(solution)/shard_map/state_part/pallas_call | solution.py:345
  38.7 0.1 collective-permute-start.9
  38.8 0.8 %state_part.3 = bf16[50,2048]{1,0:T(8,128)(2,1)S(1)} custom-call(s32[1]{0:T(128)} %bitcast.1.mine_ref, bf16[50,512]{1,0:T(8,128)(2,1)S(1)} %fusion.2.emitted_ref, bf16[8192,256]{1,0:T(8,128)(2,1)S(1)} %copy-done, bf16[8192,256]{1,0:T(8,128)(2,1)S(1)} %copy-done.1), custom_call_target="tpu_custom_call" | custom-call | flops 104857600 | bytes 2097152 | tf_op jit(solution)/shard_map/state_part/pallas_call | solution.py:345
  39.6 0.7 %collective-permute-done.9 = bf16[50,2048]{1,0:T(8,128)(2,1)S(1)} collective-permute-done((bf16[50,2048]{1,0:T(8,128)(2,1)S(1)}, bf16[50,2048]{1,0:T(8,128)(2,1)S(1)}, u32[]{:S(2)}, u32[]{:S(2)}) %collective-permute-start.9) | collective-permute-done | bytes 204832 | tf_op jit(solution)/shard_map/ppermute | solution.py:357
  40.3 0.1 add_convert_fusion.1
  40.4 1.6 %collective-permute-start.11 = (bf16[50,2048]{1,0:T(8,128)(2,1)S(1)}, bf16[50,2048]{1,0:T(8,128)(2,1)S(1)}, u32[]{:S(2)}, u32[]{:S(2)}) collective-permute-start(bf16[50,2048]{1,0:T(8,128)(2,1)S(1)} %add_convert_fusion.1), channel_id=1, source_target_pairs={{0,2},{1,3},{2,0},{3,1},{4,6},{5,7},{6,4},{7,5},{8,10},{9,11},{10,... | collective-permute-start | bytes 614408 | tf_op jit(solution)/shard_map/ppermute | solution.py:357
  41.9 1.4 %state_part.5 = (bf16[50,2048]{1,0:T(8,128)(2,1)S(1)}, bf16[50,2048]{1,0:T(8,128)(2,1)S(1)}) custom-call(s32[1]{0:T(128)} %bitcast.1.mine_ref, bf16[50,512]{1,0:T(8,128)(2,1)S(1)} %fusion.2.emitted_ref, bf16[8192,256]{1,0:T(8,128)(2,1)S(1)} %copy-done, bf16[8192,256]{1,0:T(8,128)(2,1)S(1)} %copy-done.1), custom_call_target="tpu_custom_call" | custom-call | flops 209715200 | bytes 4194304 | tf_op jit(solution)/shard_map/state_part/pallas_call | solution.py:345
  43.3 0.0 copy-start.6
  43.3 0.1 collective-permute-start.10
  43.4 3.3 %own_grads.3 = (bf16[256,2048]{1,0:T(8,128)(2,1)}, bf16[256,128]{1,0:T(8,128)(2,1)S(1)}, bf16[256,128]{1,0:T(8,128)(2,1)S(1)}) custom-call(bf16[256,2048]{1,0:T(8,128)(2,1)S(1)} %copy-done.2, bf16[256,2048]{1,0:T(8,128)(2,1)S(1)} %copy-done.3, bf16[256,256]{1,0:T(8,128)(2,1)S(1)} %copy-done.4, ...), custom_call_target="tpu_custom_call", output_to_operand_aliasing={{0}: (9, {})} | custom-call | flops 2684354560 | bytes 2097152 | tf_op jit(solution)/shard_map/own_grads/pallas_call | solution.py:312
  46.7 0.7 %pad_maximum_fusion.2 = (bf16[256,256]{1,0:T(8,128)(2,1)}, bf16[256,256]{1,0:T(8,128)(2,1)}) fusion(bf16[256,128]{1,0:T(8,128)(2,1)S(1)} %get-tuple-element.42, bf16[256,128]{1,0:T(8,128)(2,1)S(1)} %get-tuple-element.41, bf16[256,128]{1,0:T(8,128)(2,1)S(1)} %get-tuple-element.44, bf16[256,128]{1,0:T(8,128)(2,1)S(1)} %get-tuple-element.43), kind=kLoop, calls=%fused_computation.4 | loop fusion | flops 524288 | bytes 524288 | tf_op jit(solution)/shard_map/concatenate | solution.py:440
  47.4 0.7 %collective-permute-done.11 = bf16[50,2048]{1,0:T(8,128)(2,1)S(1)} collective-permute-done((bf16[50,2048]{1,0:T(8,128)(2,1)S(1)}, bf16[50,2048]{1,0:T(8,128)(2,1)S(1)}, u32[]{:S(2)}, u32[]{:S(2)}) %collective-permute-start.11) | collective-permute-done | bytes 204832 | tf_op jit(solution)/shard_map/ppermute | solution.py:357
  48.1 0.0 collective-permute-done.10
  48.1 0.0 copy-done.6
  48.1 0.8 %add_convert_fusion = bf16[50,2048]{1,0:T(8,128)(2,1)} fusion(bf16[50,2048]{1,0:T(8,128)(2,1)S(1)} %copy-done.6, bf16[50,2048]{1,0:T(8,128)(2,1)S(1)} %collective-permute-done.11, bf16[50,2048]{1,0:T(8,128)(2,1)S(1)} %collective-permute-done.10, bf16[50,2048]{1,0:T(8,128)(2,1)S(1)} %get-tuple-element.49), kind=kLoop, calls=%fused_computation | loop fusion | flops 819200 | bytes 1024000 | tf_op jit(solution)/shard_map/convert_element_type | solution.py:433
  (6 shorter events, 0.2 us)
Async XLA Ops:
  0.6 10.1 %copy-start.3 = (bf16[256,2048]{1,0:T(8,128)(2,1)S(1)}, bf16[256,2048]{1,0:T(8,128)(2,1)}, u32[]{:S(2)}) copy-start(bf16[256,2048]{1,0:T(8,128)(2,1)} %g_ref.11) | copy-start | bytes 3145732
  0.6 10.1 %copy-start.2 = (bf16[256,2048]{1,0:T(8,128)(2,1)S(1)}, bf16[256,2048]{1,0:T(8,128)(2,1)}, u32[]{:S(2)}) copy-start(bf16[256,2048]{1,0:T(8,128)(2,1)} %q_ref.11) | copy-start | bytes 3145732
  0.7 10.1 %copy-start.5 = (bf16[256,256]{1,0:T(8,128)(2,1)S(1)}, bf16[256,256]{1,0:T(8,128)(2,1)}, u32[]{:S(2)}) copy-start(bf16[256,256]{1,0:T(8,128)(2,1)} %v_ref.5) | copy-start | bytes 393220
  0.7 10.0 %copy-start.4 = (bf16[256,256]{1,0:T(8,128)(2,1)S(1)}, bf16[256,256]{1,0:T(8,128)(2,1)}, u32[]{:S(2)}) copy-start(bf16[256,256]{1,0:T(8,128)(2,1)} %k_ref.5) | copy-start | bytes 393220
  4.9 7.7 %collective-permute-start.3 = (bf16[50,512]{1,0:T(8,128)(2,1)S(1)}, bf16[50,512]{1,0:T(8,128)(2,1)S(1)}, u32[]{:S(2)}, u32[]{:S(2)}) collective-permute-start(bf16[50,512]{1,0:T(8,128)(2,1)S(1)} %project.1), channel_id=1, source_target_pairs={{0,24},{4,28},{8,16},{12,20},{16,8},{20,12},{24,0},{28,4},{1,25},{... | collective-permute-start | bytes 153608 | tf_op jit(solution)/shard_map/ppermute | solution.py:357
  10.1 4.3 %collective-permute-start.2 = (bf16[50,512]{1,0:T(8,128)(2,1)S(1)}, bf16[50,512]{1,0:T(8,128)(2,1)S(1)}, u32[]{:S(2)}, u32[]{:S(2)}) collective-permute-start(bf16[50,512]{1,0:T(8,128)(2,1)S(1)} %project.1), channel_id=1, source_target_pairs={{0,8},{4,12},{8,0},{12,4},{16,24},{20,28},{24,16},{28,20},{1,9},{5... | collective-permute-start | bytes 153608 | tf_op jit(solution)/shard_map/ppermute | solution.py:357
  10.1 6.0 %collective-permute-start = (bf16[50,512]{1,0:T(8,128)(2,1)S(1)}, bf16[50,512]{1,0:T(8,128)(2,1)S(1)}, u32[]{:S(2)}, u32[]{:S(2)}) collective-permute-start(bf16[50,512]{1,0:T(8,128)(2,1)S(1)} %project.1), channel_id=1, source_target_pairs={{0,16},{4,20},{8,24},{12,28},{16,0},{20,4},{24,8},{28,12},{1,17},{... | collective-permute-start | bytes 153608 | tf_op jit(solution)/shard_map/ppermute | solution.py:357
  14.4 4.9 %collective-permute-start.4 = (bf16[100,512]{1,0:T(8,128)(2,1)S(1)}, bf16[100,512]{1,0:T(8,128)(2,1)S(1)}, u32[]{:S(2)}, u32[]{:S(2)}) collective-permute-start(bf16[100,512]{1,0:T(8,128)(2,1)S(1)} %pad_maximum_fusion.5), channel_id=1, source_target_pairs={{0,4},{4,0},{8,12},{12,8},{16,20},{20,16},{24,28},{28,24},{1,5},{5... | collective-permute-start | bytes 307208 | tf_op jit(solution)/shard_map/ppermute | solution.py:357
  16.0 4.8 %collective-permute-start.1 = (bf16[100,512]{1,0:T(8,128)(2,1)S(1)}, bf16[100,512]{1,0:T(8,128)(2,1)S(1)}, u32[]{:S(2)}, u32[]{:S(2)}) collective-permute-start(bf16[100,512]{1,0:T(8,128)(2,1)S(1)} %pad_maximum_fusion.4), channel_id=1, source_target_pairs={{0,4},{4,0},{8,12},{12,8},{16,20},{20,16},{24,28},{28,24},{1,5},{5... | collective-permute-start | bytes 307208 | tf_op jit(solution)/shard_map/ppermute | solution.py:357
  24.0 5.8 %collective-permute-start.5 = (bf16[200,512]{1,0:T(8,128)(2,1)S(1)}, bf16[200,512]{1,0:T(8,128)(2,1)S(1)}, u32[]{:S(2)}, u32[]{:S(2)}) collective-permute-start(bf16[200,512]{1,0:T(8,128)(2,1)S(1)} %get-tuple-element.37), channel_id=1, source_target_pairs={{0,4},{4,0},{8,12},{12,8},{16,20},{20,16},{24,28},{28,24},{1,5},{5... | collective-permute-start | bytes 614408 | tf_op jit(solution)/shard_map/ppermute | solution.py:357
  30.0 7.9 %collective-permute-start.8 = (bf16[50,512]{1,0:T(8,128)(2,1)S(1)}, bf16[50,512]{1,0:T(8,128)(2,1)S(1)}, u32[]{:S(2)}, u32[]{:S(2)}) collective-permute-start(bf16[50,512]{1,0:T(8,128)(2,1)S(1)} %get-tuple-element.52), channel_id=1, source_target_pairs={{0,24},{4,28},{8,16},{12,20},{16,8},{20,12},{24,0},{28,4},{1,25},{... | collective-permute-start | bytes 153608 | tf_op jit(solution)/shard_map/ppermute | solution.py:357
  32.4 5.5 %collective-permute-start.7 = (bf16[50,512]{1,0:T(8,128)(2,1)S(1)}, bf16[50,512]{1,0:T(8,128)(2,1)S(1)}, u32[]{:S(2)}, u32[]{:S(2)}) collective-permute-start(bf16[50,512]{1,0:T(8,128)(2,1)S(1)} %get-tuple-element.53), channel_id=1, source_target_pairs={{0,16},{4,20},{8,24},{12,28},{16,0},{20,4},{24,8},{28,12},{1,17},{... | collective-permute-start | bytes 153608 | tf_op jit(solution)/shard_map/ppermute | solution.py:357
  32.7 5.2 %collective-permute-start.6 = (bf16[50,512]{1,0:T(8,128)(2,1)S(1)}, bf16[50,512]{1,0:T(8,128)(2,1)S(1)}, u32[]{:S(2)}, u32[]{:S(2)}) collective-permute-start(bf16[50,512]{1,0:T(8,128)(2,1)S(1)} %get-tuple-element.54), channel_id=1, source_target_pairs={{0,8},{4,12},{8,0},{12,4},{16,24},{20,28},{24,16},{28,20},{1,9},{5... | collective-permute-start | bytes 153608 | tf_op jit(solution)/shard_map/ppermute | solution.py:357
  34.4 3.5 %copy-start = (bf16[8192,256]{1,0:T(8,128)(2,1)S(1)}, bf16[8192,256]{1,0:T(8,128)(2,1)}, u32[]{:S(2)}) copy-start(bf16[8192,256]{1,0:T(8,128)(2,1)} %wk_ref.5) | copy-start | bytes 12582916
  34.4 3.5 %copy-start.1 = (bf16[8192,256]{1,0:T(8,128)(2,1)S(1)}, bf16[8192,256]{1,0:T(8,128)(2,1)}, u32[]{:S(2)}) copy-start(bf16[8192,256]{1,0:T(8,128)(2,1)} %wv_ref.5) | copy-start | bytes 12582916
  38.7 1.6 %collective-permute-start.9 = (bf16[50,2048]{1,0:T(8,128)(2,1)S(1)}, bf16[50,2048]{1,0:T(8,128)(2,1)S(1)}, u32[]{:S(2)}, u32[]{:S(2)}) collective-permute-start(bf16[50,2048]{1,0:T(8,128)(2,1)S(1)} %state_part.4), channel_id=1, source_target_pairs={{0,1},{1,0},{2,3},{3,2},{4,5},{5,4},{6,7},{7,6},{8,9},{9,8},{10,11... | collective-permute-start | bytes 614408 | tf_op jit(solution)/shard_map/ppermute | solution.py:357
  40.4 7.7 %collective-permute-start.11 = (bf16[50,2048]{1,0:T(8,128)(2,1)S(1)}, bf16[50,2048]{1,0:T(8,128)(2,1)S(1)}, u32[]{:S(2)}, u32[]{:S(2)}) collective-permute-start(bf16[50,2048]{1,0:T(8,128)(2,1)S(1)} %add_convert_fusion.1), channel_id=1, source_target_pairs={{0,2},{1,3},{2,0},{3,1},{4,6},{5,7},{6,4},{7,5},{8,10},{9,11},{10,... | collective-permute-start | bytes 614408 | tf_op jit(solution)/shard_map/ppermute | solution.py:357
  43.3 4.8 %copy-start.6 = (bf16[50,2048]{1,0:T(8,128)(2,1)S(1)}, bf16[50,2048]{1,0:T(8,128)(2,1)}, u32[]{:S(2)}) copy-start(bf16[50,2048]{1,0:T(8,128)(2,1)} %param.15) | copy-start | bytes 614404
  43.3 4.7 %collective-permute-start.10 = (bf16[50,2048]{1,0:T(8,128)(2,1)S(1)}, bf16[50,2048]{1,0:T(8,128)(2,1)S(1)}, u32[]{:S(2)}, u32[]{:S(2)}) collective-permute-start(bf16[50,2048]{1,0:T(8,128)(2,1)S(1)} %get-tuple-element.50), channel_id=1, source_target_pairs={{0,1},{1,0},{2,3},{3,2},{4,5},{5,4},{6,7},{7,6},{8,9},{9,8},{10,11... | collective-permute-start | bytes 614408 | tf_op jit(solution)/shard_map/ppermute | solution.py:357

commit v5 on v4

--- a/solution.py
+++ b/solution.py
@@ -270,14 +270,14 @@
 
 
 def own_grads_kernel(
-    kv, q_ref, g_ref, k_ref, v_ref, ok_ref, ek_ref, ods_ref, eds_ref, stats_ref, *rest
+    heads, last, q_ref, g_ref, k_ref, v_ref, ok_ref, ek_ref, ods_ref, eds_ref, stats_ref, *rest
 ):
-    dq_out, dk_ref, dv_ref, bias_ref, dq_ref, sem = rest[-6:]
+    *earlier, dq_out, dk_ref, dv_ref, bias_ref, dq_ref, sem = rest
+    kv = heads[0] // GROUP
     bias_ref[...] = causal_bias(bias_ref.shape[0])
     keys = k_ref[:, lanes(kv)]
     values = v_ref[:, lanes(kv)]
     keys_t = jnp.concatenate([ok_ref[:, lanes(kv)], ek_ref[:, lanes(kv)], keys], 0).T
-    heads = range(kv * GROUP, (kv + 1) * GROUP)
     all_dscores, all_probs = [], []
     for at, head in enumerate(heads):
         scores = dot(keys, q_ref[:, lanes(head)], LAST) * SCALE2 + bias_ref[...]
@@ -288,42 +288,45 @@
         all_probs.append(probs.astype(BF16))
         dquery = dot(keys_t, jnp.concatenate([ods_ref[head], eds_ref[head], dscores], 0))
         dq_ref[:, lanes(at)] = (dquery * SCALE).T.astype(BF16)
-    columns = pl.ds(kv * GROUP * HD, GROUP * HD)
+    columns = pl.ds(heads[0] * HD, len(heads) * HD)
     copy = pltpu.make_async_copy(dq_ref, dq_out.at[:, columns], sem)
     copy.start()
     queries = jnp.concatenate([q_ref[:, lanes(head)] for head in heads], 0)
     grads = jnp.concatenate([g_ref[:, lanes(head)] for head in heads], 0)
-    dk_ref[...] = (dot(jnp.concatenate(all_dscores, 1), queries) * SCALE).astype(BF16)
-    dv_ref[...] = dot(jnp.concatenate(all_probs, 1), grads).astype(BF16)
+    key_part = dot(jnp.concatenate(all_dscores, 1), queries)
+    value_part = dot(jnp.concatenate(all_probs, 1), grads)
+    if len(earlier) > 1:
+        key_part = key_part + earlier[1][...]
+        value_part = value_part + earlier[2][...]
+    if last:
+        key_part = key_part * SCALE
+    dk_ref[...] = key_part.astype(dk_ref.dtype)
+    dv_ref[...] = value_part.astype(dv_ref.dtype)
     copy.wait()
 
 
-def own_grads(kv, operands, earlier):
+def own_grads(heads, last, operands, earlier):
     queries, odd_keys, even_keys = operands[0], operands[4], operands[5]
     rows = queries.shape[0]
-    heads = queries.shape[1] // HD
     padded = odd_keys.shape[0] + even_keys.shape[0]
-    in_specs = [VMEM] * len(operands)
-    aliases = {}
-    if earlier is not None:
-        aliases = {len(operands): 0}
-        operands = [*operands, earlier]
-        in_specs.append(HBM)
-    return pl.pallas_call(
-        functools.partial(own_grads_kernel, kv),
+    in_specs = [VMEM] * len(operands) + [HBM, VMEM, VMEM][: len(earlier)]
+    aliases = {len(operands): 0} if earlier else {}
+    kind = BF16 if last else F32
+    return pl.pallas_call(
+        functools.partial(own_grads_kernel, heads, last),
         name="own_grads",
         in_specs=in_specs,
         out_specs=[HBM, VMEM, VMEM],
-        out_shape=[shape((rows, heads * HD)), shape((rows, HD)), shape((rows, HD))],
+        out_shape=[shape(queries.shape), shape((rows, HD), kind), shape((rows, HD), kind)],
         input_output_aliases=aliases,
         scratch_shapes=[
             pltpu.VMEM((rows, rows), F32),
-            pltpu.VMEM((rows, GROUP * HD), BF16),
+            pltpu.VMEM((rows, len(heads) * HD), BF16),
             pltpu.SemaphoreType.DMA,
         ],
         compiler_params=params(16 if padded <= 512 else 32),
-        cost_estimate=cost(20 * heads * rows * rows * HD, 4 * rows * heads * HD),
-    )(*operands)
+        cost_estimate=cost(20 * len(heads) * rows * rows * HD, 4 * rows * len(heads) * HD),
+    )(*operands, *earlier)
 
 
 def state_kernel(chunk, group, mine_ref, emitted_ref, wk_ref, wv_ref, *out_refs):
@@ -392,21 +395,24 @@
         True, queries, out_grad, odd, before, odd_bias
     )
 
-    got = exchange(odd_grad, "seg", n_seg, 1).astype(F32)
+    got = exchange(odd_grad, "seg", n_seg, 1)
     even_ds, _, even_keys, even_grad = slots_part(
         False, queries, out_grad, even, stats, even_bias
     )
+    operands = [
+        queries, out_grad, keys_own, values_own, odd_keys, even_keys, odd_ds, even_ds, stats
+    ]
+    begun = own_grads(range(GROUP // 2), False, operands, [])
+    got, even_grad, begun = lax.optimization_barrier((got, even_grad, begun))
     blocks = {}
     for j in sorted(evens, key=lambda j: (j.bit_count(), -j)):
         at = evens.index(j) * count
-        block = (even_grad[at : at + count] + got[at + count : at + 2 * count]).astype(BF16)
+        block = got[at + count : at + 2 * count].astype(F32) + even_grad[at : at + count]
+        block = block.astype(BF16)
         blocks[j] = exchange(block, "seg", n_seg, j)
-    operands = [
-        queries, out_grad, keys_own, values_own, odd_keys, even_keys, odd_ds, even_ds, stats
-    ]
-    query_grad, *first = own_grads(0, operands, None)
+    query_grad, *first = own_grads(range(GROUP // 2, GROUP), True, operands, begun)
     blocks, query_grad = lax.optimization_barrier((blocks, query_grad))
-    emitted = got[:count]
+    emitted = got[:count].astype(F32)
     for block in blocks.values():
         emitted = emitted + block.astype(F32)
     emitted = emitted.astype(BF16)
@@ -434,7 +440,9 @@
 
     key_blocks, value_blocks = [first[0]], [first[1]]
     for kv in range(1, kv_local):
-        query_grad, key_block, value_block = own_grads(kv, operands, query_grad)
+        query_grad, key_block, value_block = own_grads(
+            range(kv * GROUP, (kv + 1) * GROUP), True, operands, [query_grad]
+        )
         key_blocks.append(key_block)
         value_blocks.append(value_block)
     key_grad = jnp.concatenate(key_blocks, 1)

time: 49 us -> 48.3 us (0.986)
  waiting for transfers between devices: 8.28 us -> 7.58 us
    ppermute x12, waiting for transfers between devices: 8.28 us -> 7.58 us  [exchange(): return lax.ppermute(block, axis, [(i, i ^ key) for i in range(size)])]
    pallas_call x2 -> x3, Pallas kernels: 6.71 us -> 7.31 us  [own_grads(): pl.pallas_call(functools.partial(own_grads_kernel, heads, last), name='ow...]
  transfers between devices with their start and end apart: 12 -> 12, of which waited for: 7 -> 8; matrix products, arithmetic and copies ran while one was open for 2% -> 2% of each run, Pallas kernels for 28% -> 29%
where the time goes in v5:
time: 48.3 us; the launch traced here: 48.2 us
  Pallas kernels  22.2 us (46%)
  starting transfers between devices  15.7 us (33%)
  waiting for transfers between devices  7.58 us (16%)
  other arithmetic  1.82 us (4%)
  between operations  0.83 us (2%)
    ppermute x12, starting transfers between devices, exchange(): return lax.ppermute(block, axis, [(i, i ^ key) for i in range(size)])  15.7 us
    ppermute x12, waiting for transfers between devices, exchange(): return lax.ppermute(block, axis, [(i, i ^ key) for i in range(size)])  7.58 us
    pallas_call x3, Pallas kernels, own_grads(): pl.pallas_call(functools.partial(own_grads_kernel, heads, last), name='ow...  7.31 us
    pallas_call x2, Pallas kernels, slots_part(): pl.pallas_call(functools.partial(slots_kernel, last), name='odd_slots' if...  4.79 us
    pallas_call x1, Pallas kernels, project(): pl.pallas_call(functools.partial(project_kernel, pieces), name='project',...  4.26 us
    pallas_call x3, Pallas kernels, state_part(): pl.pallas_call(functools.partial(state_kernel, chunk, group), name='state...  2.88 us
    pallas_call x1, Pallas kernels, own_stats(): pl.pallas_call(own_stats_kernel, name='own_stats', in_specs=[VMEM] * 4, o...  1.68 us
    pallas_call x1, Pallas kernels, even_stats(): pl.pallas_call(functools.partial(even_stats_kernel, count, evens, odds),...  1.3 us
  transfers between devices with their start and end apart: 12, of which 8 were waited for; matrix products, arithmetic and copies ran while one was open for 2% of the time, Pallas kernels for 29%

profile of v5, /device:TPU:0, one launch (start us, length us, event | category | flops | bytes accessed | tf_op | source)
XLA Modules:
  0.0 48.2 jit_solution(16306718353672861337)
XLA Ops:
  0.6 0.0 copy-start.3
  0.6 0.0 copy-start.2
  0.7 0.0 copy-start.5
  0.7 0.0 copy-start.4
  0.7 4.3 %project.1 = bf16[50,512]{1,0:T(8,128)(2,1)S(1)} custom-call(bf16[50,8192]{1,0:T(8,128)(2,1)} %states_hbm.1, bf16[8192,256]{1,0:T(8,128)(2,1)} %wk_ref.5, bf16[8192,256]{1,0:T(8,128)(2,1)} %wv_ref.5), custom_call_target="tpu_custom_call" | custom-call | flops 419430400 | bytes 16777216 | tf_op jit(solution)/shard_map/project/pallas_call | solution.py:86
  4.9 5.1 %collective-permute-start.3 = (bf16[50,512]{1,0:T(8,128)(2,1)S(1)}, bf16[50,512]{1,0:T(8,128)(2,1)S(1)}, u32[]{:S(2)}, u32[]{:S(2)}) collective-permute-start(bf16[50,512]{1,0:T(8,128)(2,1)S(1)} %project.1), channel_id=1, source_target_pairs={{0,24},{4,28},{8,16},{12,20},{16,8},{20,12},{24,0},{28,4},{1,25},{... | collective-permute-start | bytes 153608 | tf_op jit(solution)/shard_map/ppermute | solution.py:360
  10.1 0.0 collective-permute-start.2
  10.1 0.6 %collective-permute-start = (bf16[50,512]{1,0:T(8,128)(2,1)S(1)}, bf16[50,512]{1,0:T(8,128)(2,1)S(1)}, u32[]{:S(2)}, u32[]{:S(2)}) collective-permute-start(bf16[50,512]{1,0:T(8,128)(2,1)S(1)} %project.1), channel_id=1, source_target_pairs={{0,16},{4,20},{8,24},{12,28},{16,0},{20,4},{24,8},{28,12},{1,17},{... | collective-permute-start | bytes 153608 | tf_op jit(solution)/shard_map/ppermute | solution.py:360
  10.7 0.0 copy-done.3
  10.7 0.0 copy-done.2
  10.7 0.0 copy-done.5
  10.7 0.0 copy-done.4
  10.7 1.7 %own_stats.1.own_ref = f32[16,8,256]{2,1,0:T(8,128)S(1)} custom-call(bf16[256,2048]{1,0:T(8,128)(2,1)S(1)} %copy-done.2, bf16[256,2048]{1,0:T(8,128)(2,1)S(1)} %copy-done.3, bf16[256,256]{1,0:T(8,128)(2,1)S(1)} %copy-done.4, bf16[256,256]{1,0:T(8,128)(2,1)S(1)} %copy-done.5), custom_call_target="tpu_custom_call" | custom-call | flops 2684354560 | bytes 2097152 | tf_op jit(solution)/shard_map/own_stats/pallas_call | solution.py:145
  12.4 0.3 collective-permute-done.3
  12.7 1.7 %collective-permute-done.2 = bf16[50,512]{1,0:T(8,128)(2,1)S(1)} collective-permute-done((bf16[50,512]{1,0:T(8,128)(2,1)S(1)}, bf16[50,512]{1,0:T(8,128)(2,1)S(1)}, u32[]{:S(2)}, u32[]{:S(2)}) %collective-permute-start.2) | collective-permute-done | bytes 51232 | tf_op jit(solution)/shard_map/ppermute | solution.py:360
  14.4 1.6 %collective-permute-start.4 = (bf16[100,512]{1,0:T(8,128)(2,1)S(1)}, bf16[100,512]{1,0:T(8,128)(2,1)S(1)}, u32[]{:S(2)}, u32[]{:S(2)}) collective-permute-start(bf16[100,512]{1,0:T(8,128)(2,1)S(1)} %pad_maximum_fusion.5), channel_id=1, source_target_pairs={{0,4},{4,0},{8,12},{12,8},{16,20},{20,16},{24,28},{28,24},{1,5},{5... | collective-permute-start | bytes 307208 | tf_op jit(solution)/shard_map/ppermute | solution.py:360
  16.0 0.0 collective-permute-done
  16.0 1.1 %collective-permute-start.1 = (bf16[100,512]{1,0:T(8,128)(2,1)S(1)}, bf16[100,512]{1,0:T(8,128)(2,1)S(1)}, u32[]{:S(2)}, u32[]{:S(2)}) collective-permute-start(bf16[100,512]{1,0:T(8,128)(2,1)S(1)} %pad_maximum_fusion.4), channel_id=1, source_target_pairs={{0,4},{4,0},{8,12},{12,8},{16,20},{20,16},{24,28},{28,24},{1,5},{5... | collective-permute-start | bytes 307208 | tf_op jit(solution)/shard_map/ppermute | solution.py:360
  17.1 1.3 %even_stats.1 = (f32[16,8,256]{2,1,0:T(8,128)S(1)}, f32[160,256]{1,0:T(8,128)S(1)}, f32[208,256]{1,0:T(8,128)S(1)}) custom-call(s32[1]{0:T(128)} %bitcast.seg_ref, bf16[256,2048]{1,0:T(8,128)(2,1)S(1)} %copy-done.2, bf16[256,2048]{1,0:T(8,128)(2,1)S(1)} %copy-done.3, bf16[150,512]{1,0:T(8,128)(2,1)S(1)} %pad_maximum_fusion.1.even_ref.slots_ref, ...), custom_call_target="tpu_custom_call" | custom-call | flops 1677721600 | bytes 2097152 | tf_op jit(solution)/shard_map/even_stats/pallas_call | solution.py:187
  18.4 0.9 %collective-permute-done.4 = bf16[100,512]{1,0:T(8,128)(2,1)S(1)} collective-permute-done((bf16[100,512]{1,0:T(8,128)(2,1)S(1)}, bf16[100,512]{1,0:T(8,128)(2,1)S(1)}, u32[]{:S(2)}, u32[]{:S(2)}) %collective-permute-start.4) | collective-permute-done | bytes 102432 | tf_op jit(solution)/shard_map/ppermute | solution.py:360
  19.3 1.5 %collective-permute-done.1 = bf16[100,512]{1,0:T(8,128)(2,1)S(1)} collective-permute-done((bf16[100,512]{1,0:T(8,128)(2,1)S(1)}, bf16[100,512]{1,0:T(8,128)(2,1)S(1)}, u32[]{:S(2)}, u32[]{:S(2)}) %collective-permute-start.1) | collective-permute-done | bytes 102432 | tf_op jit(solution)/shard_map/ppermute | solution.py:360
  20.8 3.0 %odd_slots.1 = (bf16[16,208,256]{2,1,0:T(8,128)(2,1)S(1)}, f32[16,8,256]{2,1,0:T(8,128)S(1)}, bf16[208,256]{1,0:T(8,128)(2,1)S(1)}, bf16[200,512]{1,0:T(8,128)(2,1)S(1)}) custom-call(bf16[256,2048]{1,0:T(8,128)(2,1)S(1)} %copy-done.2, bf16[256,2048]{1,0:T(8,128)(2,1)S(1)} %copy-done.3, bf16[200,512]{1,0:T(8,128)(2,1)S(1)} %pad_maximum_fusion.slots_ref, ...), custom_call_target="tpu_custom_call" | custom-call | flops 3271557120 | bytes 2097152 | tf_op jit(solution)/shard_map/odd_slots/pallas_call | solution.py:255
  23.9 1.1 %collective-permute-start.5 = (bf16[200,512]{1,0:T(8,128)(2,1)S(1)}, bf16[200,512]{1,0:T(8,128)(2,1)S(1)}, u32[]{:S(2)}, u32[]{:S(2)}) collective-permute-start(bf16[200,512]{1,0:T(8,128)(2,1)S(1)} %get-tuple-element.44), channel_id=1, source_target_pairs={{0,4},{4,0},{8,12},{12,8},{16,20},{20,16},{24,28},{28,24},{1,5},{5... | collective-permute-start | bytes 614408 | tf_op jit(solution)/shard_map/ppermute | solution.py:360
  25.0 1.8 %even_slots.1 = (bf16[16,160,256]{2,1,0:T(8,128)(2,1)S(1)}, f32[8,128]{1,0:T(8,128)}, bf16[160,256]{1,0:T(8,128)(2,1)S(1)}, f32[150,512]{1,0:T(8,128)S(1)}) custom-call(bf16[256,2048]{1,0:T(8,128)(2,1)S(1)} %copy-done.2, bf16[256,2048]{1,0:T(8,128)(2,1)S(1)} %copy-done.3, bf16[150,512]{1,0:T(8,128)(2,1)S(1)} %pad_maximum_fusion.1.even_ref.slots_ref, ...), custom_call_target="tpu_custom_call" | custom-call | flops 2516582400 | bytes 2097152 | tf_op jit(solution)/shard_map/even_slots/pallas_call | solution.py:255
  26.8 0.0 copy-start.1
  26.8 2.0 %own_grads.3 = (bf16[256,2048]{1,0:T(8,128)(2,1)}, f32[256,128]{1,0:T(8,128)S(1)}, f32[256,128]{1,0:T(8,128)S(1)}) custom-call(bf16[256,2048]{1,0:T(8,128)(2,1)S(1)} %copy-done.2, bf16[256,2048]{1,0:T(8,128)(2,1)S(1)} %copy-done.3, bf16[256,256]{1,0:T(8,128)(2,1)S(1)} %copy-done.4, bf16[256,256]{1,0:T(8,128)(2,1)S(1)} %copy-done.5, ...), custom_call_target="tpu_custom_call" | custom-call | flops 671088640 | bytes 524288 | tf_op jit(solution)/shard_map/own_grads/pallas_call | solution.py:315
  28.7 0.0 copy-start
  28.7 0.9 %collective-permute-done.5 = bf16[200,512]{1,0:T(8,128)(2,1)S(1)} collective-permute-done((bf16[200,512]{1,0:T(8,128)(2,1)S(1)}, bf16[200,512]{1,0:T(8,128)(2,1)S(1)}, u32[]{:S(2)}, u32[]{:S(2)}) %collective-permute-start.5) | collective-permute-done | bytes 204832 | tf_op jit(solution)/shard_map/ppermute | solution.py:360
  29.7 0.1 add_convert_fusion.3
  29.8 2.4 %collective-permute-start.8 = (bf16[50,512]{1,0:T(8,128)(2,1)S(1)}, bf16[50,512]{1,0:T(8,128)(2,1)S(1)}, u32[]{:S(2)}, u32[]{:S(2)}) collective-permute-start(bf16[50,512]{1,0:T(8,128)(2,1)S(1)} %get-tuple-element.68), channel_id=1, source_target_pairs={{0,24},{4,28},{8,16},{12,20},{16,8},{20,12},{24,0},{28,4},{1,25},{... | collective-permute-start | bytes 153608 | tf_op jit(solution)/shard_map/ppermute | solution.py:360
  32.2 0.3 collective-permute-start.7
  32.4 1.8 %collective-permute-start.6 = (bf16[50,512]{1,0:T(8,128)(2,1)S(1)}, bf16[50,512]{1,0:T(8,128)(2,1)S(1)}, u32[]{:S(2)}, u32[]{:S(2)}) collective-permute-start(bf16[50,512]{1,0:T(8,128)(2,1)S(1)} %get-tuple-element.70), channel_id=1, source_target_pairs={{0,8},{4,12},{8,0},{12,4},{16,24},{20,28},{24,16},{28,20},{1,9},{5... | collective-permute-start | bytes 153608 | tf_op jit(solution)/shard_map/ppermute | solution.py:360
  34.2 2.1 %own_grads.4 = (bf16[256,2048]{1,0:T(8,128)(2,1)}, bf16[256,128]{1,0:T(8,128)(2,1)S(1)}, bf16[256,128]{1,0:T(8,128)(2,1)S(1)}) custom-call(bf16[256,2048]{1,0:T(8,128)(2,1)S(1)} %copy-done.2, bf16[256,2048]{1,0:T(8,128)(2,1)S(1)} %copy-done.3, bf16[256,256]{1,0:T(8,128)(2,1)S(1)} %copy-done.4, ...), custom_call_target="tpu_custom_call", output_to_operand_aliasing={{0}: (9, {})} | custom-call | flops 671088640 | bytes 524288 | tf_op jit(solution)/shard_map/own_grads/pallas_call | solution.py:315
  36.4 0.0 collective-permute-done.8
  36.4 0.9 %collective-permute-done.7 = bf16[50,512]{1,0:T(8,128)(2,1)S(1)} collective-permute-done((bf16[50,512]{1,0:T(8,128)(2,1)S(1)}, bf16[50,512]{1,0:T(8,128)(2,1)S(1)}, u32[]{:S(2)}, u32[]{:S(2)}) %collective-permute-start.7) | collective-permute-done | bytes 51232 | tf_op jit(solution)/shard_map/ppermute | solution.py:360
  37.2 0.0 collective-permute-done.6
  37.3 0.0 copy-done.1
  37.3 0.0 copy-done
  37.3 0.8 %state_part.4 = bf16[50,2048]{1,0:T(8,128)(2,1)S(1)} custom-call(s32[1]{0:T(128)} %bitcast.1.mine_ref, bf16[50,512]{1,0:T(8,128)(2,1)S(1)} %add_convert_fusion.2.emitted_ref, bf16[8192,256]{1,0:T(8,128)(2,1)S(1)} %copy-done, bf16[8192,256]{1,0:T(8,128)(2,1)S(1)} %copy-done.1), custom_call_target="tpu_custom_call" | custom-call | flops 104857600 | bytes 2097152 | tf_op jit(solution)/shard_map/state_part/pallas_call | solution.py:348
  38.1 0.1 collective-permute-start.9
  38.1 0.8 %state_part.3 = bf16[50,2048]{1,0:T(8,128)(2,1)S(1)} custom-call(s32[1]{0:T(128)} %bitcast.1.mine_ref, bf16[50,512]{1,0:T(8,128)(2,1)S(1)} %add_convert_fusion.2.emitted_ref, bf16[8192,256]{1,0:T(8,128)(2,1)S(1)} %copy-done, bf16[8192,256]{1,0:T(8,128)(2,1)S(1)} %copy-done.1), custom_call_target="tpu_custom_call" | custom-call | flops 104857600 | bytes 2097152 | tf_op jit(solution)/shard_map/state_part/pallas_call | solution.py:348
  38.9 0.7 %collective-permute-done.9 = bf16[50,2048]{1,0:T(8,128)(2,1)S(1)} collective-permute-done((bf16[50,2048]{1,0:T(8,128)(2,1)S(1)}, bf16[50,2048]{1,0:T(8,128)(2,1)S(1)}, u32[]{:S(2)}, u32[]{:S(2)}) %collective-permute-start.9) | collective-permute-done | bytes 204832 | tf_op jit(solution)/shard_map/ppermute | solution.py:360
  39.6 0.1 add_convert_fusion.1
  39.7 1.6 %collective-permute-start.11 = (bf16[50,2048]{1,0:T(8,128)(2,1)S(1)}, bf16[50,2048]{1,0:T(8,128)(2,1)S(1)}, u32[]{:S(2)}, u32[]{:S(2)}) collective-permute-start(bf16[50,2048]{1,0:T(8,128)(2,1)S(1)} %add_convert_fusion.1), channel_id=1, source_target_pairs={{0,2},{1,3},{2,0},{3,1},{4,6},{5,7},{6,4},{7,5},{8,10},{9,11},{10,... | collective-permute-start | bytes 614408 | tf_op jit(solution)/shard_map/ppermute | solution.py:360
  41.2 1.4 %state_part.5 = (bf16[50,2048]{1,0:T(8,128)(2,1)S(1)}, bf16[50,2048]{1,0:T(8,128)(2,1)S(1)}) custom-call(s32[1]{0:T(128)} %bitcast.1.mine_ref, bf16[50,512]{1,0:T(8,128)(2,1)S(1)} %add_convert_fusion.2.emitted_ref, bf16[8192,256]{1,0:T(8,128)(2,1)S(1)} %copy-done, bf16[8192,256]{1,0:T(8,128)(2,1)S(1)} %copy-done.1), custom_call_target="tpu_custom_call" | custom-call | flops 209715200 | bytes 4194304 | tf_op jit(solution)/shard_map/state_part/pallas_call | solution.py:348
  42.6 0.0 copy-start.6
  42.6 0.1 collective-permute-start.10
  42.7 3.2 %own_grads.5 = (bf16[256,2048]{1,0:T(8,128)(2,1)}, bf16[256,128]{1,0:T(8,128)(2,1)S(1)}, bf16[256,128]{1,0:T(8,128)(2,1)S(1)}) custom-call(bf16[256,2048]{1,0:T(8,128)(2,1)S(1)} %copy-done.2, bf16[256,2048]{1,0:T(8,128)(2,1)S(1)} %copy-done.3, bf16[256,256]{1,0:T(8,128)(2,1)S(1)} %copy-done.4, ...), custom_call_target="tpu_custom_call", output_to_operand_aliasing={{0}: (9, {})} | custom-call | flops 1342177280 | bytes 1048576 | tf_op jit(solution)/shard_map/own_grads/pallas_call | solution.py:315
  45.9 0.7 %pad_maximum_fusion.2 = (bf16[256,256]{1,0:T(8,128)(2,1)}, bf16[256,256]{1,0:T(8,128)(2,1)}) fusion(bf16[256,128]{1,0:T(8,128)(2,1)S(1)} %get-tuple-element.58, bf16[256,128]{1,0:T(8,128)(2,1)S(1)} %get-tuple-element.57, bf16[256,128]{1,0:T(8,128)(2,1)S(1)} %get-tuple-element.60, bf16[256,128]{1,0:T(8,128)(2,1)S(1)} %get-tuple-element.59), kind=kLoop, calls=%fused_computation.4 | loop fusion | flops 524288 | bytes 524288 | tf_op jit(solution)/shard_map/concatenate | solution.py:448
  46.7 0.7 %collective-permute-done.11 = bf16[50,2048]{1,0:T(8,128)(2,1)S(1)} collective-permute-done((bf16[50,2048]{1,0:T(8,128)(2,1)S(1)}, bf16[50,2048]{1,0:T(8,128)(2,1)S(1)}, u32[]{:S(2)}, u32[]{:S(2)}) %collective-permute-start.11) | collective-permute-done | bytes 204832 | tf_op jit(solution)/shard_map/ppermute | solution.py:360
  47.4 0.0 collective-permute-done.10
  47.4 0.0 copy-done.6
  47.4 0.8 %add_convert_fusion = bf16[50,2048]{1,0:T(8,128)(2,1)} fusion(bf16[50,2048]{1,0:T(8,128)(2,1)S(1)} %copy-done.6, bf16[50,2048]{1,0:T(8,128)(2,1)S(1)} %collective-permute-done.11, bf16[50,2048]{1,0:T(8,128)(2,1)S(1)} %collective-permute-done.10, bf16[50,2048]{1,0:T(8,128)(2,1)S(1)} %get-tuple-element.65), kind=kLoop, calls=%fused_computation | loop fusion | flops 819200 | bytes 1024000 | tf_op jit(solution)/shard_map/convert_element_type | solution.py:439
  (5 shorter events, 0.2 us)
Async XLA Ops:
  0.6 10.1 %copy-start.3 = (bf16[256,2048]{1,0:T(8,128)(2,1)S(1)}, bf16[256,2048]{1,0:T(8,128)(2,1)}, u32[]{:S(2)}) copy-start(bf16[256,2048]{1,0:T(8,128)(2,1)} %g_ref.13) | copy-start | bytes 3145732
  0.6 10.1 %copy-start.2 = (bf16[256,2048]{1,0:T(8,128)(2,1)S(1)}, bf16[256,2048]{1,0:T(8,128)(2,1)}, u32[]{:S(2)}) copy-start(bf16[256,2048]{1,0:T(8,128)(2,1)} %q_ref.13) | copy-start | bytes 3145732
  0.7 10.1 %copy-start.5 = (bf16[256,256]{1,0:T(8,128)(2,1)S(1)}, bf16[256,256]{1,0:T(8,128)(2,1)}, u32[]{:S(2)}) copy-start(bf16[256,256]{1,0:T(8,128)(2,1)} %v_ref.7) | copy-start | bytes 393220
  0.7 10.0 %copy-start.4 = (bf16[256,256]{1,0:T(8,128)(2,1)S(1)}, bf16[256,256]{1,0:T(8,128)(2,1)}, u32[]{:S(2)}) copy-start(bf16[256,256]{1,0:T(8,128)(2,1)} %k_ref.7) | copy-start | bytes 393220
  4.9 7.7 %collective-permute-start.3 = (bf16[50,512]{1,0:T(8,128)(2,1)S(1)}, bf16[50,512]{1,0:T(8,128)(2,1)S(1)}, u32[]{:S(2)}, u32[]{:S(2)}) collective-permute-start(bf16[50,512]{1,0:T(8,128)(2,1)S(1)} %project.1), channel_id=1, source_target_pairs={{0,24},{4,28},{8,16},{12,20},{16,8},{20,12},{24,0},{28,4},{1,25},{... | collective-permute-start | bytes 153608 | tf_op jit(solution)/shard_map/ppermute | solution.py:360
  10.1 4.3 %collective-permute-start.2 = (bf16[50,512]{1,0:T(8,128)(2,1)S(1)}, bf16[50,512]{1,0:T(8,128)(2,1)S(1)}, u32[]{:S(2)}, u32[]{:S(2)}) collective-permute-start(bf16[50,512]{1,0:T(8,128)(2,1)S(1)} %project.1), channel_id=1, source_target_pairs={{0,8},{4,12},{8,0},{12,4},{16,24},{20,28},{24,16},{28,20},{1,9},{5... | collective-permute-start | bytes 153608 | tf_op jit(solution)/shard_map/ppermute | solution.py:360
  10.1 6.0 %collective-permute-start = (bf16[50,512]{1,0:T(8,128)(2,1)S(1)}, bf16[50,512]{1,0:T(8,128)(2,1)S(1)}, u32[]{:S(2)}, u32[]{:S(2)}) collective-permute-start(bf16[50,512]{1,0:T(8,128)(2,1)S(1)} %project.1), channel_id=1, source_target_pairs={{0,16},{4,20},{8,24},{12,28},{16,0},{20,4},{24,8},{28,12},{1,17},{... | collective-permute-start | bytes 153608 | tf_op jit(solution)/shard_map/ppermute | solution.py:360
  14.4 4.9 %collective-permute-start.4 = (bf16[100,512]{1,0:T(8,128)(2,1)S(1)}, bf16[100,512]{1,0:T(8,128)(2,1)S(1)}, u32[]{:S(2)}, u32[]{:S(2)}) collective-permute-start(bf16[100,512]{1,0:T(8,128)(2,1)S(1)} %pad_maximum_fusion.5), channel_id=1, source_target_pairs={{0,4},{4,0},{8,12},{12,8},{16,20},{20,16},{24,28},{28,24},{1,5},{5... | collective-permute-start | bytes 307208 | tf_op jit(solution)/shard_map/ppermute | solution.py:360
  16.0 4.8 %collective-permute-start.1 = (bf16[100,512]{1,0:T(8,128)(2,1)S(1)}, bf16[100,512]{1,0:T(8,128)(2,1)S(1)}, u32[]{:S(2)}, u32[]{:S(2)}) collective-permute-start(bf16[100,512]{1,0:T(8,128)(2,1)S(1)} %pad_maximum_fusion.4), channel_id=1, source_target_pairs={{0,4},{4,0},{8,12},{12,8},{16,20},{20,16},{24,28},{28,24},{1,5},{5... | collective-permute-start | bytes 307208 | tf_op jit(solution)/shard_map/ppermute | solution.py:360
  23.9 5.8 %collective-permute-start.5 = (bf16[200,512]{1,0:T(8,128)(2,1)S(1)}, bf16[200,512]{1,0:T(8,128)(2,1)S(1)}, u32[]{:S(2)}, u32[]{:S(2)}) collective-permute-start(bf16[200,512]{1,0:T(8,128)(2,1)S(1)} %get-tuple-element.44), channel_id=1, source_target_pairs={{0,4},{4,0},{8,12},{12,8},{16,20},{20,16},{24,28},{28,24},{1,5},{5... | collective-permute-start | bytes 614408 | tf_op jit(solution)/shard_map/ppermute | solution.py:360
  26.8 10.5 %copy-start.1 = (bf16[8192,256]{1,0:T(8,128)(2,1)S(1)}, bf16[8192,256]{1,0:T(8,128)(2,1)}, u32[]{:S(2)}) copy-start(bf16[8192,256]{1,0:T(8,128)(2,1)} %wv_ref.5) | copy-start | bytes 12582916
  28.7 8.6 %copy-start = (bf16[8192,256]{1,0:T(8,128)(2,1)S(1)}, bf16[8192,256]{1,0:T(8,128)(2,1)}, u32[]{:S(2)}) copy-start(bf16[8192,256]{1,0:T(8,128)(2,1)} %wk_ref.5) | copy-start | bytes 12582916
  29.8 6.6 %collective-permute-start.8 = (bf16[50,512]{1,0:T(8,128)(2,1)S(1)}, bf16[50,512]{1,0:T(8,128)(2,1)S(1)}, u32[]{:S(2)}, u32[]{:S(2)}) collective-permute-start(bf16[50,512]{1,0:T(8,128)(2,1)S(1)} %get-tuple-element.68), channel_id=1, source_target_pairs={{0,24},{4,28},{8,16},{12,20},{16,8},{20,12},{24,0},{28,4},{1,25},{... | collective-permute-start | bytes 153608 | tf_op jit(solution)/shard_map/ppermute | solution.py:360
  32.2 5.1 %collective-permute-start.7 = (bf16[50,512]{1,0:T(8,128)(2,1)S(1)}, bf16[50,512]{1,0:T(8,128)(2,1)S(1)}, u32[]{:S(2)}, u32[]{:S(2)}) collective-permute-start(bf16[50,512]{1,0:T(8,128)(2,1)S(1)} %get-tuple-element.69), channel_id=1, source_target_pairs={{0,16},{4,20},{8,24},{12,28},{16,0},{20,4},{24,8},{28,12},{1,17},{... | collective-permute-start | bytes 153608 | tf_op jit(solution)/shard_map/ppermute | solution.py:360
  32.4 4.8 %collective-permute-start.6 = (bf16[50,512]{1,0:T(8,128)(2,1)S(1)}, bf16[50,512]{1,0:T(8,128)(2,1)S(1)}, u32[]{:S(2)}, u32[]{:S(2)}) collective-permute-start(bf16[50,512]{1,0:T(8,128)(2,1)S(1)} %get-tuple-element.70), channel_id=1, source_target_pairs={{0,8},{4,12},{8,0},{12,4},{16,24},{20,28},{24,16},{28,20},{1,9},{5... | collective-permute-start | bytes 153608 | tf_op jit(solution)/shard_map/ppermute | solution.py:360
  38.1 1.6 %collective-permute-start.9 = (bf16[50,2048]{1,0:T(8,128)(2,1)S(1)}, bf16[50,2048]{1,0:T(8,128)(2,1)S(1)}, u32[]{:S(2)}, u32[]{:S(2)}) collective-permute-start(bf16[50,2048]{1,0:T(8,128)(2,1)S(1)} %state_part.4), channel_id=1, source_target_pairs={{0,1},{1,0},{2,3},{3,2},{4,5},{5,4},{6,7},{7,6},{8,9},{9,8},{10,11... | collective-permute-start | bytes 614408 | tf_op jit(solution)/shard_map/ppermute | solution.py:360
  39.7 7.7 %collective-permute-start.11 = (bf16[50,2048]{1,0:T(8,128)(2,1)S(1)}, bf16[50,2048]{1,0:T(8,128)(2,1)S(1)}, u32[]{:S(2)}, u32[]{:S(2)}) collective-permute-start(bf16[50,2048]{1,0:T(8,128)(2,1)S(1)} %add_convert_fusion.1), channel_id=1, source_target_pairs={{0,2},{1,3},{2,0},{3,1},{4,6},{5,7},{6,4},{7,5},{8,10},{9,11},{10,... | collective-permute-start | bytes 614408 | tf_op jit(solution)/shard_map/ppermute | solution.py:360
  42.6 4.8 %copy-start.6 = (bf16[50,2048]{1,0:T(8,128)(2,1)S(1)}, bf16[50,2048]{1,0:T(8,128)(2,1)}, u32[]{:S(2)}) copy-start(bf16[50,2048]{1,0:T(8,128)(2,1)} %param.15) | copy-start | bytes 614404
  42.6 4.8 %collective-permute-start.10 = (bf16[50,2048]{1,0:T(8,128)(2,1)S(1)}, bf16[50,2048]{1,0:T(8,128)(2,1)S(1)}, u32[]{:S(2)}, u32[]{:S(2)}) collective-permute-start(bf16[50,2048]{1,0:T(8,128)(2,1)S(1)} %get-tuple-element.66), channel_id=1, source_target_pairs={{0,1},{1,0},{2,3},{3,2},{4,5},{5,4},{6,7},{7,6},{8,9},{9,8},{10,11... | collective-permute-start | bytes 614408 | tf_op jit(solution)/shard_map/ppermute | solution.py:360

commit v6 on v5

--- a/solution.py
+++ b/solution.py
@@ -204,14 +204,17 @@
     last, q_ref, g_ref, slots_ref, before_ref, bias_ref,
     ds_ref, stats_ref, keys_ref, grad_ref, wide_ref,
 ):
-    shown = slots_ref.shape[0]
+    shown = grad_ref.shape[0]
     kv_local = keys_ref.shape[1] // HD
     width = kv_local * HD
-    fill_padded(wide_ref, slots_ref)
-    keys_ref[...] = wide_ref[:, :width].astype(BF16)
+    if last:
+        keys_ref[...] = slots_ref[:, :width]
+    else:
+        fill_padded(wide_ref, slots_ref)
+        keys_ref[...] = wide_ref[:, :width].astype(BF16)
     for kv in range(kv_local):
-        keys = keys_ref[:, lanes(kv)]
-        values = wide_ref[:, lanes(kv_local + kv)].astype(BF16)
+        keys = (slots_ref if last else keys_ref)[:, lanes(kv)]
+        values = (slots_ref if last else wide_ref)[:, lanes(kv_local + kv)].astype(BF16)
         heads = range(kv * GROUP, (kv + 1) * GROUP)
         all_dscores, all_probs = [], []
         for head in heads:
@@ -247,9 +250,9 @@
         stats_ref[...] = jnp.zeros_like(stats_ref)
 
 
-def slots_part(last, queries, out_grad, slots, before, bias):
+def slots_part(last, shown, queries, out_grad, slots, before, bias):
     rows = queries.shape[0]
-    shown, width = slots.shape[0], slots.shape[1] // 2
+    width = slots.shape[1] // 2
     heads = queries.shape[1] // HD
     padded = round_up(shown, 16)
     return pl.pallas_call(
@@ -261,7 +264,7 @@
             shape((heads, padded, rows)),
             shape((heads, 8, rows) if last else (8, HD), F32),
             shape((padded, width)),
-            shape(slots.shape, BF16 if last else F32),
+            shape((shown, 2 * width), BF16 if last else F32),
         ],
         scratch_shapes=[pltpu.VMEM((padded, 2 * width), F32)],
         compiler_params=params(16 if padded <= 512 else 40),
@@ -270,89 +273,105 @@
 
 
 def own_grads_kernel(
-    heads, last, q_ref, g_ref, k_ref, v_ref, ok_ref, ek_ref, ods_ref, eds_ref, stats_ref, *rest
+    heads, carried, q_ref, g_ref, k_ref, v_ref, ok_ref, ek_ref, ods_ref, eds_ref, stats_ref, *rest
 ):
-    *earlier, dq_out, dk_ref, dv_ref, bias_ref, dq_ref, sem = rest
-    kv = heads[0] // GROUP
+    *sums, dq_out, dk_out, dv_out, dk_next, dv_next, bias_ref, dq_ref, grad_ref, sems = rest
     bias_ref[...] = causal_bias(bias_ref.shape[0])
-    keys = k_ref[:, lanes(kv)]
-    values = v_ref[:, lanes(kv)]
-    keys_t = jnp.concatenate([ok_ref[:, lanes(kv)], ek_ref[:, lanes(kv)], keys], 0).T
-    all_dscores, all_probs = [], []
-    for at, head in enumerate(heads):
-        scores = dot(keys, q_ref[:, lanes(head)], LAST) * SCALE2 + bias_ref[...]
-        probs = jnp.exp2(scores - stats_ref[head, 0:1, :]) * stats_ref[head, 1:2, :]
-        dprobs = dot(values, g_ref[:, lanes(head)], LAST)
-        dscores = (probs * (dprobs - stats_ref[head, 2:3, :])).astype(BF16)
-        all_dscores.append(dscores)
-        all_probs.append(probs.astype(BF16))
-        dquery = dot(keys_t, jnp.concatenate([ods_ref[head], eds_ref[head], dscores], 0))
-        dq_ref[:, lanes(at)] = (dquery * SCALE).T.astype(BF16)
-    columns = pl.ds(heads[0] * HD, len(heads) * HD)
-    copy = pltpu.make_async_copy(dq_ref, dq_out.at[:, columns], sem)
-    copy.start()
-    queries = jnp.concatenate([q_ref[:, lanes(head)] for head in heads], 0)
-    grads = jnp.concatenate([g_ref[:, lanes(head)] for head in heads], 0)
-    key_part = dot(jnp.concatenate(all_dscores, 1), queries)
-    value_part = dot(jnp.concatenate(all_probs, 1), grads)
-    if len(earlier) > 1:
-        key_part = key_part + earlier[1][...]
-        value_part = value_part + earlier[2][...]
-    if last:
-        key_part = key_part * SCALE
-    dk_ref[...] = key_part.astype(dk_ref.dtype)
-    dv_ref[...] = value_part.astype(dv_ref.dtype)
-    copy.wait()
-
-
-def own_grads(heads, last, operands, earlier):
-    queries, odd_keys, even_keys = operands[0], operands[4], operands[5]
+    copies = []
+
+    def send(source, target, at):
+        copies.append(pltpu.make_async_copy(source, target, sems.at[at]))
+        copies[-1].start()
+
+    for kv in range(heads[0] // GROUP, heads[-1] // GROUP + 1):
+        keys = k_ref[:, lanes(kv)]
+        values = v_ref[:, lanes(kv)]
+        keys_t = jnp.concatenate([ok_ref[:, lanes(kv)], ek_ref[:, lanes(kv)], keys], 0).T
+        mine = [head for head in heads if head // GROUP == kv]
+        all_dscores, all_probs = [], []
+        for head in mine:
+            scores = dot(keys, q_ref[:, lanes(head)], LAST) * SCALE2 + bias_ref[...]
+            probs = jnp.exp2(scores - stats_ref[head, 0:1, :]) * stats_ref[head, 1:2, :]
+            dprobs = dot(values, g_ref[:, lanes(head)], LAST)
+            dscores = (probs * (dprobs - stats_ref[head, 2:3, :])).astype(BF16)
+            all_dscores.append(dscores)
+            all_probs.append(probs.astype(BF16))
+            dquery = dot(keys_t, jnp.concatenate([ods_ref[head], eds_ref[head], dscores], 0))
+            dq_ref[:, lanes(head - heads[0])] = (dquery * SCALE).T.astype(BF16)
+        if mine[-1] == heads[-1]:
+            send(dq_ref, dq_out.at[:, pl.ds(heads[0] * HD, len(heads) * HD)], 0)
+        queries = jnp.concatenate([q_ref[:, lanes(head)] for head in mine], 0)
+        grads = jnp.concatenate([g_ref[:, lanes(head)] for head in mine], 0)
+        key_part = dot(jnp.concatenate(all_dscores, 1), queries)
+        value_part = dot(jnp.concatenate(all_probs, 1), grads)
+        if carried and mine[0] == heads[0]:
+            key_part = key_part + sums[-2][...]
+            value_part = value_part + sums[-1][...]
+        if mine[-1] % GROUP == GROUP - 1:
+            grad_ref[:, lanes(2 * kv)] = (key_part * SCALE).astype(BF16)
+            grad_ref[:, lanes(2 * kv + 1)] = value_part.astype(BF16)
+            column = pl.ds(kv * HD, HD)
+            send(grad_ref.at[:, pl.ds(2 * kv * HD, HD)], dk_out.at[:, column], 2 * kv + 1)
+            send(grad_ref.at[:, pl.ds((2 * kv + 1) * HD, HD)], dv_out.at[:, column], 2 * kv + 2)
+        else:
+            dk_next[...] = key_part
+            dv_next[...] = value_part
+    if heads[-1] % GROUP == GROUP - 1:
+        dk_next[...] = jnp.zeros_like(dk_next)
+        dv_next[...] = jnp.zeros_like(dv_next)
+    for copy in copies:
+        copy.wait()
+
+
+def own_grads(heads, operands, earlier):
+    queries, keys, odd_keys, even_keys = operands[0], operands[2], operands[4], operands[5]
     rows = queries.shape[0]
+    kv_local = keys.shape[1] // HD
     padded = odd_keys.shape[0] + even_keys.shape[0]
-    in_specs = [VMEM] * len(operands) + [HBM, VMEM, VMEM][: len(earlier)]
-    aliases = {len(operands): 0} if earlier else {}
-    kind = BF16 if last else F32
-    return pl.pallas_call(
-        functools.partial(own_grads_kernel, heads, last),
+    return pl.pallas_call(
+        functools.partial(own_grads_kernel, heads, heads[0] % GROUP != 0),
         name="own_grads",
-        in_specs=in_specs,
-        out_specs=[HBM, VMEM, VMEM],
-        out_shape=[shape(queries.shape), shape((rows, HD), kind), shape((rows, HD), kind)],
-        input_output_aliases=aliases,
+        in_specs=[VMEM] * len(operands) + [HBM, HBM, HBM, VMEM, VMEM][: len(earlier)],
+        out_specs=[HBM, HBM, HBM, VMEM, VMEM],
+        out_shape=[shape(queries.shape), shape(keys.shape), shape(keys.shape)]
+        + [shape((rows, HD), F32)] * 2,
+        input_output_aliases={len(operands) + at: at for at in range(3)} if earlier else {},
         scratch_shapes=[
             pltpu.VMEM((rows, rows), F32),
             pltpu.VMEM((rows, len(heads) * HD), BF16),
-            pltpu.SemaphoreType.DMA,
+            pltpu.VMEM((rows, 2 * kv_local * HD), BF16),
+            pltpu.SemaphoreType.DMA((2 * kv_local + 1,)),
         ],
         compiler_params=params(16 if padded <= 512 else 32),
         cost_estimate=cost(20 * len(heads) * rows * rows * HD, 4 * rows * len(heads) * HD),
     )(*operands, *earlier)
 
 
-def state_kernel(chunk, group, mine_ref, emitted_ref, wk_ref, wv_ref, *out_refs):
+def state_kernel(chunk, blocks, mine_ref, emitted_ref, wk_ref, wv_ref, *out_refs):
     width = wk_ref.shape[1]
     keys = emitted_ref[:, :width]
     values = emitted_ref[:, width:]
-    wide = out_refs[0].shape[1]
-    for at, out_ref in enumerate(out_refs):
+    for (key, split, part), out_ref in zip(blocks, out_refs):
+        wide = out_ref.shape[1]
+        first = (mine_ref[0] ^ key) * split + part
         for step in range(wide // chunk):
-            rows = pl.ds(pl.multiple_of((mine_ref[0] ^ group[at]) * wide + step * chunk, chunk), chunk)
+            rows = pl.ds(pl.multiple_of(first * wide + step * chunk, chunk), chunk)
             total = dot(keys, wk_ref[rows, :], LAST) + dot(values, wv_ref[rows, :], LAST)
             out_ref[:, step * chunk : (step + 1) * chunk] = total.astype(BF16)
 
 
-def state_part(mine, emitted, w_key, w_value, wide, group, chunk=512):
+def state_part(mine, emitted, w_key, w_value, wide, blocks, chunk=512):
     rows = emitted.shape[0]
     width = w_key.shape[1]
-    count = len(group)
-    return pl.pallas_call(
-        functools.partial(state_kernel, chunk, group),
+    columns = sum(wide // split for _, split, _ in blocks)
+    return pl.pallas_call(
+        functools.partial(state_kernel, chunk, blocks),
         name="state_part",
         in_specs=[SMEM] + [VMEM] * 3,
-        out_specs=[VMEM] * count,
-        out_shape=[shape((rows, wide))] * count,
+        out_specs=[VMEM] * len(blocks),
+        out_shape=[shape((rows, wide // split)) for _, split, _ in blocks],
         compiler_params=params(14),
-        cost_estimate=cost(4 * rows * count * wide * width, 4 * count * wide * width),
+        cost_estimate=cost(4 * rows * columns * width, 4 * columns * width),
     )(mine, emitted, w_key, w_value)
 
 
@@ -373,17 +392,21 @@
     projected = project(summary_states, w_key, w_value)
     own = own_stats(queries, out_grad, keys_own, values_own)
 
-    near = [j for j in range(0, n_seg, 2) if not j & 2]
-    far = [j for j in range(0, n_seg, 2) if j & 2]
+    middle = [j for j in range(4, n_seg, 4)]
+    last = [j for j in range(2, n_seg, 4)]
+    near, far = [0], middle + last
     evens = (near + far)[1:]
     odds = [j + 1 for j in near + far]
     chunks = {j: exchange(projected, "seg", n_seg, j) for j in range(2, n_seg, 2)}
     chunks[0] = projected
+    shown = len(odds) * count
+    padding = round_up(shown, 16) - shown
     odd = jnp.concatenate(
         [
             exchange(jnp.concatenate([chunks[j] for j in group], 0), "seg", n_seg, 1)
-            for group in (near, far)
-        ],
+            for group in (near, middle, last)
+        ]
+        + [jnp.zeros((padding, projected.shape[1]), BF16)] * (padding > 0),
         0,
     )
     even = jnp.concatenate([chunks[j] for j in evens], 0)
@@ -392,17 +415,19 @@
         position, queries, out_grad, even, own, count, evens, odds
     )
     odd_ds, stats, odd_keys, odd_grad = slots_part(
-        True, queries, out_grad, odd, before, odd_bias
+        True, shown, queries, out_grad, odd, before, odd_bias
     )
 
     got = exchange(odd_grad, "seg", n_seg, 1)
     even_ds, _, even_keys, even_grad = slots_part(
-        False, queries, out_grad, even, stats, even_bias
+        False, even.shape[0], queries, out_grad, even, stats, even_bias
     )
     operands = [
         queries, out_grad, keys_own, values_own, odd_keys, even_keys, odd_ds, even_ds, stats
     ]
-    begun = own_grads(range(GROUP // 2), False, operands, [])
+    cuts = [0, kv_local * GROUP * 4 // 16, kv_local * GROUP * 8 // 16, kv_local * GROUP]
+    shares = [range(*pair) for pair in zip(cuts, cuts[1:])]
+    begun = own_grads(shares[0], operands, [])
     got, even_grad, begun = lax.optimization_barrier((got, even_grad, begun))
     blocks = {}
     for j in sorted(evens, key=lambda j: (j.bit_count(), -j)):
@@ -410,43 +435,42 @@
         block = got[at + count : at + 2 * count].astype(F32) + even_grad[at : at + count]
         block = block.astype(BF16)
         blocks[j] = exchange(block, "seg", n_seg, j)
-    query_grad, *first = own_grads(range(GROUP // 2, GROUP), True, operands, begun)
-    blocks, query_grad = lax.optimization_barrier((blocks, query_grad))
+    begun = own_grads(shares[1], operands, begun)
+    blocks, begun = lax.optimization_barrier((blocks, begun))
     emitted = got[:count].astype(F32)
     for block in blocks.values():
         emitted = emitted + block.astype(F32)
     emitted = emitted.astype(BF16)
 
     wide = w_key.shape[0] // n_tp
-    far_group, near_group = list(range(n_tp - 1, 1, -1)), [1, 0]
+    halves = 1
+    far = range(n_tp - 1, 1, -1)
+    calls = [[(j, halves, part) for j in far if j & 1] for part in range(halves)]
+    calls.append([(j, halves, part) for part in range(halves) for j in far if not j & 1])
     terms = {}
-    for group in ([j for j in far_group if j & 1], [j for j in far_group if not j & 1]):
-        terms.update(zip(group, state_part(mine, emitted, w_key, w_value, wide, group)))
-    bit = 1
-    while bit < n_tp:
-        for j in sorted((j for j in terms if j & bit and j > bit), reverse=True):
-            got = exchange(terms.pop(j).astype(BF16), "tp", n_tp, bit)
-            terms[j ^ bit] = terms[j ^ bit].astype(F32) + got.astype(F32)
-        bit *= 2
-    terms = {j: terms[j].astype(BF16) for j in terms}
-    terms, emitted = lax.optimization_barrier((terms, emitted))
-    sent = {j: exchange(terms[j], "tp", n_tp, j) for j in terms}
-    other, state = state_part(mine, emitted, w_key, w_value, wide, near_group)
+    for blocks in calls:
+        results = state_part(mine, emitted, w_key, w_value, wide, blocks)
+        terms.update(((j, part), result) for (j, _, part), result in zip(blocks, results))
+    for part in range(halves):
+        bit = 1
+        while bit < n_tp:
+            for j in [j for j in far if (j, part) in terms and j & bit and j > bit]:
+                got = exchange(terms.pop((j, part)).astype(BF16), "tp", n_tp, bit)
+                total = terms[j ^ bit, part].astype(F32) + got.astype(F32)
+                terms[j ^ bit, part] = total.astype(BF16)
+            bit *= 2
+    late = {at: terms[at] for at in terms if at[1] == halves - 1}
+    late, emitted, begun = lax.optimization_barrier((late, emitted, begun))
+    terms.update(late)
+    arrived = {at: exchange(terms[at], "tp", n_tp, at[0]) for at in sorted(terms, key=lambda at: at[1])}
+    other, state = state_part(mine, emitted, w_key, w_value, wide, [(1, 1, 0), (0, 1, 0)])
     state = state.astype(F32) + exchange(other, "tp", n_tp, 1).astype(F32)
-    for j in sent:
-        state = state + sent[j].astype(F32)
-    terms = {0: state}
-    state_grad = (terms[0] + summary_grad.astype(F32)).astype(BF16)
-
-    key_blocks, value_blocks = [first[0]], [first[1]]
-    for kv in range(1, kv_local):
-        query_grad, key_block, value_block = own_grads(
-            range(kv * GROUP, (kv + 1) * GROUP), True, operands, [query_grad]
-        )
-        key_blocks.append(key_block)
-        value_blocks.append(value_block)
-    key_grad = jnp.concatenate(key_blocks, 1)
-    value_grad = jnp.concatenate(value_blocks, 1)
+    for j in sorted({j for j, _ in arrived}):
+        pieces = [arrived[j, part] for part in range(halves)]
+        state = state + jnp.concatenate(pieces, 1).astype(F32)
+    state_grad = (state + summary_grad.astype(F32)).astype(BF16)
+
+    query_grad, key_grad, value_grad, *_ = own_grads(shares[2], operands, begun)
     return (query_grad, key_grad, value_grad, state_grad)
 
 

time: 48.3 us -> 48.4 us (level)
  waiting for transfers between devices: 7.58 us -> 5.65 us
  starting transfers between devices: 15.7 us -> 17.4 us
  Pallas kernels: 22.2 us -> 23.1 us
  other arithmetic: 1.82 us -> 1.14 us
    ppermute x12 -> x13, waiting for transfers between devices: 7.58 us -> 5.65 us  [exchange(): return lax.ppermute(block, axis, [(i, i ^ key) for i in range(size)])]
    ppermute x12 -> x13, starting transfers between devices: 15.7 us -> 17.4 us  [exchange(): return lax.ppermute(block, axis, [(i, i ^ key) for i in range(size)])]
    pallas_call x6, Pallas kernels: 10.2 us -> 11.1 us  [the longest x3 8.23 us: own_grads(): pl.pallas_call(functools.partial(own_grads_kernel, heads, heads[0] % GROU...]
    concatenate x1 -> x0, other arithmetic: 0.73 us -> none  [per_device(): key_grad = jnp.concatenate(key_blocks, 1)]
  transfers between devices with their start and end apart: 12 -> 13, of which waited for: 8 -> 6; matrix products, arithmetic and copies ran while one was open for 2% -> 0% of each run, Pallas kernels for 29% -> 31%
where the time goes in v6:
time: 48.4 us; the launch traced here: 48.2 us
  Pallas kernels  23.1 us (48%)
  starting transfers between devices  17.4 us (36%)
  waiting for transfers between devices  5.65 us (12%)
  other arithmetic  1.14 us (2%)
  between operations  0.84 us (2%)
    ppermute x13, starting transfers between devices, exchange(): return lax.ppermute(block, axis, [(i, i ^ key) for i in range(size)])  17.4 us
    pallas_call x3, Pallas kernels, own_grads(): pl.pallas_call(functools.partial(own_grads_kernel, heads, heads[0] % GROU...  8.23 us
    ppermute x13, waiting for transfers between devices, exchange(): return lax.ppermute(block, axis, [(i, i ^ key) for i in range(size)])  5.65 us
    pallas_call x2, Pallas kernels, slots_part(): pl.pallas_call(functools.partial(slots_kernel, last), name='odd_slots' if...  4.75 us
    pallas_call x1, Pallas kernels, project(): pl.pallas_call(functools.partial(project_kernel, pieces), name='project',...  4.26 us
    pallas_call x3, Pallas kernels, state_part(): pl.pallas_call(functools.partial(state_kernel, chunk, blocks), name='stat...  2.88 us
    pallas_call x1, Pallas kernels, own_stats(): pl.pallas_call(own_stats_kernel, name='own_stats', in_specs=[VMEM] * 4, o...  1.67 us
    pallas_call x1, Pallas kernels, even_stats(): pl.pallas_call(functools.partial(even_stats_kernel, count, evens, odds),...  1.29 us
  transfers between devices with their start and end apart: 13, of which 6 were waited for; matrix products, arithmetic and copies ran while one was open for 0% of the time, Pallas kernels for 31%

profile of v6, /device:TPU:0, one launch (start us, length us, event | category | flops | bytes accessed | tf_op | source)
XLA Modules:
  0.0 48.2 jit_solution(6088083700540962180)
XLA Ops:
  0.6 0.0 copy-start.3
  0.6 0.0 copy-start.2
  0.7 0.0 copy-start.5
  0.7 0.0 copy-start.4
  0.7 4.3 %project.1 = bf16[50,512]{1,0:T(8,128)(2,1)S(1)} custom-call(bf16[50,8192]{1,0:T(8,128)(2,1)} %states_hbm.1, bf16[8192,256]{1,0:T(8,128)(2,1)} %wk_ref.5, bf16[8192,256]{1,0:T(8,128)(2,1)} %wv_ref.5), custom_call_target="tpu_custom_call" | custom-call | flops 419430400 | bytes 16777216 | tf_op jit(solution)/shard_map/project/pallas_call | solution.py:86
  4.9 5.1 %collective-permute-start.4 = (bf16[50,512]{1,0:T(8,128)(2,1)S(1)}, bf16[50,512]{1,0:T(8,128)(2,1)S(1)}, u32[]{:S(2)}, u32[]{:S(2)}) collective-permute-start(bf16[50,512]{1,0:T(8,128)(2,1)S(1)} %project.1), channel_id=1, source_target_pairs={{0,24},{4,28},{8,16},{12,20},{16,8},{20,12},{24,0},{28,4},{1,25},{... | collective-permute-start | bytes 153608 | tf_op jit(solution)/shard_map/ppermute | solution.py:379
  10.1 0.0 collective-permute-start.3
  10.1 0.6 %collective-permute-start.1 = (bf16[50,512]{1,0:T(8,128)(2,1)S(1)}, bf16[50,512]{1,0:T(8,128)(2,1)S(1)}, u32[]{:S(2)}, u32[]{:S(2)}) collective-permute-start(bf16[50,512]{1,0:T(8,128)(2,1)S(1)} %project.1), channel_id=1, source_target_pairs={{0,16},{4,20},{8,24},{12,28},{16,0},{20,4},{24,8},{28,12},{1,17},{... | collective-permute-start | bytes 153608 | tf_op jit(solution)/shard_map/ppermute | solution.py:379
  10.7 1.6 %collective-permute-start = (bf16[50,512]{1,0:T(8,128)(2,1)S(1)}, bf16[50,512]{1,0:T(8,128)(2,1)S(1)}, u32[]{:S(2)}, u32[]{:S(2)}) collective-permute-start(bf16[50,512]{1,0:T(8,128)(2,1)S(1)} %project.1), channel_id=1, source_target_pairs={{0,4},{4,0},{8,12},{12,8},{16,20},{20,16},{24,28},{28,24},{1,5},{5... | collective-permute-start | bytes 153608 | tf_op jit(solution)/shard_map/ppermute | solution.py:379
  12.3 0.0 copy-done.3
  12.3 0.0 copy-done.2
  12.3 0.0 copy-done.5
  12.3 0.0 copy-done.4
  12.3 1.7 %own_stats.1.own_ref = f32[16,8,256]{2,1,0:T(8,128)S(1)} custom-call(bf16[256,2048]{1,0:T(8,128)(2,1)S(1)} %copy-done.2, bf16[256,2048]{1,0:T(8,128)(2,1)S(1)} %copy-done.3, bf16[256,256]{1,0:T(8,128)(2,1)S(1)} %copy-done.4, bf16[256,256]{1,0:T(8,128)(2,1)S(1)} %copy-done.5), custom_call_target="tpu_custom_call" | custom-call | flops 2684354560 | bytes 2097152 | tf_op jit(solution)/shard_map/own_stats/pallas_call | solution.py:145
  14.0 0.1 pad.6.clone
  14.1 0.0 collective-permute-done.4
  14.1 0.2 collective-permute-done.3
  14.4 1.6 %collective-permute-start.5 = (bf16[100,512]{1,0:T(8,128)(2,1)S(1)}, bf16[100,512]{1,0:T(8,128)(2,1)S(1)}, u32[]{:S(2)}, u32[]{:S(2)}) collective-permute-start(bf16[100,512]{1,0:T(8,128)(2,1)S(1)} %pad_maximum_fusion.1), channel_id=1, source_target_pairs={{0,4},{4,0},{8,12},{12,8},{16,20},{20,16},{24,28},{28,24},{1,5},{5... | collective-permute-start | bytes 307208 | tf_op jit(solution)/shard_map/ppermute | solution.py:379
  16.0 0.0 collective-permute-done.1
  16.0 1.0 %collective-permute-start.2 = (bf16[50,512]{1,0:T(8,128)(2,1)S(1)}, bf16[50,512]{1,0:T(8,128)(2,1)S(1)}, u32[]{:S(2)}, u32[]{:S(2)}) collective-permute-start(bf16[50,512]{1,0:T(8,128)(2,1)S(1)} %collective-permute-done.1), channel_id=1, source_target_pairs={{0,4},{4,0},{8,12},{12,8},{16,20},{20,16},{24,28},{28,24},{1,5},{5... | collective-permute-start | bytes 153608 | tf_op jit(solution)/shard_map/ppermute | solution.py:379
  17.0 1.3 %even_stats.1 = (f32[16,8,256]{2,1,0:T(8,128)S(1)}, f32[160,256]{1,0:T(8,128)S(1)}, f32[208,256]{1,0:T(8,128)S(1)}) custom-call(s32[1]{0:T(128)} %bitcast.seg_ref, bf16[256,2048]{1,0:T(8,128)(2,1)S(1)} %copy-done.2, bf16[256,2048]{1,0:T(8,128)(2,1)S(1)} %copy-done.3, bf16[150,512]{1,0:T(8,128)(2,1)S(1)} %pad_maximum_fusion.even_ref.slots_ref, ...), custom_call_target="tpu_custom_call" | custom-call | flops 1677721600 | bytes 2097152 | tf_op jit(solution)/shard_map/even_stats/pallas_call | solution.py:187
  18.3 0.0 collective-permute-done
  18.4 1.8 %collective-permute-done.2 = bf16[50,512]{1,0:T(8,128)(2,1)S(1)} collective-permute-done((bf16[50,512]{1,0:T(8,128)(2,1)S(1)}, bf16[50,512]{1,0:T(8,128)(2,1)S(1)}, u32[]{:S(2)}, u32[]{:S(2)}) %collective-permute-start.2) | collective-permute-done | bytes 51232 | tf_op jit(solution)/shard_map/ppermute | solution.py:379
  20.2 0.0 collective-permute-done.5
  20.2 0.1 maximum_maximum_fusion.slots_ref
  20.3 3.0 %odd_slots.1 = (bf16[16,208,256]{2,1,0:T(8,128)(2,1)S(1)}, f32[16,8,256]{2,1,0:T(8,128)S(1)}, bf16[208,256]{1,0:T(8,128)(2,1)S(1)}, bf16[200,512]{1,0:T(8,128)(2,1)S(1)}) custom-call(bf16[256,2048]{1,0:T(8,128)(2,1)S(1)} %copy-done.2, bf16[256,2048]{1,0:T(8,128)(2,1)S(1)} %copy-done.3, bf16[208,512]{1,0:T(8,128)(2,1)S(1)} %maximum_maximum_fusion.slots_ref, ...), custom_call_target="tpu_custom_call" | custom-call | flops 3271557120 | bytes 2097152 | tf_op jit(solution)/shard_map/odd_slots/pallas_call | solution.py:258
  23.3 1.2 %collective-permute-start.6 = (bf16[200,512]{1,0:T(8,128)(2,1)S(1)}, bf16[200,512]{1,0:T(8,128)(2,1)S(1)}, u32[]{:S(2)}, u32[]{:S(2)}) collective-permute-start(bf16[200,512]{1,0:T(8,128)(2,1)S(1)} %get-tuple-element.59), channel_id=1, source_target_pairs={{0,4},{4,0},{8,12},{12,8},{16,20},{20,16},{24,28},{28,24},{1,5},{5... | collective-permute-start | bytes 614408 | tf_op jit(solution)/shard_map/ppermute | solution.py:379
  24.5 1.8 %even_slots.1 = (bf16[16,160,256]{2,1,0:T(8,128)(2,1)S(1)}, f32[8,128]{1,0:T(8,128)}, bf16[160,256]{1,0:T(8,128)(2,1)S(1)}, f32[150,512]{1,0:T(8,128)S(1)}) custom-call(bf16[256,2048]{1,0:T(8,128)(2,1)S(1)} %copy-done.2, bf16[256,2048]{1,0:T(8,128)(2,1)S(1)} %copy-done.3, bf16[150,512]{1,0:T(8,128)(2,1)S(1)} %pad_maximum_fusion.even_ref.slots_ref, ...), custom_call_target="tpu_custom_call" | custom-call | flops 2516582400 | bytes 2097152 | tf_op jit(solution)/shard_map/even_slots/pallas_call | solution.py:258
  26.3 0.0 copy-start.1
  26.3 2.0 %own_grads.3 = (bf16[256,2048]{1,0:T(8,128)(2,1)}, bf16[256,256]{1,0:T(8,128)(2,1)}, bf16[256,256]{1,0:T(8,128)(2,1)}, f32[256,128]{1,0:T(8,128)S(1)}, f32[256,128]{1,0:T(8,128)S(1)}) custom-call(bf16[256,2048]{1,0:T(8,128)(2,1)S(1)} %copy-done.2, bf16[256,2048]{1,0:T(8,128)(2,1)S(1)} %copy-done.3, bf16[256,256]{1,0:T(8,128)(2,1)S(1)} %copy-done.4, ...), custom_call_target="tpu_custom_call" | custom-call | flops 671088640 | bytes 524288 | tf_op jit(solution)/shard_map/own_grads/pallas_call | solution.py:331
  28.3 0.0 copy-start
  28.3 0.8 %collective-permute-done.6 = bf16[200,512]{1,0:T(8,128)(2,1)S(1)} collective-permute-done((bf16[200,512]{1,0:T(8,128)(2,1)S(1)}, bf16[200,512]{1,0:T(8,128)(2,1)S(1)}, u32[]{:S(2)}, u32[]{:S(2)}) %collective-permute-start.6) | collective-permute-done | bytes 204832 | tf_op jit(solution)/shard_map/ppermute | solution.py:379
  29.1 0.1 add_convert_fusion.3
  29.2 3.0 %collective-permute-start.9 = (bf16[50,512]{1,0:T(8,128)(2,1)S(1)}, bf16[50,512]{1,0:T(8,128)(2,1)S(1)}, u32[]{:S(2)}, u32[]{:S(2)}) collective-permute-start(bf16[50,512]{1,0:T(8,128)(2,1)S(1)} %get-tuple-element.98), channel_id=1, source_target_pairs={{0,24},{4,28},{8,16},{12,20},{16,8},{20,12},{24,0},{28,4},{1,25},{... | collective-permute-start | bytes 153608 | tf_op jit(solution)/shard_map/ppermute | solution.py:379
  32.2 0.0 collective-permute-start.8
  32.2 1.4 %collective-permute-start.7 = (bf16[50,512]{1,0:T(8,128)(2,1)S(1)}, bf16[50,512]{1,0:T(8,128)(2,1)S(1)}, u32[]{:S(2)}, u32[]{:S(2)}) collective-permute-start(bf16[50,512]{1,0:T(8,128)(2,1)S(1)} %get-tuple-element.100), channel_id=1, source_target_pairs={{0,8},{4,12},{8,0},{12,4},{16,24},{20,28},{24,16},{28,20},{1,9},{5... | collective-permute-start | bytes 153608 | tf_op jit(solution)/shard_map/ppermute | solution.py:379
  33.6 2.2 %own_grads.4 = (bf16[256,2048]{1,0:T(8,128)(2,1)}, bf16[256,256]{1,0:T(8,128)(2,1)}, bf16[256,256]{1,0:T(8,128)(2,1)}, f32[256,128]{1,0:T(8,128)S(1)}, f32[256,128]{1,0:T(8,128)S(1)}) custom-call(bf16[256,2048]{1,0:T(8,128)(2,1)S(1)} %copy-done.2, bf16[256,2048]{1,0:T(8,128)(2,1)S(1)} %copy-done.3, ...), custom_call_target="tpu_custom_call", output_to_operand_aliasing={{0}: (9, {}), {1}: (10, {}), {2}: (11, {})} | custom-call | flops 671088640 | bytes 524288 | tf_op jit(solution)/shard_map/own_grads/pallas_call | solution.py:331
  35.9 0.0 collective-permute-done.9
  35.9 1.4 %collective-permute-done.8 = bf16[50,512]{1,0:T(8,128)(2,1)S(1)} collective-permute-done((bf16[50,512]{1,0:T(8,128)(2,1)S(1)}, bf16[50,512]{1,0:T(8,128)(2,1)S(1)}, u32[]{:S(2)}, u32[]{:S(2)}) %collective-permute-start.8) | collective-permute-done | bytes 51232 | tf_op jit(solution)/shard_map/ppermute | solution.py:379
  37.3 0.0 collective-permute-done.7
  37.3 0.0 copy-done.1
  37.3 0.0 copy-done
  37.3 0.8 %state_part.4 = bf16[50,2048]{1,0:T(8,128)(2,1)S(1)} custom-call(s32[1]{0:T(128)} %bitcast.1.mine_ref, bf16[50,512]{1,0:T(8,128)(2,1)S(1)} %add_convert_fusion.2.emitted_ref, bf16[8192,256]{1,0:T(8,128)(2,1)S(1)} %copy-done, bf16[8192,256]{1,0:T(8,128)(2,1)S(1)} %copy-done.1), custom_call_target="tpu_custom_call" | custom-call | flops 104857600 | bytes 2097152 | tf_op jit(solution)/shard_map/state_part/pallas_call | solution.py:367
  38.1 0.1 collective-permute-start.10
  38.2 0.8 %state_part.3 = bf16[50,2048]{1,0:T(8,128)(2,1)S(1)} custom-call(s32[1]{0:T(128)} %bitcast.1.mine_ref, bf16[50,512]{1,0:T(8,128)(2,1)S(1)} %add_convert_fusion.2.emitted_ref, bf16[8192,256]{1,0:T(8,128)(2,1)S(1)} %copy-done, bf16[8192,256]{1,0:T(8,128)(2,1)S(1)} %copy-done.1), custom_call_target="tpu_custom_call" | custom-call | flops 104857600 | bytes 2097152 | tf_op jit(solution)/shard_map/state_part/pallas_call | solution.py:367
  38.9 0.7 %collective-permute-done.10 = bf16[50,2048]{1,0:T(8,128)(2,1)S(1)} collective-permute-done((bf16[50,2048]{1,0:T(8,128)(2,1)S(1)}, bf16[50,2048]{1,0:T(8,128)(2,1)S(1)}, u32[]{:S(2)}, u32[]{:S(2)}) %collective-permute-start.10) | collective-permute-done | bytes 204832 | tf_op jit(solution)/shard_map/ppermute | solution.py:379
  39.6 0.1 add_convert_fusion.1
  39.7 1.6 %collective-permute-start.12 = (bf16[50,2048]{1,0:T(8,128)(2,1)S(1)}, bf16[50,2048]{1,0:T(8,128)(2,1)S(1)}, u32[]{:S(2)}, u32[]{:S(2)}) collective-permute-start(bf16[50,2048]{1,0:T(8,128)(2,1)S(1)} %add_convert_fusion.1), channel_id=1, source_target_pairs={{0,2},{1,3},{2,0},{3,1},{4,6},{5,7},{6,4},{7,5},{8,10},{9,11},{10,... | collective-permute-start | bytes 614408 | tf_op jit(solution)/shard_map/ppermute | solution.py:379
  41.3 1.4 %state_part.5 = (bf16[50,2048]{1,0:T(8,128)(2,1)S(1)}, bf16[50,2048]{1,0:T(8,128)(2,1)S(1)}) custom-call(s32[1]{0:T(128)} %bitcast.1.mine_ref, bf16[50,512]{1,0:T(8,128)(2,1)S(1)} %add_convert_fusion.2.emitted_ref, bf16[8192,256]{1,0:T(8,128)(2,1)S(1)} %copy-done, bf16[8192,256]{1,0:T(8,128)(2,1)S(1)} %copy-done.1), custom_call_target="tpu_custom_call" | custom-call | flops 209715200 | bytes 4194304 | tf_op jit(solution)/shard_map/state_part/pallas_call | solution.py:367
  42.7 0.0 copy-start.6
  42.7 0.1 collective-permute-start.11
  42.7 4.0 %own_grads.5 = (bf16[256,2048]{1,0:T(8,128)(2,1)}, bf16[256,256]{1,0:T(8,128)(2,1)}, bf16[256,256]{1,0:T(8,128)(2,1)}, f32[256,128]{1,0:T(8,128)}, f32[256,128]{1,0:T(8,128)}) custom-call(bf16[256,2048]{1,0:T(8,128)(2,1)S(1)} %copy-done.2, bf16[256,2048]{1,0:T(8,128)(2,1)S(1)} %copy-done.3, ...), custom_call_target="tpu_custom_call", output_to_operand_aliasing={{0}: (9, {}), {1}: (10, {}), {2}: (11, {})} | custom-call | flops 1342177280 | bytes 1048576 | tf_op jit(solution)/shard_map/own_grads/pallas_call | solution.py:331
  46.8 0.7 %collective-permute-done.12 = bf16[50,2048]{1,0:T(8,128)(2,1)S(1)} collective-permute-done((bf16[50,2048]{1,0:T(8,128)(2,1)S(1)}, bf16[50,2048]{1,0:T(8,128)(2,1)S(1)}, u32[]{:S(2)}, u32[]{:S(2)}) %collective-permute-start.12) | collective-permute-done | bytes 204832 | tf_op jit(solution)/shard_map/ppermute | solution.py:379
  47.4 0.0 collective-permute-done.11
  47.4 0.0 copy-done.6
  47.4 0.8 %add_convert_fusion = bf16[50,2048]{1,0:T(8,128)(2,1)} fusion(bf16[50,2048]{1,0:T(8,128)(2,1)S(1)} %copy-done.6, bf16[50,2048]{1,0:T(8,128)(2,1)S(1)} %collective-permute-done.12, bf16[50,2048]{1,0:T(8,128)(2,1)S(1)} %collective-permute-done.11, bf16[50,2048]{1,0:T(8,128)(2,1)S(1)} %get-tuple-element.95), kind=kLoop, calls=%fused_computation | loop fusion | flops 819200 | bytes 1024000 | tf_op jit(solution)/shard_map/convert_element_type | solution.py:471
  (4 shorter events, 0.1 us)
Async XLA Ops:
  0.6 11.7 %copy-start.3 = (bf16[256,2048]{1,0:T(8,128)(2,1)S(1)}, bf16[256,2048]{1,0:T(8,128)(2,1)}, u32[]{:S(2)}) copy-start(bf16[256,2048]{1,0:T(8,128)(2,1)} %g_ref.13) | copy-start | bytes 3145732
  0.6 11.7 %copy-start.2 = (bf16[256,2048]{1,0:T(8,128)(2,1)S(1)}, bf16[256,2048]{1,0:T(8,128)(2,1)}, u32[]{:S(2)}) copy-start(bf16[256,2048]{1,0:T(8,128)(2,1)} %q_ref.13) | copy-start | bytes 3145732
  0.7 11.7 %copy-start.5 = (bf16[256,256]{1,0:T(8,128)(2,1)S(1)}, bf16[256,256]{1,0:T(8,128)(2,1)}, u32[]{:S(2)}) copy-start(bf16[256,256]{1,0:T(8,128)(2,1)} %v_ref.7) | copy-start | bytes 393220
  0.7 11.7 %copy-start.4 = (bf16[256,256]{1,0:T(8,128)(2,1)S(1)}, bf16[256,256]{1,0:T(8,128)(2,1)}, u32[]{:S(2)}) copy-start(bf16[256,256]{1,0:T(8,128)(2,1)} %k_ref.7) | copy-start | bytes 393220
  4.9 9.2 %collective-permute-start.4 = (bf16[50,512]{1,0:T(8,128)(2,1)S(1)}, bf16[50,512]{1,0:T(8,128)(2,1)S(1)}, u32[]{:S(2)}, u32[]{:S(2)}) collective-permute-start(bf16[50,512]{1,0:T(8,128)(2,1)S(1)} %project.1), channel_id=1, source_target_pairs={{0,24},{4,28},{8,16},{12,20},{16,8},{20,12},{24,0},{28,4},{1,25},{... | collective-permute-start | bytes 153608 | tf_op jit(solution)/shard_map/ppermute | solution.py:379
  10.1 4.3 %collective-permute-start.3 = (bf16[50,512]{1,0:T(8,128)(2,1)S(1)}, bf16[50,512]{1,0:T(8,128)(2,1)S(1)}, u32[]{:S(2)}, u32[]{:S(2)}) collective-permute-start(bf16[50,512]{1,0:T(8,128)(2,1)S(1)} %project.1), channel_id=1, source_target_pairs={{0,8},{4,12},{8,0},{12,4},{16,24},{20,28},{24,16},{28,20},{1,9},{5... | collective-permute-start | bytes 153608 | tf_op jit(solution)/shard_map/ppermute | solution.py:379
  10.1 6.0 %collective-permute-start.1 = (bf16[50,512]{1,0:T(8,128)(2,1)S(1)}, bf16[50,512]{1,0:T(8,128)(2,1)S(1)}, u32[]{:S(2)}, u32[]{:S(2)}) collective-permute-start(bf16[50,512]{1,0:T(8,128)(2,1)S(1)} %project.1), channel_id=1, source_target_pairs={{0,16},{4,20},{8,24},{12,28},{16,0},{20,4},{24,8},{28,12},{1,17},{... | collective-permute-start | bytes 153608 | tf_op jit(solution)/shard_map/ppermute | solution.py:379
  10.7 7.6 %collective-permute-start = (bf16[50,512]{1,0:T(8,128)(2,1)S(1)}, bf16[50,512]{1,0:T(8,128)(2,1)S(1)}, u32[]{:S(2)}, u32[]{:S(2)}) collective-permute-start(bf16[50,512]{1,0:T(8,128)(2,1)S(1)} %project.1), channel_id=1, source_target_pairs={{0,4},{4,0},{8,12},{12,8},{16,20},{20,16},{24,28},{28,24},{1,5},{5... | collective-permute-start | bytes 153608 | tf_op jit(solution)/shard_map/ppermute | solution.py:379
  14.4 5.8 %collective-permute-start.5 = (bf16[100,512]{1,0:T(8,128)(2,1)S(1)}, bf16[100,512]{1,0:T(8,128)(2,1)S(1)}, u32[]{:S(2)}, u32[]{:S(2)}) collective-permute-start(bf16[100,512]{1,0:T(8,128)(2,1)S(1)} %pad_maximum_fusion.1), channel_id=1, source_target_pairs={{0,4},{4,0},{8,12},{12,8},{16,20},{20,16},{24,28},{28,24},{1,5},{5... | collective-permute-start | bytes 307208 | tf_op jit(solution)/shard_map/ppermute | solution.py:379
  16.0 4.2 %collective-permute-start.2 = (bf16[50,512]{1,0:T(8,128)(2,1)S(1)}, bf16[50,512]{1,0:T(8,128)(2,1)S(1)}, u32[]{:S(2)}, u32[]{:S(2)}) collective-permute-start(bf16[50,512]{1,0:T(8,128)(2,1)S(1)} %collective-permute-done.1), channel_id=1, source_target_pairs={{0,4},{4,0},{8,12},{12,8},{16,20},{20,16},{24,28},{28,24},{1,5},{5... | collective-permute-start | bytes 153608 | tf_op jit(solution)/shard_map/ppermute | solution.py:379
  23.3 5.8 %collective-permute-start.6 = (bf16[200,512]{1,0:T(8,128)(2,1)S(1)}, bf16[200,512]{1,0:T(8,128)(2,1)S(1)}, u32[]{:S(2)}, u32[]{:S(2)}) collective-permute-start(bf16[200,512]{1,0:T(8,128)(2,1)S(1)} %get-tuple-element.59), channel_id=1, source_target_pairs={{0,4},{4,0},{8,12},{12,8},{16,20},{20,16},{24,28},{28,24},{1,5},{5... | collective-permute-start | bytes 614408 | tf_op jit(solution)/shard_map/ppermute | solution.py:379
  26.3 11.0 %copy-start.1 = (bf16[8192,256]{1,0:T(8,128)(2,1)S(1)}, bf16[8192,256]{1,0:T(8,128)(2,1)}, u32[]{:S(2)}) copy-start(bf16[8192,256]{1,0:T(8,128)(2,1)} %wv_ref.5) | copy-start | bytes 12582916
  28.3 9.0 %copy-start = (bf16[8192,256]{1,0:T(8,128)(2,1)S(1)}, bf16[8192,256]{1,0:T(8,128)(2,1)}, u32[]{:S(2)}) copy-start(bf16[8192,256]{1,0:T(8,128)(2,1)} %wk_ref.5) | copy-start | bytes 12582916
  29.2 6.7 %collective-permute-start.9 = (bf16[50,512]{1,0:T(8,128)(2,1)S(1)}, bf16[50,512]{1,0:T(8,128)(2,1)S(1)}, u32[]{:S(2)}, u32[]{:S(2)}) collective-permute-start(bf16[50,512]{1,0:T(8,128)(2,1)S(1)} %get-tuple-element.98), channel_id=1, source_target_pairs={{0,24},{4,28},{8,16},{12,20},{16,8},{20,12},{24,0},{28,4},{1,25},{... | collective-permute-start | bytes 153608 | tf_op jit(solution)/shard_map/ppermute | solution.py:379
  32.2 5.1 %collective-permute-start.8 = (bf16[50,512]{1,0:T(8,128)(2,1)S(1)}, bf16[50,512]{1,0:T(8,128)(2,1)S(1)}, u32[]{:S(2)}, u32[]{:S(2)}) collective-permute-start(bf16[50,512]{1,0:T(8,128)(2,1)S(1)} %get-tuple-element.99), channel_id=1, source_target_pairs={{0,16},{4,20},{8,24},{12,28},{16,0},{20,4},{24,8},{28,12},{1,17},{... | collective-permute-start | bytes 153608 | tf_op jit(solution)/shard_map/ppermute | solution.py:379
  32.2 5.1 %collective-permute-start.7 = (bf16[50,512]{1,0:T(8,128)(2,1)S(1)}, bf16[50,512]{1,0:T(8,128)(2,1)S(1)}, u32[]{:S(2)}, u32[]{:S(2)}) collective-permute-start(bf16[50,512]{1,0:T(8,128)(2,1)S(1)} %get-tuple-element.100), channel_id=1, source_target_pairs={{0,8},{4,12},{8,0},{12,4},{16,24},{20,28},{24,16},{28,20},{1,9},{5... | collective-permute-start | bytes 153608 | tf_op jit(solution)/shard_map/ppermute | solution.py:379
  38.1 1.6 %collective-permute-start.10 = (bf16[50,2048]{1,0:T(8,128)(2,1)S(1)}, bf16[50,2048]{1,0:T(8,128)(2,1)S(1)}, u32[]{:S(2)}, u32[]{:S(2)}) collective-permute-start(bf16[50,2048]{1,0:T(8,128)(2,1)S(1)} %state_part.4), channel_id=1, source_target_pairs={{0,1},{1,0},{2,3},{3,2},{4,5},{5,4},{6,7},{7,6},{8,9},{9,8},{10,11... | collective-permute-start | bytes 614408 | tf_op jit(solution)/shard_map/ppermute | solution.py:379
  39.7 7.7 %collective-permute-start.12 = (bf16[50,2048]{1,0:T(8,128)(2,1)S(1)}, bf16[50,2048]{1,0:T(8,128)(2,1)S(1)}, u32[]{:S(2)}, u32[]{:S(2)}) collective-permute-start(bf16[50,2048]{1,0:T(8,128)(2,1)S(1)} %add_convert_fusion.1), channel_id=1, source_target_pairs={{0,2},{1,3},{2,0},{3,1},{4,6},{5,7},{6,4},{7,5},{8,10},{9,11},{10,... | collective-permute-start | bytes 614408 | tf_op jit(solution)/shard_map/ppermute | solution.py:379
  42.7 4.8 %copy-start.6 = (bf16[50,2048]{1,0:T(8,128)(2,1)S(1)}, bf16[50,2048]{1,0:T(8,128)(2,1)}, u32[]{:S(2)}) copy-start(bf16[50,2048]{1,0:T(8,128)(2,1)} %param.15) | copy-start | bytes 614404
  42.7 4.7 %collective-permute-start.11 = (bf16[50,2048]{1,0:T(8,128)(2,1)S(1)}, bf16[50,2048]{1,0:T(8,128)(2,1)S(1)}, u32[]{:S(2)}, u32[]{:S(2)}) collective-permute-start(bf16[50,2048]{1,0:T(8,128)(2,1)S(1)} %get-tuple-element.96), channel_id=1, source_target_pairs={{0,1},{1,0},{2,3},{3,2},{4,5},{5,4},{6,7},{7,6},{8,9},{9,8},{10,11... | collective-permute-start | bytes 614408 | tf_op jit(solution)/shard_map/ppermute | solution.py:379
